TPU v7x, 32 devices: a whole 2x2x4 slice. The times are simulated.
32 devices in a mesh: frames: 4 (over y, core), rows: 8 (over z, x).
Axes of the slice: x: 2, y: 2, z: 4, core: 2. Of those that a mesh axis runs over, the one named last changes fastest.
Arguments:
- fine_q: bfloat16 [4, 64, 16, 256], P('frames', 'rows'), may hold values from -24 to 24
- fine_kv: bfloat16 [4, 64, 16, 512], P('frames', 'rows'), may hold values from -24 to 24
- coarse_q: bfloat16 [4, 8, 2, 1024], P('frames', 'rows'), may hold values from -24 to 24
- coarse_kv: bfloat16 [4, 8, 2, 2048], P('frames', 'rows'), may hold values from -24 to 24
- cotangent: bfloat16 [4, 64, 16, 256], P('frames', 'rows'), may hold values from -6 to 6
- gain_table: float32 [1000, 256], replicated, may hold values from 0.3 to 3
- timesteps: int32 [4], P('frames'), may hold values from 0 to 999
- valid_cols: int32 [4], replicated, may hold values from 8 to 16
Outputs:
- grad_fine_q: bfloat16 [4, 64, 16, 256], P('frames', 'rows')
- grad_fine_kv: bfloat16 [4, 64, 16, 512], P('frames', 'rows')
- grad_coarse_q: bfloat16 [4, 8, 2, 1024], P(None, 'rows', None, 'frames')
- grad_coarse_k: bfloat16 [4, 8, 2, 1024], P(None, 'rows', None, 'frames')
- grad_coarse_v: bfloat16 [4, 8, 2, 1024], P(None, 'rows', None, 'frames')
All inputs are finite; a program needn't handle non-finite values.
Results may differ from a plain program's by a relative error of at most 0.023.
Values may be sent and summed in bfloat16 or wider, within the bound.
No kernel may reach another device: no remote copies, remote signals or barrier semaphores. Data moves between devices by JAX's collectives and lax.ppermute only.
A program may use at most 64 MiB of HBM per device.

v0:
```python
import math

import jax
import jax.numpy as jnp
from jax import lax
from jax.sharding import PartitionSpec as P

HD = 64
KERNEL = 7
POOL = 8


NEGATIVE = -1e30


def passed_along(value, axis, steps):
    count = lax.axis_size(axis)
    initial, last = (max(0, -steps), min(count, count - steps))
    return lax.ppermute(value, axis, [(source, source + steps) for source in range(initial, last)])


def extended(cells, sides, width):
    for axis, dim in sides:
        count = lax.axis_size(axis)
        ends = count - 1
        head = lax.slice_in_dim(cells, 0, width, axis=dim)
        tail = lax.slice_in_dim(cells, cells.shape[dim] - width, cells.shape[dim], axis=dim)
        cells = jnp.concatenate(
            [
                lax.ppermute(tail, axis, [(i, (i + 1) % count) for i in range(ends)]),
                cells,
                lax.ppermute(head, axis, [((i + 1) % count, i) for i in range(ends)]),
            ],
            axis=dim,
        )
    return cells


def normalize(scores):
    row_max = jnp.max(scores, axis=-1, keepdims=True)
    return row_max + jnp.log(jnp.sum(jnp.exp(scores - row_max), axis=-1, keepdims=True))


def pass_rim(rim, offset):
    return passed_along(rim.astype(jnp.bfloat16), "rows", offset).astype(rim.dtype)


def local(fine_q, fine_kv, coarse_q, coarse_kv, cotangent, gain_table, timesteps, valid_cols):
    score_scale = 1.0 / math.sqrt(HD)
    frame_dev = lax.axis_index("frames")
    row_dev = lax.axis_index("rows")
    row_devices = lax.axis_size("rows")
    frames_here, rows_here, cols_here, fine_width = fine_q.shape
    head_count = fine_width // HD
    radius = KERNEL // 2
    band_rows = rows_here + 2 * radius
    total_frames = valid_cols.shape[0]
    steps_all = gain_table.shape[0]
    tile_cols = 16
    tile_count = cols_here // tile_cols
    tile_keys = tile_cols + 2 * radius
    both_width = 2 * fine_width
    select = (timesteps[:, None] == jnp.arange(steps_all)[None, :]).astype(jnp.float32)
    frame_gain = jnp.dot(select, gain_table, precision=lax.Precision.HIGHEST)
    scaled_grad = frame_gain[:, None, None, :] * cotangent.astype(jnp.float32)
    grad_low = scaled_grad.astype(jnp.bfloat16)
    frame_ids = frame_dev * frames_here + jnp.arange(frames_here)
    frame_match = frame_ids[:, None] == jnp.arange(total_frames)[None, :]
    valid_here = jnp.sum(jnp.where(frame_match, valid_cols[None, :], 0), axis=1)
    half_pool = POOL // 2
    coarse_cols = cols_here // POOL
    coarse_width = coarse_q.shape[-1]
    coarse_count = frames_here * coarse_cols
    blocks = scaled_grad.reshape(frames_here, 2, half_pool, coarse_cols, 2, half_pool, fine_width)
    pooled = (
        jnp.sum(blocks, axis=(2, 5))
        .transpose(0, 2, 1, 3, 4)
        .reshape(coarse_count, coarse_width)
        .astype(jnp.bfloat16)
    )
    mine_query = coarse_q.reshape(coarse_count, coarse_width)
    mine_keys = coarse_kv[..., :coarse_width].reshape(coarse_count, coarse_width)
    mine_values = coarse_kv[..., coarse_width:].reshape(coarse_count, coarse_width)
    head_query, head_keys, head_values, head_grad = (
        lax.all_to_all(mine_query, "frames", split_axis=1, concat_axis=0, tiled=True),
        lax.all_to_all(mine_keys, "frames", split_axis=1, concat_axis=0, tiled=True),
        lax.all_to_all(mine_values, "frames", split_axis=1, concat_axis=0, tiled=True),
        lax.all_to_all(pooled, "frames", split_axis=1, concat_axis=0, tiled=True),
    )
    padded = extended(fine_kv, (("rows", 1),), radius)
    widened = jnp.pad(padded, ((0, 0), (0, 0), (radius, tile_cols - radius), (0, 0)))
    main_cols = widened[:, :, :cols_here].reshape(
        frames_here, band_rows, tile_count, tile_cols, both_width
    )
    extra_cols = widened[:, :, tile_cols:].reshape(
        frames_here, band_rows, tile_count, tile_cols, both_width
    )[:, :, :, : 2 * radius]
    kv_tiles = jnp.concatenate([main_cols, extra_cols], axis=3).transpose(0, 2, 1, 3, 4)
    key_count = band_rows * tile_keys
    query_count = rows_here * tile_cols
    kv_tiles = kv_tiles.reshape(frames_here, tile_count, key_count, both_width)
    key_wide = kv_tiles[..., :fine_width].reshape(
        frames_here, tile_count, key_count, head_count, HD
    )
    value_wide = kv_tiles[..., fine_width:].reshape(
        frames_here, tile_count, key_count, head_count, HD
    )

    def to_tiles(table):
        return (
            table.reshape(frames_here, rows_here, tile_count, tile_cols, fine_width)
            .transpose(0, 2, 1, 3, 4)
            .reshape(frames_here, tile_count, query_count, head_count, HD)
        )

    query_wide = to_tiles(fine_q)
    grad_wide = to_tiles(grad_low)
    query_index = jnp.arange(query_count)
    key_index = jnp.arange(key_count)
    query_row = query_index // tile_cols
    query_col = query_index % tile_cols
    key_row = key_index // tile_keys - radius
    key_col = key_index % tile_keys - radius
    row_gap = key_row[None, :] - query_row[:, None]
    col_gap = key_col[None, :] - query_col[:, None]
    key_global = row_dev * rows_here + key_row
    nearby = (
        (jnp.abs(row_gap) <= radius)
        & (jnp.abs(col_gap) <= radius)
        & ((key_global >= 0) & (key_global < rows_here * row_devices))[None, :]
    )
    centre = (row_gap == 0) & (col_gap == 0)
    col_global = jnp.arange(tile_count)[:, None] * tile_cols + key_col[None, :]
    col_fine = (col_global >= 0) & (col_global < cols_here)
    col_valid = col_fine[None] & (col_global[None] < valid_here[:, None, None])
    allowed = nearby[None, None] & col_valid[:, :, None, :] | centre[None, None]
    scores = (
        jnp.einsum("fnqhd,fnkhd->fnhqk", query_wide, key_wide, preferred_element_type=jnp.float32)
        * score_scale
    )
    scores = jnp.where(allowed[:, :, None], scores, NEGATIVE)
    weights = jnp.exp(scores - normalize(scores))
    weights_low = weights.astype(jnp.bfloat16)
    attended = jnp.einsum(
        "fnhqk,fnkhd->fnqhd", weights_low, value_wide, preferred_element_type=jnp.float32
    )
    row_dot = jnp.sum(grad_wide.astype(jnp.float32) * attended, axis=-1)
    weight_grad = jnp.einsum(
        "fnqhd,fnkhd->fnhqk", grad_wide, value_wide, preferred_element_type=jnp.float32
    )
    score_grad = (weights * (weight_grad - jnp.moveaxis(row_dot, 3, 2)[..., None])).astype(
        jnp.bfloat16
    )
    query_grad = (
        jnp.einsum("fnhqk,fnkhd->fnqhd", score_grad, key_wide, preferred_element_type=jnp.float32)
        * score_scale
    )
    key_grad = (
        jnp.einsum("fnhqk,fnqhd->fnkhd", score_grad, query_wide, preferred_element_type=jnp.float32)
        * score_scale
    )
    value_grad = jnp.einsum(
        "fnhqk,fnqhd->fnkhd", weights_low, grad_wide, preferred_element_type=jnp.float32
    )
    grad_fine_q = (
        query_grad.reshape(frames_here, tile_count, rows_here, tile_cols, fine_width)
        .transpose(0, 2, 1, 3, 4)
        .reshape(frames_here, rows_here, cols_here, fine_width)
        .astype(jnp.bfloat16)
    )
    tile_grads = jnp.concatenate(
        [
            key_grad.reshape(frames_here, tile_count, band_rows, tile_keys, fine_width),
            value_grad.reshape(frames_here, tile_count, band_rows, tile_keys, fine_width),
        ],
        axis=-1,
    )
    tile_grads = tile_grads.transpose(0, 2, 1, 3, 4)
    main_part = tile_grads[:, :, :, :tile_cols].reshape(
        frames_here, band_rows, cols_here, both_width
    )
    extra_part = jnp.pad(
        tile_grads[:, :, :, tile_cols:],
        ((0, 0), (0, 0), (0, 0), (0, tile_cols - 2 * radius), (0, 0)),
    ).reshape(frames_here, band_rows, cols_here, both_width)
    summed_cols = jnp.zeros(
        (frames_here, band_rows, cols_here + tile_cols, both_width), jnp.float32
    )
    summed_cols = (
        summed_cols.at[:, :, :cols_here].add(main_part).at[:, :, tile_cols:].add(extra_part)
    )
    key_value = summed_cols[:, :, radius : radius + cols_here]
    owned_rows = key_value[:, radius : radius + rows_here]
    from_below = pass_rim(key_value[:, :radius], -1)
    from_above = pass_rim(key_value[:, radius + rows_here :], 1)
    owned_rows = (
        owned_rows.at[:, :radius].add(from_above).at[:, rows_here - radius :].add(from_below)
    )
    grad_fine_kv = owned_rows.astype(jnp.bfloat16)
    head_tokens, head_width = head_query.shape
    head_groups = head_width // HD
    query_heads = head_query.reshape(head_tokens, head_groups, HD)
    grad_heads = head_grad.reshape(head_tokens, head_groups, HD)
    every_keys, every_values = (
        lax.all_gather(head_keys, "rows", axis=0, tiled=True),
        lax.all_gather(head_values, "rows", axis=0, tiled=True),
    )
    every_count = every_keys.shape[0]
    key_heads = every_keys.reshape(every_count, head_groups, HD)
    value_heads = every_values.reshape(every_count, head_groups, HD)
    position = jnp.arange(every_count) % head_tokens
    key_frame = position // coarse_cols
    key_column = position % coarse_cols
    col_limit = jnp.sum(
        jnp.where(key_frame[:, None] == jnp.arange(total_frames)[None, :], valid_cols[None, :], 0),
        axis=1,
    )
    key_ok = key_column * POOL < col_limit
    coarse_scores = (
        jnp.einsum("qhd,khd->hqk", query_heads, key_heads, preferred_element_type=jnp.float32)
        * score_scale
    )
    coarse_scores = jnp.where(key_ok[None, None, :], coarse_scores, NEGATIVE)
    log_total = normalize(coarse_scores)
    coarse_weights = jnp.exp(coarse_scores - log_total)
    coarse_low = coarse_weights.astype(jnp.bfloat16)
    coarse_out = jnp.einsum(
        "hqk,khd->qhd", coarse_low, value_heads, preferred_element_type=jnp.float32
    )
    coarse_dot = jnp.sum(grad_heads.astype(jnp.float32) * coarse_out, axis=-1)
    coarse_wgrad = jnp.einsum(
        "qhd,khd->hqk", grad_heads, value_heads, preferred_element_type=jnp.float32
    )
    coarse_sgrad = (coarse_weights * (coarse_wgrad - coarse_dot.T[:, :, None])).astype(jnp.bfloat16)
    coarse_qgrad = (
        jnp.einsum("hqk,khd->qhd", coarse_sgrad, key_heads, preferred_element_type=jnp.float32)
        * score_scale
    )
    count = head_tokens * lax.axis_size("rows")
    key_part = (
        jnp.einsum("hqk,qhd->khd", coarse_sgrad, query_heads, preferred_element_type=jnp.float32)
        * score_scale
    )
    value_part = jnp.einsum(
        "hqk,qhd->khd", coarse_low, grad_heads, preferred_element_type=jnp.float32
    )
    terms = lax.psum_scatter(
        jnp.concatenate(
            [key_part.reshape(count, head_width), value_part.reshape(count, head_width)], axis=1
        ),
        "rows",
        scatter_dimension=0,
        tiled=True,
    )
    total_keys = terms[:, :head_width]
    total_values = terms[:, head_width:]
    out_dims = (head_tokens // coarse_cols, 1, coarse_cols, head_width)
    grad_coarse_q = coarse_qgrad.reshape(out_dims).astype(jnp.bfloat16)
    grad_coarse_k = total_keys.reshape(out_dims).astype(jnp.bfloat16)
    grad_coarse_v = total_values.reshape(out_dims).astype(jnp.bfloat16)
    return (grad_fine_q, grad_fine_kv, grad_coarse_q, grad_coarse_k, grad_coarse_v)


def solution(mesh):
    placed = (
        P("frames", "rows", None, None),
        P("frames", "rows", None, None),
        P("frames", "rows", None, None),
        P("frames", "rows", None, None),
        P("frames", "rows", None, None),
        P(),
        P("frames"),
        P(),
    )
    return jax.shard_map(
        local,
        mesh=mesh,
        in_specs=placed,
        out_specs=(
            P("frames", "rows", None, None),
            P("frames", "rows", None, None),
            P(None, "rows", None, "frames"),
            P(None, "rows", None, "frames"),
            P(None, "rows", None, "frames"),
        ),
        check_vma=False,
    )
```

profile of v0, /device:TPU:0, one launch (start us, length us, event | category | flops | bytes accessed | tf_op | source)
XLA Modules:
  0.0 176.9 jit_solution(3862449581879356350)
XLA Ops:
  7.2 1.4 fusion.67
  8.6 4.2 %all-to-all-start.3 = ((bf16[2,4,256]{2,0,1:T(2,128)(2,1)}), bf16[2,4,256]{2,0,1:T(2,128)(2,1)S(1)}, u32[]{:S(2)}, u32[]{:S(2)}) async-start(bf16[2,4,256]{2,0,1:T(2,128)(2,1)} %bitcast.30), calls=%async_computation.3 | async-start | bytes 8192 | tf_op jit(solution)/shard_map/all_to_all | solution.py:87
  12.8 0.8 fusion.65
  13.6 3.9 %collective-permute-start = (bf16[1,3,16,512]{3,2,1,0:T(8,128)(2,1)S(1)}, bf16[1,3,16,512]{3,2,1,0:T(8,128)(2,1)S(1)}, u32[]{:S(2)}, u32[]{:S(2)}) collective-permute-start(bf16[1,3,16,512]{3,2,1,0:T(8,128)(2,1)S(1)} %get-tuple-element.79), channel_id=1, source_target_pairs={{0,1},{1,2},{2,3},{3,4},{4,5},{5,6},{6,7},{8,9},{9,10},{10,11},{11... | collective-permute-start | bytes 147464 | tf_op jit(solution)/shard_map/ppermute | solution.py:30
  17.5 1.3 collective-permute-start.1
  19.5 0.6 copy-done.4
  20.2 0.6 fusion.60
  20.8 0.7 compare_and_fusion
  22.6 3.3 %all-to-all-start.1 = ((bf16[2,4,256]{2,0,1:T(2,128)(2,1)}), bf16[2,4,256]{2,0,1:T(2,128)(2,1)S(1)}, u32[]{:S(2)}, u32[]{:S(2)}) async-start(bf16[2,4,256]{2,0,1:T(2,128)(2,1)} %bitcast.24), calls=%async_computation.1 | async-start | bytes 8192 | tf_op jit(solution)/shard_map/all_to_all | solution.py:86
  26.0 3.7 %all-to-all-done.1 = bf16[2,4,256]{2,0,1:T(2,128)(2,1)S(1)} async-done(((bf16[2,4,256]{2,0,1:T(2,128)(2,1)}), bf16[2,4,256]{2,0,1:T(2,128)(2,1)S(1)}, u32[]{:S(2)}, u32[]{:S(2)}) %all-to-all-start.1) | async-done | bytes 4128 | tf_op jit(solution)/shard_map/all_to_all | solution.py:86
  29.7 3.2 %all-to-all-start = ((bf16[2,4,256]{2,0,1:T(2,128)(2,1)}), bf16[2,4,256]{2,0,1:T(2,128)(2,1)S(1)}, u32[]{:S(2)}, u32[]{:S(2)}) async-start(bf16[2,4,256]{2,0,1:T(2,128)(2,1)} %bitcast.22), calls=%async_computation | async-start | bytes 8192 | tf_op jit(solution)/shard_map/all_to_all | solution.py:85
  33.2 0.7 copy-done.2
  34.2 0.6 copy.98
  35.1 1.6 all-to-all-done
  36.7 3.2 %all-to-all-start.2 = ((bf16[2,4,256]{2,0,1:T(2,128)(2,1)}), bf16[2,4,256]{2,0,1:T(2,128)(2,1)S(1)}, u32[]{:S(2)}, u32[]{:S(2)}) async-start(bf16[2,4,256]{2,0,1:T(2,128)(2,1)} %bitcast.28), calls=%async_computation.2 | async-start | bytes 8192 | tf_op jit(solution)/shard_map/all_to_all | solution.py:88
  40.1 32.8 %all_gather.6 = bf16[64,256]{1,0:T(8,128)(2,1)S(1)} all-gather(bf16[8,256]{1,0:T(8,128)(2,1)S(1)} %all_to_all.56), channel_id=1, replica_groups=mesh['frames'=4,'rows'=8] {'rows'}, dimensions={0}, use_global_device_ids=true | all-gather | bytes 36864 | tf_op jit(solution)/shard_map/all_gather | solution.py:205
  73.4 30.4 %all_gather.7 = bf16[64,256]{1,0:T(8,128)(2,1)S(1)} all-gather(bf16[8,256]{1,0:T(8,128)(2,1)S(1)} %all_to_all.62), channel_id=1, replica_groups=mesh['frames'=4,'rows'=8] {'rows'}, dimensions={0}, use_global_device_ids=true | all-gather | bytes 36864 | tf_op jit(solution)/shard_map/all_gather | solution.py:206
  105.3 0.7 pad_maximum_fusion.1
  106.0 0.7 convert_element_type.149
  109.8 0.6 reshape.640
  110.7 0.6 reshape.641
  111.3 0.5 maximum_bitcast_fusion
  112.7 1.0 maximum_convert_fusion
  113.9 2.5 %collective-permute-start.2 = (bf16[1,3,16,512]{3,0,2,1:T(2,128)(2,1)S(1)}, bf16[1,3,16,512]{3,0,2,1:T(2,128)(2,1)S(1)}, u32[]{:S(2)}, u32[]{:S(2)}) collective-permute-start(bf16[1,3,16,512]{3,0,2,1:T(2,128)(2,1)S(1)} %get-tuple-element.74), channel_id=1, source_target_pairs={{0,1},{1,2},{2,3},{3,4},{4,5},{5,6},{6,7},{8,9},{9,10},{10,11},{11... | collective-permute-start | bytes 147464 | tf_op jit(solution)/shard_map/ppermute | solution.py:19
  116.8 0.8 convert_element_type.136
  117.6 1.3 collective-permute-start.3
  119.1 5.0 %collective-permute-done.3 = bf16[1,3,16,512]{3,0,2,1:T(2,128)(2,1)S(1)} collective-permute-done((bf16[1,3,16,512]{3,0,2,1:T(2,128)(2,1)S(1)}, bf16[1,3,16,512]{3,0,2,1:T(2,128)(2,1)S(1)}, u32[]{:S(2)}, u32[]{:S(2)}) %collective-permute-start.3) | collective-permute-done | bytes 49184 | tf_op jit(solution)/shard_map/ppermute | solution.py:19
  124.5 0.7 copy.110
  125.2 42.9 %reduce-scatter.2.cloned.1.call-done = f32[8,512]{1,0:T(8,128)} async-done(((f32[64,512]{1,0:T(8,128)}), f32[8,512]{1,0:T(8,128)}) %reduce-scatter.2.cloned.1.call-update) | async-done | bytes 16400 | tf_op jit(solution)/shard_map/reduce_scatter | solution.py:247
  168.1 0.7 convert.10
  168.9 0.6 convert_element_type.151
  169.5 0.6 convert_element_type.150
  (79 shorter events, 9.5 us)
Async XLA Ops:
  7.2 14.3 %copy-start = (f32[1000,256]{1,0:T(8,128)S(1)}, f32[1000,256]{1,0:T(8,128)}, u32[]{:S(2)}) copy-start(f32[1000,256]{1,0:T(8,128)} %param.21) | copy-start | bytes 3072004
  8.6 14.0 %all-to-all-start.3 = ((bf16[2,4,256]{2,0,1:T(2,128)(2,1)}), bf16[2,4,256]{2,0,1:T(2,128)(2,1)S(1)}, u32[]{:S(2)}, u32[]{:S(2)}) async-start(bf16[2,4,256]{2,0,1:T(2,128)(2,1)} %bitcast.30), calls=%async_computation.3 | async-start | bytes 8192 | tf_op jit(solution)/shard_map/all_to_all | solution.py:87
  13.6 93.1 %collective-permute-start = (bf16[1,3,16,512]{3,2,1,0:T(8,128)(2,1)S(1)}, bf16[1,3,16,512]{3,2,1,0:T(8,128)(2,1)S(1)}, u32[]{:S(2)}, u32[]{:S(2)}) collective-permute-start(bf16[1,3,16,512]{3,2,1,0:T(8,128)(2,1)S(1)} %get-tuple-element.79), channel_id=1, source_target_pairs={{0,1},{1,2},{2,3},{3,4},{4,5},{5,6},{6,7},{8,9},{9,10},{10,11},{11... | collective-permute-start | bytes 147464 | tf_op jit(solution)/shard_map/ppermute | solution.py:30
  17.5 89.2 %collective-permute-start.1 = (bf16[1,3,16,512]{3,2,1,0:T(8,128)(2,1)S(1)}, bf16[1,3,16,512]{3,2,1,0:T(8,128)(2,1)S(1)}, u32[]{:S(2)}, u32[]{:S(2)}) collective-permute-start(bf16[1,3,16,512]{3,2,1,0:T(8,128)(2,1)S(1)} %get-tuple-element.80), channel_id=1, source_target_pairs={{1,0},{2,1},{3,2},{4,3},{5,4},{6,5},{7,6},{9,8},{10,9},{11,10},{12... | collective-permute-start | bytes 147464 | tf_op jit(solution)/shard_map/ppermute | solution.py:32
  19.5 0.7 copy-start.4
  21.5 0.8 copy-start.3
  22.6 7.1 %all-to-all-start.1 = ((bf16[2,4,256]{2,0,1:T(2,128)(2,1)}), bf16[2,4,256]{2,0,1:T(2,128)(2,1)S(1)}, u32[]{:S(2)}, u32[]{:S(2)}) async-start(bf16[2,4,256]{2,0,1:T(2,128)(2,1)} %bitcast.24), calls=%async_computation.1 | async-start | bytes 8192 | tf_op jit(solution)/shard_map/all_to_all | solution.py:86
  29.7 7.0 %all-to-all-start = ((bf16[2,4,256]{2,0,1:T(2,128)(2,1)}), bf16[2,4,256]{2,0,1:T(2,128)(2,1)S(1)}, u32[]{:S(2)}, u32[]{:S(2)}) async-start(bf16[2,4,256]{2,0,1:T(2,128)(2,1)} %bitcast.22), calls=%async_computation | async-start | bytes 8192 | tf_op jit(solution)/shard_map/all_to_all | solution.py:85
  33.1 0.8 copy-start.2
  36.7 67.2 %all-to-all-start.2 = ((bf16[2,4,256]{2,0,1:T(2,128)(2,1)}), bf16[2,4,256]{2,0,1:T(2,128)(2,1)S(1)}, u32[]{:S(2)}, u32[]{:S(2)}) async-start(bf16[2,4,256]{2,0,1:T(2,128)(2,1)} %bitcast.28), calls=%async_computation.2 | async-start | bytes 8192 | tf_op jit(solution)/shard_map/all_to_all | solution.py:88
  39.9 128.2 %reduce-scatter.2.cloned.1.call-start = ((), (), s32[]{:S(2)}) async-start(), calls=%async_computation.5 | async-start | bytes 147456 | tf_op jit(solution)/shard_map/reduce_scatter | solution.py:247
  106.0 0.9 copy-start.1
  113.9 5.0 %collective-permute-start.2 = (bf16[1,3,16,512]{3,0,2,1:T(2,128)(2,1)S(1)}, bf16[1,3,16,512]{3,0,2,1:T(2,128)(2,1)S(1)}, u32[]{:S(2)}, u32[]{:S(2)}) collective-permute-start(bf16[1,3,16,512]{3,0,2,1:T(2,128)(2,1)S(1)} %get-tuple-element.74), channel_id=1, source_target_pairs={{0,1},{1,2},{2,3},{3,4},{4,5},{5,6},{6,7},{8,9},{9,10},{10,11},{11... | collective-permute-start | bytes 147464 | tf_op jit(solution)/shard_map/ppermute | solution.py:19
  117.6 6.5 %collective-permute-start.3 = (bf16[1,3,16,512]{3,0,2,1:T(2,128)(2,1)S(1)}, bf16[1,3,16,512]{3,0,2,1:T(2,128)(2,1)S(1)}, u32[]{:S(2)}, u32[]{:S(2)}) collective-permute-start(bf16[1,3,16,512]{3,0,2,1:T(2,128)(2,1)S(1)} %get-tuple-element.73), channel_id=1, source_target_pairs={{1,0},{2,1},{3,2},{4,3},{5,4},{6,5},{7,6},{9,8},{10,9},{11,10},{12... | collective-permute-start | bytes 147464 | tf_op jit(solution)/shard_map/ppermute | solution.py:19
Sparse Core Ops, SparseCore 0:
  106.8 61.2 reduce-scatter.1
where the time goes:
time: 178 us; the launch traced here: 177 us
  blocking collectives  63.2 us (36%)
  waiting for transfers between devices  53.2 us (30%)
  starting transfers between devices  23 us (13%)
  between operations  15.2 us (9%)
  local copies, waits for them, and re-layouts  13 us (7%)
  other arithmetic  5.97 us (3%)
  matrix products  3.41 us (2%)
    reduce_scatter x1, waiting for transfers between devices, local(): lax.psum_scatter(jnp.concatenate([key_part.reshape(count, head_width), va...  42.9 us
    all_gather x1, blocking collectives, local(): lax.all_gather(head_keys, 'rows', axis=0, tiled=True)  32.8 us
    all_gather x1, blocking collectives, local(): lax.all_gather(head_values, 'rows', axis=0, tiled=True)  30.4 us
    ppermute x2, waiting for transfers between devices, passed_along(): lax.ppermute(value, axis, [(source, source + steps) for source in range(i...  5.04 us
    all_to_all x1, starting transfers between devices, local(): lax.all_to_all(mine_values, 'frames', split_axis=1, concat_axis=0, tiled=...  4.24 us
    ppermute x1, starting transfers between devices, extended(): lax.ppermute(tail, axis, [(i, (i + 1) % count) for i in range(ends)])  3.86 us
    ppermute x2, starting transfers between devices, passed_along(): lax.ppermute(value, axis, [(source, source + steps) for source in range(i...  3.78 us
    all_to_all x1, waiting for transfers between devices, local(): lax.all_to_all(mine_keys, 'frames', split_axis=1, concat_axis=0, tiled=True)  3.7 us
  transfers between devices with their start and end apart: 9, of which 4 were waited for; matrix products, arithmetic and copies ran while one was open for 10% of the time, Pallas kernels for 0%

commit v1 on v0

v1 whole, which is shorter than its diff:
```python
import functools
import math

import jax
import jax.numpy as jnp
from jax import lax
from jax.experimental import pallas as pl
from jax.experimental.pallas import tpu as pltpu
from jax.sharding import PartitionSpec as P

HD = 64
KERNEL = 7
POOL = 8
LANES = 128

NEGATIVE = -1e30

F32 = jnp.float32
BF16 = jnp.bfloat16


def dot_nt(left, right):
    return lax.dot_general(left, right, (((1,), (1,)), ((), ())), preferred_element_type=F32)


def dot_nn(left, right):
    return jnp.dot(left, right, preferred_element_type=F32)


def iota(shape, dim):
    return lax.broadcasted_iota(jnp.int32, shape, dim)


def per_head(table):
    head = iota(table.shape, 1) // HD
    return [jnp.where(head == h, table, jnp.zeros_like(table)) for h in range(table.shape[1] // HD)]


def softmax_grads(scores, weight_grad, axis):
    top = jnp.max(scores, axis=axis, keepdims=True)
    raised = jnp.exp(scores - top)
    weights = raised * (1.0 / jnp.sum(raised, axis=axis, keepdims=True))
    low = weights.astype(BF16)
    row_dot = jnp.sum(low.astype(F32) * weight_grad, axis=axis, keepdims=True)
    return low, (weights * (weight_grad - row_dot)).astype(BF16)


def gain_row(step_ref, gain_ref):
    step = step_ref[0] % gain_ref.shape[0]
    rows = iota(gain_ref.shape, 0)
    return jnp.sum(jnp.where(rows == step, gain_ref[...], 0.0), axis=0, keepdims=True)


def prep_kernel(cols, step_ref, q_ref, kv_ref, cot_ref, gain_ref, near_ref, far_ref, grad_ref):
    radius = KERNEL // 2
    pixels, width = q_ref.shape
    one, two = radius * cols, 2 * radius * cols
    even = lax.axis_index("rows") % 2 == 0
    gain = gain_row(step_ref, gain_ref)
    grad_ref[...] = (gain * cot_ref[...].astype(F32)).astype(BF16)

    def pack(target, top):
        lo_one, lo_two = (0, 0) if top else (pixels - one, pixels - two)
        target[:two, :] = kv_ref[lo_two : lo_two + two, :]
        target[two:, :width] = q_ref[lo_one : lo_one + one, :]
        target[two:, width:] = grad_ref[lo_one : lo_one + one, :]

    @pl.when(even)
    def _():
        pack(near_ref, False)
        pack(far_ref, True)

    @pl.when(jnp.logical_not(even))
    def _():
        pack(near_ref, True)
        pack(far_ref, False)


def send_kernel(cols, bands, step_ref, cot_ref, gain_ref, cq_ref, ckv_ref, send_ref):
    pixels, width = cot_ref.shape
    tokens, cwidth = cq_ref.shape
    half = POOL // 2
    groups = cwidth // width
    part = iota((groups * tokens, pixels), 0)
    group, token = part // tokens, part % tokens
    pixel = iota((groups * tokens, pixels), 1)
    row, col = pixel // cols, pixel % cols
    inside = (row // half == group // 2) & (col // half == token * 2 + group % 2)
    pooled = dot_nn(inside.astype(BF16), cot_ref[...]) * gain_row(step_ref, gain_ref)
    query = cq_ref[...].astype(F32)
    both = ckv_ref[...].astype(F32)
    for g in range(groups):
        lo = g * width
        arrays = (
            query[:, lo : lo + width],
            both[:, lo : lo + width],
            both[:, cwidth + lo : cwidth + lo + width],
            pooled[g * tokens : (g + 1) * tokens, :],
        )
        tile = jnp.concatenate(
            [a[:, b : b + LANES] for a in arrays for b in range(0, width, LANES)], axis=0
        ).astype(BF16)
        height = tile.shape[0]
        for r in range(bands):
            start = (g * bands + r) * height
            send_ref[start : start + height, :] = tile


def fine_kernel(cols, valid_ref, q_ref, kv_ref, grad_ref, near_ref, far_ref, dq_ref, dkv_ref):
    radius = KERNEL // 2
    pixels, width = q_ref.shape
    rows = pixels // cols
    one, two = radius * cols, 2 * radius * cols
    scale = 1.0 / math.sqrt(HD)
    band = lax.axis_index("rows")
    valid = valid_ref[lax.axis_index("frames")]
    first, last = band == 0, band == lax.axis_size("rows") - 1
    even = band % 2 == 0

    def received(rows_at, cols_at):
        near, far = near_ref[rows_at, cols_at], far_ref[rows_at, cols_at]
        return jnp.where(even, far, near), jnp.where(even, near, far)

    def extended(cols_at):
        above, below = received(slice(0, two), cols_at)
        return jnp.concatenate([above, kv_ref[:, cols_at], below], axis=0)

    keys, values = extended(slice(0, width)), extended(slice(width, 2 * width))
    q_above, q_below = received(slice(two, two + one), slice(0, width))
    g_above, g_below = received(slice(two, two + one), slice(width, 2 * width))

    def bias(key_count, key_row, lanes, query_count, query_row, ends):
        key, lane = iota((key_count, lanes), 0), iota((key_count, lanes), 1) % query_count
        krow, kcol = key // cols + key_row, key % cols
        qrow, qcol = lane // cols + query_row, lane % cols
        seen = (jnp.abs(krow - qrow) <= radius) & (jnp.abs(kcol - qcol) <= radius) & (kcol < valid)
        if ends:
            seen = seen & ((krow >= 0) | jnp.logical_not(first))
            seen = seen & ((krow < rows) | jnp.logical_not(last))
        seen = seen | ((krow == qrow) & (kcol == qcol))
        return jnp.where(seen, 0.0, NEGATIVE)

    lo, hi = one, one + pixels + two
    own_keys, own_values = keys[lo:hi], values[lo:hi]
    own_bias = bias(hi - lo, -radius, pixels, pixels, 0, True)
    queries, grads = per_head(q_ref[...] * scale), per_head(grad_ref[...])
    keys_t = own_keys.T
    lows, sgrads, dq_t = [], [], []
    for h, (query, grad) in enumerate(zip(queries, grads)):
        low, sgrad = softmax_grads(
            dot_nt(own_keys, query) + own_bias, dot_nt(own_values, grad), 0
        )
        lows.append(low[one : one + pixels])
        sgrads.append(sgrad[one : one + pixels])
        dq_t.append(dot_nn(keys_t[h * HD : (h + 1) * HD], sgrad))
    dq_ref[...] = (jnp.concatenate(dq_t, axis=0).T * scale).astype(BF16)
    dk = dot_nn(jnp.concatenate(sgrads, axis=1), jnp.concatenate(queries, axis=0))
    dv = dot_nn(jnp.concatenate(lows, axis=1), jnp.concatenate(grads, axis=0))

    pad = jnp.zeros((cols, width), BF16)

    def outside(query, grad, key_lo, key_row, query_row, keep):
        stacked = [
            jnp.concatenate([x for head in per_head(t) for x in (head, pad)], axis=0)
            for t in (query * scale, grad)
        ]
        count = one + two
        lanes = stacked[0].shape[0]
        low, sgrad = softmax_grads(
            dot_nt(keys[key_lo : key_lo + count], stacked[0])
            + bias(count, key_row, lanes, one + cols, query_row, False),
            dot_nt(values[key_lo : key_lo + count], stacked[1]),
            0,
        )
        return (
            dot_nn(sgrad[keep : keep + one], stacked[0]),
            dot_nn(low[keep : keep + one], stacked[1]),
        )

    dk_above, dv_above = outside(q_above, g_above, 0, -2 * radius, -radius, two)
    dk_below, dv_below = outside(q_below, g_below, pixels + one, rows - radius, rows, 0)
    for at, (inner, above, below) in enumerate(((dk, dk_above, dk_below), (dv, dv_above, dv_below))):
        dkv_ref[:, at * width : (at + 1) * width] = jnp.concatenate(
            [inner[:one] + above, inner[one : pixels - one], inner[pixels - one :] + below], axis=0
        ).astype(BF16)


def coarse_kernel(frames, tokens, valid_ref, x_ref, dq_ref, dk_ref, dv_ref, wide, low_ref, sg_ref):
    bands = lax.axis_size("rows")
    width = dq_ref.shape[-1]
    parts = width // LANES
    height = x_ref.shape[0] // (frames * bands)
    band = lax.axis_index("rows")
    scale = 1.0 / math.sqrt(HD)
    wide[...] = x_ref[...].astype(F32)

    def every(array):
        def piece(t, b):
            return wide[pl.ds((array * parts + b) * tokens + t, frames * bands, stride=height), :]

        return jnp.concatenate(
            [
                jnp.concatenate([piece(t, b) for b in range(parts)], axis=1)
                for t in range(tokens)
            ],
            axis=0,
        ).astype(BF16)

    def mine(array):
        def piece(f, b):
            start = (f * bands + band) * height + (array * parts + b) * tokens
            return wide[pl.ds(start, tokens), :]

        return jnp.concatenate(
            [
                jnp.concatenate([piece(f, b) for b in range(parts)], axis=1)
                for f in range(frames)
            ],
            axis=0,
        ).astype(BF16)

    query, key, value, grad = (every(a) for a in range(4))
    count = query.shape[0]

    def key_bias(shape, dim):
        place = iota(shape, dim)
        token, frame = place // (frames * bands), place // bands % frames
        limit = jnp.zeros(shape, jnp.int32)
        for f in range(frames):
            limit = jnp.where(frame == f, valid_ref[f], limit)
        return jnp.where(token * POOL < limit, 0.0, NEGATIVE)

    own_query, own_grad = per_head(mine(0) * scale), per_head(mine(3))
    own = frames * tokens
    heads = len(own_query)
    stacked = jnp.concatenate(own_query, axis=0)
    _, sgrad = softmax_grads(
        dot_nt(stacked, key) + key_bias((heads * own, count), 1),
        dot_nt(jnp.concatenate(own_grad, axis=0), value),
        1,
    )
    full = dot_nn(sgrad, key)
    head = iota((own, width), 1) // HD
    dq = sum(
        jnp.where(head == h, full[h * own : (h + 1) * own], 0.0) for h in range(heads)
    )
    queries = jnp.concatenate(per_head(query * scale), axis=0)
    grads = jnp.concatenate(per_head(grad), axis=0)
    low, sgrad = softmax_grads(
        dot_nt(key, queries) + key_bias((count, heads * count), 0), dot_nt(value, grads), 0
    )
    low_ref[...] = low.astype(F32)
    sg_ref[...] = sgrad.astype(F32)

    def mine_rows(ref):
        pieces = [
            ref[pl.ds(t * frames * bands + f * bands + band, 1), :]
            for f in range(frames)
            for t in range(tokens)
        ]
        return jnp.concatenate(pieces, axis=0).astype(BF16)

    dk = dot_nn(mine_rows(sg_ref), queries)
    dv = dot_nn(mine_rows(low_ref), grads)
    for ref, table in ((dq_ref, dq * scale), (dk_ref, dk), (dv_ref, dv)):
        rounded = table.astype(BF16)
        for f in range(frames):
            ref[f] = rounded[f * tokens : (f + 1) * tokens]


def vmem():
    return pl.BlockSpec(memory_space=pltpu.VMEM)


def smem():
    return pl.BlockSpec(memory_space=pltpu.SMEM)


def with_gain(kernel, ins, outs, scratch=()):
    def whole(shape):
        return pl.BlockSpec(shape, lambda i, step: (0,) * len(shape))

    def call(step, *operands):
        specs = [
            whole(x.shape)
            if at != ins
            else pl.BlockSpec((8, x.shape[1]), lambda i, step: (step[0] // 8, 0))
            for at, x in enumerate(operands)
        ]
        return pl.pallas_call(
            kernel,
            grid_spec=pltpu.PrefetchScalarGridSpec(
                num_scalar_prefetch=1,
                grid=(1,),
                in_specs=specs,
                out_specs=[whole(shape) for shape in outs],
                scratch_shapes=scratch,
            ),
            out_shape=[jax.ShapeDtypeStruct(shape, BF16) for shape in outs],
        )(step, *operands)

    return call


def fine_level(fine_q, fine_kv, cotangent, gain_table, timesteps, valid_cols):
    bands = lax.axis_size("rows")
    _, rows, cols, width = fine_q.shape
    pixels = rows * cols
    radius = KERNEL // 2
    query = fine_q.reshape(pixels, width)
    key_value = fine_kv.reshape(pixels, 2 * width)
    cot = cotangent.reshape(pixels, width)
    packed = (3 * radius * cols, 2 * width)
    near, far, grad = with_gain(
        functools.partial(prep_kernel, cols), 3, (packed, packed, (pixels, width))
    )(timesteps, query, key_value, cot, gain_table)
    pairs = [(i, i ^ 1) for i in range(bands) if i ^ 1 < bands]
    others = [(i, ((i + 1) ^ 1) - 1) for i in range(1, bands) if ((i + 1) ^ 1) - 1 < bands]
    near = lax.ppermute(near, "rows", pairs)
    far = lax.ppermute(far, "rows", others)
    grad_q, grad_kv = pl.pallas_call(
        functools.partial(fine_kernel, cols),
        in_specs=[smem()] + [vmem()] * 5,
        out_specs=[vmem()] * 2,
        out_shape=[
            jax.ShapeDtypeStruct((pixels, width), BF16),
            jax.ShapeDtypeStruct((pixels, 2 * width), BF16),
        ],
        cost_estimate=pl.CostEstimate(flops=400_000_000, bytes_accessed=1_000_000, transcendentals=300_000),
    )(valid_cols, query, key_value, grad, near, far)
    return grad_q.reshape(fine_q.shape), grad_kv.reshape(fine_kv.shape)


def coarse_direct(coarse_q, coarse_kv, cotangent, gain_table, timesteps, valid_cols):
    frames, bands = lax.axis_size("frames"), lax.axis_size("rows")
    _, rows, cols, width = cotangent.shape
    tokens, cwidth = coarse_q.shape[-2:]
    head_width = cwidth // frames
    tile = 4 * tokens * head_width // LANES
    (sent,) = with_gain(
        functools.partial(send_kernel, cols, bands), 1, ((frames * bands * tile, LANES),)
    )(
        timesteps,
        cotangent.reshape(rows * cols, width),
        gain_table,
        coarse_q.reshape(tokens, cwidth),
        coarse_kv.reshape(tokens, 2 * cwidth),
    )
    held = lax.all_to_all(
        sent.reshape(frames * bands, tile, LANES),
        ("frames", "rows"),
        split_axis=0,
        concat_axis=0,
        tiled=True,
    ).reshape(frames * bands * tile, LANES)
    count = frames * bands * tokens
    heads = head_width // HD
    outs = pl.pallas_call(
        functools.partial(coarse_kernel, frames, tokens),
        in_specs=[smem(), vmem()],
        out_specs=[vmem()] * 3,
        out_shape=[jax.ShapeDtypeStruct((frames, tokens, head_width), BF16)] * 3,
        scratch_shapes=[
            pltpu.VMEM(held.shape, F32),
            pltpu.VMEM((count, heads * count), F32),
            pltpu.VMEM((count, heads * count), F32),
        ],
    )(valid_cols, held)
    return tuple(out.reshape(frames, 1, tokens, head_width) for out in outs)


def normalize(scores):
    row_max = jnp.max(scores, axis=-1, keepdims=True)
    return row_max + jnp.log(jnp.sum(jnp.exp(scores - row_max), axis=-1, keepdims=True))


def coarse_gathered(coarse_q, coarse_kv, cotangent, gain_table, timesteps, valid_cols):
    score_scale = 1.0 / math.sqrt(HD)
    frames_here, _, cols_here, fine_width = cotangent.shape
    total_frames = valid_cols.shape[0]
    steps_all = gain_table.shape[0]
    select = (timesteps[:, None] == jnp.arange(steps_all)[None, :]).astype(F32)
    frame_gain = jnp.dot(select, gain_table, precision=lax.Precision.HIGHEST)
    scaled_grad = frame_gain[:, None, None, :] * cotangent.astype(F32)
    half_pool = POOL // 2
    coarse_cols = cols_here // POOL
    coarse_width = coarse_q.shape[-1]
    coarse_count = frames_here * coarse_cols
    blocks = scaled_grad.reshape(frames_here, 2, half_pool, coarse_cols, 2, half_pool, fine_width)
    pooled = (
        jnp.sum(blocks, axis=(2, 5))
        .transpose(0, 2, 1, 3, 4)
        .reshape(coarse_count, coarse_width)
        .astype(BF16)
    )
    mine_query = coarse_q.reshape(coarse_count, coarse_width)
    mine_keys = coarse_kv[..., :coarse_width].reshape(coarse_count, coarse_width)
    mine_values = coarse_kv[..., coarse_width:].reshape(coarse_count, coarse_width)
    head_query, head_keys, head_values, head_grad = (
        lax.all_to_all(mine_query, "frames", split_axis=1, concat_axis=0, tiled=True),
        lax.all_to_all(mine_keys, "frames", split_axis=1, concat_axis=0, tiled=True),
        lax.all_to_all(mine_values, "frames", split_axis=1, concat_axis=0, tiled=True),
        lax.all_to_all(pooled, "frames", split_axis=1, concat_axis=0, tiled=True),
    )
    head_tokens, head_width = head_query.shape
    head_groups = head_width // HD
    query_heads = head_query.reshape(head_tokens, head_groups, HD)
    grad_heads = head_grad.reshape(head_tokens, head_groups, HD)
    every_keys, every_values = (
        lax.all_gather(head_keys, "rows", axis=0, tiled=True),
        lax.all_gather(head_values, "rows", axis=0, tiled=True),
    )
    every_count = every_keys.shape[0]
    key_heads = every_keys.reshape(every_count, head_groups, HD)
    value_heads = every_values.reshape(every_count, head_groups, HD)
    position = jnp.arange(every_count) % head_tokens
    key_frame = position // coarse_cols
    key_column = position % coarse_cols
    col_limit = jnp.sum(
        jnp.where(key_frame[:, None] == jnp.arange(total_frames)[None, :], valid_cols[None, :], 0),
        axis=1,
    )
    key_ok = key_column * POOL < col_limit
    coarse_scores = (
        jnp.einsum("qhd,khd->hqk", query_heads, key_heads, preferred_element_type=F32)
        * score_scale
    )
    coarse_scores = jnp.where(key_ok[None, None, :], coarse_scores, NEGATIVE)
    log_total = normalize(coarse_scores)
    coarse_weights = jnp.exp(coarse_scores - log_total)
    coarse_low = coarse_weights.astype(BF16)
    coarse_out = jnp.einsum("hqk,khd->qhd", coarse_low, value_heads, preferred_element_type=F32)
    coarse_dot = jnp.sum(grad_heads.astype(F32) * coarse_out, axis=-1)
    coarse_wgrad = jnp.einsum("qhd,khd->hqk", grad_heads, value_heads, preferred_element_type=F32)
    coarse_sgrad = (coarse_weights * (coarse_wgrad - coarse_dot.T[:, :, None])).astype(BF16)
    coarse_qgrad = (
        jnp.einsum("hqk,khd->qhd", coarse_sgrad, key_heads, preferred_element_type=F32)
        * score_scale
    )
    count = head_tokens * lax.axis_size("rows")
    key_part = (
        jnp.einsum("hqk,qhd->khd", coarse_sgrad, query_heads, preferred_element_type=F32)
        * score_scale
    )
    value_part = jnp.einsum("hqk,qhd->khd", coarse_low, grad_heads, preferred_element_type=F32)
    terms = lax.psum_scatter(
        jnp.concatenate(
            [key_part.reshape(count, head_width), value_part.reshape(count, head_width)], axis=1
        ),
        "rows",
        scatter_dimension=0,
        tiled=True,
    )
    total_keys = terms[:, :head_width]
    total_values = terms[:, head_width:]
    out_dims = (head_tokens // coarse_cols, 1, coarse_cols, head_width)
    return (
        coarse_qgrad.reshape(out_dims).astype(BF16),
        total_keys.reshape(out_dims).astype(BF16),
        total_values.reshape(out_dims).astype(BF16),
    )


def local(fine_q, fine_kv, coarse_q, coarse_kv, cotangent, gain_table, timesteps, valid_cols):
    frames, bands = lax.axis_size("frames"), lax.axis_size("rows")
    head_width = coarse_q.shape[-1] // frames
    tokens = coarse_q.shape[-2]
    direct = (
        head_width == cotangent.shape[-1]
        and 4 * tokens * head_width // LANES == 16
        and frames * bands * tokens <= 128
    )
    coarse = coarse_direct if direct else coarse_gathered
    coarse_grads = coarse(coarse_q, coarse_kv, cotangent, gain_table, timesteps, valid_cols)
    fine_grads = fine_level(fine_q, fine_kv, cotangent, gain_table, timesteps, valid_cols)
    return fine_grads + coarse_grads


def solution(mesh):
    placed = (
        P("frames", "rows", None, None),
        P("frames", "rows", None, None),
        P("frames", "rows", None, None),
        P("frames", "rows", None, None),
        P("frames", "rows", None, None),
        P(),
        P("frames"),
        P(),
    )
    return jax.shard_map(
        local,
        mesh=mesh,
        in_specs=placed,
        out_specs=(
            P("frames", "rows", None, None),
            P("frames", "rows", None, None),
            P(None, "rows", None, "frames"),
            P(None, "rows", None, "frames"),
            P(None, "rows", None, "frames"),
        ),
        check_vma=False,
    )
```

time: 178 us -> 28.6 us (0.16)
  blocking collectives: 63.2 us -> 0 us
  waiting for transfers between devices: 53.2 us -> 6.64 us
  between operations: 15.2 us -> 1.3 us
  starting transfers between devices: 23 us -> 9.72 us
  local copies, waits for them, and re-layouts: 13 us -> 1.35 us
  Pallas kernels: 0 us -> 9.34 us
  other arithmetic: 5.97 us -> 0 us
  matrix products: 3.41 us -> 0 us
    all_gather x2 -> x0, blocking collectives: 63.2 us -> none  [the longest x1 32.8 us: local(): lax.all_gather(head_keys, 'rows', axis=0, tiled=True)]
    reduce_scatter x1 -> x0, waiting for transfers between devices: 42.9 us -> none  [local(): lax.psum_scatter(jnp.concatenate([key_part.reshape(count, head_width), va...]
    pallas_call x0 -> x4, Pallas kernels: none -> 9.34 us  [the longest x1 3.68 us: fine_level(): pl.pallas_call(functools.partial(fine_kernel, cols), in_specs=[smem()] +...]
    all_to_all x4 -> x1, starting transfers between devices: 14 us -> 7.3 us  [coarse_direct(): lax.all_to_all(sent.reshape(frames * bands, tile, LANES), ('frames', 'row...]
    ppermute x4 -> x2, starting transfers between devices: 8.92 us -> 2.42 us  [the longest x1 1.77 us: fine_level(): near = lax.ppermute(near, 'rows', pairs)]
    all_to_all x4 -> x1, waiting for transfers between devices: 5.28 us -> 0.01 us  [coarse_direct(): lax.all_to_all(sent.reshape(frames * bands, tile, LANES), ('frames', 'row...]
    convert_element_type x9 -> x0, local copies, waits for them, and re-layouts: 3.67 us -> none  [the longest x2 0.91 us: local(): grad_fine_q = query_grad.reshape(frames_here, tile_count, rows_here, tile...]
    dot_general x13 -> x0, matrix products: 3.41 us -> none  [the longest x1 0.45 us: local(): frame_gain = jnp.dot(select, gain_table, precision=lax.Precision.HIGHEST)]
  transfers between devices with their start and end apart: 9 -> 3, of which waited for: 4 -> 1; matrix products, arithmetic and copies ran while one was open for 10% -> 0% of each run, Pallas kernels for 0% -> 19%
where the time goes in v1:
time: 28.6 us; the launch traced here: 28.3 us
  starting transfers between devices  9.72 us (34%)
  Pallas kernels  9.34 us (33%)
  waiting for transfers between devices  6.64 us (23%)
  local copies, waits for them, and re-layouts  1.35 us (5%)
  between operations  1.3 us (5%)
    all_to_all x1, starting transfers between devices, coarse_direct(): lax.all_to_all(sent.reshape(frames * bands, tile, LANES), ('frames', 'row...  7.3 us
    ppermute x1, waiting for transfers between devices, fine_level(): near = lax.ppermute(near, 'rows', pairs)  6.63 us
    pallas_call x1, Pallas kernels, fine_level(): pl.pallas_call(functools.partial(fine_kernel, cols), in_specs=[smem()] +...  3.68 us
    pallas_call x2, Pallas kernels, call(): pl.pallas_call(kernel, grid_spec=pltpu.PrefetchScalarGridSpec(num_scalar_...  3.37 us
    pallas_call x1, Pallas kernels, coarse_direct(): pl.pallas_call(functools.partial(coarse_kernel, frames, tokens), in_specs...  2.29 us
    ppermute x1, starting transfers between devices, fine_level(): near = lax.ppermute(near, 'rows', pairs)  1.77 us
    unnamed x6, local copies, waits for them, and re-layouts  1.35 us
    ppermute x1, starting transfers between devices, fine_level(): far = lax.ppermute(far, 'rows', others)  0.66 us
  transfers between devices with their start and end apart: 3, of which 1 were waited for; matrix products, arithmetic and copies ran while one was open for 0% of the time, Pallas kernels for 19%

profile of v1, /device:TPU:0, one launch (start us, length us, event | category | flops | bytes accessed | tf_op | source)
XLA Modules:
  0.0 28.3 jit_solution(11465836379966580618)
XLA Ops:
  1.3 1.7 %shard_map.121 = bf16[512,128]{1,0:T(8,128)(2,1)} custom-call(s32[1]{0:T(128)S(6)} %copy.16.step_ref, bf16[128,256]{1,0:T(8,128)(2,1)} %bitcast.20, f32[1000,256]{1,0:T(8,128)} %gain_ref.3, bf16[2,1024]{1,0:T(2,128)(2,1)} %bitcast.27, bf16[2,2048]{1,0:T(2,128)(2,1)} %bitcast.26), custom_call_target="tpu_custom_call" | custom-call | tf_op jit(solution)/shard_map/pallas_call | solution.py:290
  2.9 7.3 %all-to-all-start = ((bf16[32,16,128]{2,1,0:T(8,128)(2,1)}), bf16[32,16,128]{2,1,0:T(8,128)(2,1)S(1)}, u32[]{:S(2)}, u32[]{:S(2)}) async-start(bf16[32,16,128]{2,1,0:T(8,128)(2,1)} %bitcast.18), calls=%async_computation | async-start | bytes 262144 | tf_op jit(solution)/shard_map/all_to_all | solution.py:349
  10.2 1.7 %shard_map.119 = (bf16[144,512]{1,0:T(8,128)(2,1)}, bf16[144,512]{1,0:T(8,128)(2,1)}, bf16[128,256]{1,0:T(8,128)(2,1)}) custom-call(s32[1]{0:T(128)S(6)} %copy.16.step_ref, bf16[128,256]{1,0:T(8,128)(2,1)} %bitcast.24, bf16[128,512]{1,0:T(8,128)(2,1)} %bitcast.22, bf16[128,256]{1,0:T(8,128)(2,1)} %bitcast.21, f32[1000,256]{1,0:T(8,128)} %gain_ref.3), custom_call_target="tpu_custom_call" | custom-call | tf_op jit(solution)/shard_map/pallas_call | solution.py:290
  12.0 1.8 %collective-permute-start = (bf16[144,512]{1,0:T(8,128)(2,1)}, bf16[144,512]{1,0:T(8,128)(2,1)S(1)}, u32[]{:S(2)}, u32[]{:S(2)}) collective-permute-start(bf16[144,512]{1,0:T(8,128)(2,1)} %get-tuple-element.14), channel_id=1, source_target_pairs={{0,1},{1,0},{2,3},{3,2},{4,5},{5,4},{6,7},{7,6},{8,9},{9,8},{10,11... | collective-permute-start | bytes 442376 | tf_op jit(solution)/shard_map/ppermute | solution.py:319
  13.7 0.7 %collective-permute-start.1 = (bf16[144,512]{1,0:T(8,128)(2,1)}, bf16[144,512]{1,0:T(8,128)(2,1)S(1)}, u32[]{:S(2)}, u32[]{:S(2)}) collective-permute-start(bf16[144,512]{1,0:T(8,128)(2,1)} %get-tuple-element.15), channel_id=1, source_target_pairs={{1,2},{2,1},{3,4},{4,3},{5,6},{6,5},{9,10},{10,9},{11,12},{12,11},... | collective-permute-start | bytes 442376 | tf_op jit(solution)/shard_map/ppermute | solution.py:320
  14.4 6.6 %collective-permute-done.near_ref = bf16[144,512]{1,0:T(8,128)(2,1)S(1)} collective-permute-done((bf16[144,512]{1,0:T(8,128)(2,1)}, bf16[144,512]{1,0:T(8,128)(2,1)S(1)}, u32[]{:S(2)}, u32[]{:S(2)}) %collective-permute-start) | collective-permute-done | bytes 147488 | tf_op jit(solution)/shard_map/ppermute | solution.py:319
  21.0 0.0 copy-start.1
  21.0 0.0 collective-permute-done.1.far_ref
  21.0 0.0 copy-start.2
  21.0 0.7 %copy-done.1 = bf16[144,512]{1,0:T(8,128)(2,1)} copy-done((bf16[144,512]{1,0:T(8,128)(2,1)}, bf16[144,512]{1,0:T(8,128)(2,1)S(1)}, u32[]{:S(2)}) %copy-start.1) | copy-done | bytes 147480
  21.7 0.0 copy-done.2
  21.7 3.7 %shard_map.120 = (bf16[128,256]{1,0:T(8,128)(2,1)}, bf16[128,512]{1,0:T(8,128)(2,1)}) custom-call(s32[4]{0:T(128)} %valid_ref.3, bf16[128,256]{1,0:T(8,128)(2,1)} %bitcast.25, bf16[128,512]{1,0:T(8,128)(2,1)} %bitcast.23, bf16[128,256]{1,0:T(8,128)(2,1)} %get-tuple-element.13.grad_ref, bf16[144,512]{1,0:T(8,128)(2,1)} %copy-done.1, bf16[144,512]{1,0:T(8,128)(2,1)} %copy-done.2), custom_call_target="tpu_custom_call" | custom-call | flops 400000000 | bytes 1000000 | tf_op jit(solution)/shard_map/pallas_call | solution.py:321
  25.4 0.0 all-to-all-done
  25.4 0.0 copy-start
  25.4 0.6 %copy-done = bf16[32,16,128]{2,1,0:T(8,128)(2,1)} copy-done((bf16[32,16,128]{2,1,0:T(8,128)(2,1)}, bf16[32,16,128]{2,1,0:T(8,128)(2,1)S(1)}, u32[]{:S(2)}) %copy-start) | copy-done | bytes 131096
  26.1 2.3 %shard_map.122 = (bf16[4,2,256]{2,1,0:T(2,128)(2,1)}, bf16[4,2,256]{2,1,0:T(2,128)(2,1)}, bf16[4,2,256]{2,1,0:T(2,128)(2,1)}) custom-call(s32[4]{0:T(128)} %valid_ref.3, bf16[512,128]{1,0:T(8,128)(2,1)} %bitcast.19), custom_call_target="tpu_custom_call" | custom-call | tf_op jit(solution)/shard_map/pallas_call | solution.py:358
Async XLA Ops:
  2.9 22.5 %all-to-all-start = ((bf16[32,16,128]{2,1,0:T(8,128)(2,1)}), bf16[32,16,128]{2,1,0:T(8,128)(2,1)S(1)}, u32[]{:S(2)}, u32[]{:S(2)}) async-start(bf16[32,16,128]{2,1,0:T(8,128)(2,1)} %bitcast.18), calls=%async_computation | async-start | bytes 262144 | tf_op jit(solution)/shard_map/all_to_all | solution.py:349
  12.0 9.1 %collective-permute-start = (bf16[144,512]{1,0:T(8,128)(2,1)}, bf16[144,512]{1,0:T(8,128)(2,1)S(1)}, u32[]{:S(2)}, u32[]{:S(2)}) collective-permute-start(bf16[144,512]{1,0:T(8,128)(2,1)} %get-tuple-element.14), channel_id=1, source_target_pairs={{0,1},{1,0},{2,3},{3,2},{4,5},{5,4},{6,7},{7,6},{8,9},{9,8},{10,11... | collective-permute-start | bytes 442376 | tf_op jit(solution)/shard_map/ppermute | solution.py:319
  13.7 7.3 %collective-permute-start.1 = (bf16[144,512]{1,0:T(8,128)(2,1)}, bf16[144,512]{1,0:T(8,128)(2,1)S(1)}, u32[]{:S(2)}, u32[]{:S(2)}) collective-permute-start(bf16[144,512]{1,0:T(8,128)(2,1)} %get-tuple-element.15), channel_id=1, source_target_pairs={{1,2},{2,1},{3,4},{4,3},{5,6},{6,5},{9,10},{10,9},{11,12},{12,11},... | collective-permute-start | bytes 442376 | tf_op jit(solution)/shard_map/ppermute | solution.py:320
  21.0 0.7 %copy-start.1 = (bf16[144,512]{1,0:T(8,128)(2,1)}, bf16[144,512]{1,0:T(8,128)(2,1)S(1)}, u32[]{:S(2)}) copy-start(bf16[144,512]{1,0:T(8,128)(2,1)S(1)} %collective-permute-done.near_ref) | copy-start | bytes 442372
  21.0 0.7 %copy-start.2 = (bf16[144,512]{1,0:T(8,128)(2,1)}, bf16[144,512]{1,0:T(8,128)(2,1)S(1)}, u32[]{:S(2)}) copy-start(bf16[144,512]{1,0:T(8,128)(2,1)S(1)} %collective-permute-done.1.far_ref) | copy-start | bytes 442372
  25.4 0.6 %copy-start = (bf16[32,16,128]{2,1,0:T(8,128)(2,1)}, bf16[32,16,128]{2,1,0:T(8,128)(2,1)S(1)}, u32[]{:S(2)}) copy-start(bf16[32,16,128]{2,1,0:T(8,128)(2,1)S(1)} %all-to-all-done) | copy-start | bytes 393220

commit v2 on v1

v2 whole, which is shorter than its diff:
```python
import functools
import math

import jax
import jax.numpy as jnp
from jax import lax
from jax.experimental import pallas as pl
from jax.experimental.pallas import tpu as pltpu
from jax.sharding import PartitionSpec as P

HD = 64
KERNEL = 7
POOL = 8
LANES = 128

NEGATIVE = -1e30

F32 = jnp.float32
BF16 = jnp.bfloat16


def dot_nt(left, right):
    return lax.dot_general(left, right, (((1,), (1,)), ((), ())), preferred_element_type=F32)


def dot_nn(left, right):
    return jnp.dot(left, right, preferred_element_type=F32)


def iota(shape, dim):
    return lax.broadcasted_iota(jnp.int32, shape, dim)


def pairs_of(table):
    blocks = []
    for lo in range(0, table.shape[1], LANES):
        part = table[:, lo : lo + LANES]
        first = iota(part.shape, 1) < HD
        zero = jnp.zeros_like(part)
        blocks.append(
            jnp.concatenate([jnp.where(first, part, zero), jnp.where(first, zero, part)], axis=0)
        )
    return blocks


def softmax_grads(scores, weight_grad, axis):
    top = jnp.max(scores, axis=axis, keepdims=True)
    raised = jnp.exp(scores - top)
    weights = raised * (1.0 / jnp.sum(raised, axis=axis, keepdims=True))
    low = weights.astype(BF16)
    row_dot = jnp.sum(low.astype(F32) * weight_grad, axis=axis, keepdims=True)
    return low, (weights * (weight_grad - row_dot)).astype(BF16)


def send_kernel(
    cols, bands, step_ref, cot_hbm, gain_hbm, cq_hbm, ckv_hbm,
    send_ref, gain_ref, cot_ref, eight_ref, cq_ref, ckv_ref, sems,
):
    step = step_ref[0]
    eight = eight_ref.shape[0]
    first = pl.multiple_of(step // eight * eight, eight)
    gain_copy = pltpu.make_async_copy(gain_hbm.at[pl.ds(first, eight)], eight_ref, sems.at[0])
    gain_copy.start()
    copies = [
        pltpu.make_async_copy(source, target, sems.at[1 + at])
        for at, (source, target) in enumerate(
            ((cot_hbm, cot_ref), (cq_hbm, cq_ref), (ckv_hbm, ckv_ref))
        )
    ]
    for copy in copies:
        copy.start()
    pixels, width = cot_ref.shape
    tokens, cwidth = cq_ref.shape
    half = POOL // 2
    groups = cwidth // width
    part = iota((groups * tokens, pixels), 0)
    group, token = part // tokens, part % tokens
    pixel = iota((groups * tokens, pixels), 1)
    row, col = pixel // cols, pixel % cols
    inside = (row // half == group // 2) & (col // half == token * 2 + group % 2)
    for copy in copies:
        copy.wait()
    summed = dot_nn(inside.astype(BF16), cot_ref[...])
    query = cq_ref[...].astype(F32)
    both = ckv_ref[...].astype(F32)
    gain_copy.wait()
    gain = eight_ref[pl.ds(step - first, 1), :]
    gain_ref[...] = gain
    pooled = summed * gain
    for g in range(groups):
        lo = g * width
        arrays = (
            query[:, lo : lo + width],
            both[:, lo : lo + width],
            both[:, cwidth + lo : cwidth + lo + width],
            pooled[g * tokens : (g + 1) * tokens, :],
        )
        tile = jnp.concatenate(
            [a[:, b : b + LANES] for a in arrays for b in range(0, width, LANES)], axis=0
        ).astype(BF16)
        height = tile.shape[0]
        for r in range(bands):
            start = (g * bands + r) * height
            send_ref[start : start + height, :] = tile


def prep_kernel(cols, gain_ref, q_ref, kv_ref, cot_ref, near_ref, far_ref, grad_ref):
    radius = KERNEL // 2
    pixels, width = q_ref.shape
    one, two = radius * cols, 2 * radius * cols
    even = lax.axis_index("rows") % 2 == 0
    grad_ref[...] = (gain_ref[...] * cot_ref[...].astype(F32)).astype(BF16)

    def pack(target, top):
        lo_one, lo_two = (0, 0) if top else (pixels - one, pixels - two)
        target[:two, :] = kv_ref[lo_two : lo_two + two, :]
        target[two:, :width] = q_ref[lo_one : lo_one + one, :]
        target[two:, width:] = grad_ref[lo_one : lo_one + one, :]

    @pl.when(even)
    def _():
        pack(near_ref, False)
        pack(far_ref, True)

    @pl.when(jnp.logical_not(even))
    def _():
        pack(near_ref, True)
        pack(far_ref, False)


def fine_kernel(cols, valid_ref, after_ref, q_ref, kv_ref, grad_ref, near_ref, far_ref, dq_ref, dkv_ref):
    radius = KERNEL // 2
    pixels, width = q_ref.shape
    rows = pixels // cols
    one, two = radius * cols, 2 * radius * cols
    scale = 1.0 / math.sqrt(HD)
    band = lax.axis_index("rows")
    valid = valid_ref[lax.axis_index("frames")]
    first, last = band == 0, band == lax.axis_size("rows") - 1
    even = band % 2 == 0

    def received(rows_at, cols_at):
        near, far = near_ref[rows_at, cols_at], far_ref[rows_at, cols_at]
        return jnp.where(even, far, near), jnp.where(even, near, far)

    def extended(cols_at):
        above, below = received(slice(0, two), cols_at)
        return jnp.concatenate([above, kv_ref[:, cols_at], below], axis=0)

    keys, values = extended(slice(0, width)), extended(slice(width, 2 * width))
    q_above, q_below = received(slice(two, two + one), slice(0, width))
    g_above, g_below = received(slice(two, two + one), slice(width, 2 * width))

    def bias(key_count, key_row, lanes, query_count, query_row, ends):
        key, lane = iota((key_count, lanes), 0), iota((key_count, lanes), 1) & (query_count - 1)
        krow, kcol = (key >> 4) + key_row, key & (cols - 1)
        qrow, qcol = (lane >> 4) + query_row, lane & (cols - 1)
        seen = (jnp.abs(krow - qrow) <= radius) & (jnp.abs(kcol - qcol) <= radius) & (kcol < valid)
        if ends:
            seen = seen & ((krow >= 0) | jnp.logical_not(first))
            seen = seen & ((krow < rows) | jnp.logical_not(last))
        seen = seen | ((krow == qrow) & (kcol == qcol))
        return jnp.where(seen, 0.0, NEGATIVE)

    lo, hi = one, one + pixels + two
    own_keys, own_values = keys[lo:hi], values[lo:hi]
    own_bias = bias(hi - lo, -radius, pixels, pixels, 0, True)
    own_bias = jnp.concatenate([own_bias, own_bias], axis=1)
    keys_t = own_keys.T
    dq, dk, dv = [], [], []
    for p, (query, grad) in enumerate(zip(pairs_of(q_ref[...] * scale), pairs_of(grad_ref[...]))):
        at = slice(p * LANES, (p + 1) * LANES)
        low, sgrad = softmax_grads(
            dot_nt(own_keys[:, at], query) + own_bias, dot_nt(own_values[:, at], grad), 0
        )
        dq_t = dot_nn(keys_t[at], sgrad)
        dq_t = jnp.concatenate([dq_t[:HD, :pixels], dq_t[HD:, pixels:]], axis=0)
        dq.append((dq_t * scale).T)
        dk.append(dot_nn(sgrad[one : one + pixels], query))
        dv.append(dot_nn(low[one : one + pixels], grad))
    dq_ref[...] = jnp.concatenate(dq, axis=1).astype(BF16)

    pad = jnp.zeros((cols, width), BF16)

    def outside(query, grad, key_lo, key_row, query_row, keep):
        count, lanes = one + two, 2 * (one + cols)
        outside_bias = bias(count, key_row, lanes, one + cols, query_row, False)
        query, grad = (
            pairs_of(jnp.concatenate([t, pad], axis=0)) for t in (query * scale, grad)
        )
        found = []
        for p in range(len(query)):
            at = slice(p * LANES, (p + 1) * LANES)
            low, sgrad = softmax_grads(
                dot_nt(keys[key_lo : key_lo + count, at], query[p]) + outside_bias,
                dot_nt(values[key_lo : key_lo + count, at], grad[p]),
                0,
            )
            found.append(
                (
                    dot_nn(sgrad[keep : keep + one], query[p]),
                    dot_nn(low[keep : keep + one], grad[p]),
                )
            )
        return found

    above = outside(q_above, g_above, 0, -2 * radius, -radius, two)
    below = outside(q_below, g_below, pixels + one, rows - radius, rows, 0)
    for p in range(len(dk)):
        for at, inner in enumerate((dk[p], dv[p])):
            lo = at * width + p * LANES
            dkv_ref[:, lo : lo + LANES] = jnp.concatenate(
                [
                    inner[:one] + above[p][at],
                    inner[one : pixels - one],
                    inner[pixels - one :] + below[p][at],
                ],
                axis=0,
            ).astype(BF16)


def coarse_kernel(frames, tokens, valid_ref, x_ref, dq_ref, dk_ref, dv_ref, after_ref, wide, low_ref, sg_ref):
    bands = lax.axis_size("rows")
    width = dq_ref.shape[-1]
    parts = width // LANES
    height = x_ref.shape[0] // (frames * bands)
    band = lax.axis_index("rows")
    scale = 1.0 / math.sqrt(HD)
    wide[...] = x_ref[...].astype(F32)
    after_ref[...] = jnp.zeros_like(after_ref)
    devices, own = frames * bands, frames * tokens

    def every(array, b):
        first = (array * parts + b) * tokens
        return jnp.concatenate(
            [wide[pl.ds(first + t, devices, stride=height), :] for t in range(tokens)], axis=0
        ).astype(BF16)

    def mine(array, b):
        first = band * height + (array * parts + b) * tokens
        return jnp.concatenate(
            [wide[pl.ds(first + f * bands * height, tokens), :] for f in range(frames)], axis=0
        ).astype(BF16)

    count = devices * tokens

    def key_bias(shape, dim):
        place = iota(shape, dim)
        token, frame = place // devices, place // bands % frames
        limit = jnp.zeros(shape, jnp.int32)
        for f in range(frames):
            limit = jnp.where(frame == f, valid_ref[f], limit)
        return jnp.where(token * POOL < limit, 0.0, NEGATIVE)

    bias, own_bias = key_bias((count, 2 * count), 0), key_bias((2 * own, count), 1)
    for b in range(parts):
        at = slice(b * LANES, (b + 1) * LANES)
        key, value = every(1, b), every(2, b)
        (query,), (grad,) = pairs_of(every(0, b) * scale), pairs_of(every(3, b))
        low, sgrad = softmax_grads(dot_nt(key, query) + bias, dot_nt(value, grad), 0)
        low_ref[b] = low.astype(F32)
        sg_ref[b] = sgrad.astype(F32)

        def mine_rows(ref):
            pieces = [
                ref[b, pl.ds(t * devices + f * bands + band, 1), :]
                for f in range(frames)
                for t in range(tokens)
            ]
            return jnp.concatenate(pieces, axis=0).astype(BF16)

        (own_query,), (own_grad,) = pairs_of(mine(0, b) * scale), pairs_of(mine(3, b))
        _, own_sgrad = softmax_grads(
            dot_nt(own_query, key) + own_bias, dot_nt(own_grad, value), 1
        )
        full = dot_nn(own_sgrad, key)
        dq = jnp.where(iota((own, LANES), 1) < HD, full[:own], full[own:]) * scale
        dk = dot_nn(mine_rows(sg_ref), query)
        dv = dot_nn(mine_rows(low_ref), grad)
        for ref, table in ((dq_ref, dq), (dk_ref, dk), (dv_ref, dv)):
            rounded = table.astype(BF16)
            for f in range(frames):
                ref[f, :, at] = rounded[f * tokens : (f + 1) * tokens]


def vmem():
    return pl.BlockSpec(memory_space=pltpu.VMEM)


def smem():
    return pl.BlockSpec(memory_space=pltpu.SMEM)


def hbm():
    return pl.BlockSpec(memory_space=pltpu.HBM)


def in_hbm(array):
    return pltpu.with_memory_space_constraint(array, pltpu.HBM)


def params():
    return pltpu.CompilerParams(vmem_limit_bytes=16 * 2**20)


def out(shape, dtype=BF16):
    return jax.ShapeDtypeStruct(shape, dtype)


def fine_level(after, gain, fine_q, fine_kv, cotangent, valid_cols):
    bands = lax.axis_size("rows")
    _, rows, cols, width = fine_q.shape
    pixels = rows * cols
    radius = KERNEL // 2
    query = fine_q.reshape(pixels, width)
    key_value = fine_kv.reshape(pixels, 2 * width)
    cot = cotangent.reshape(pixels, width)
    packed = (3 * radius * cols, 2 * width)
    near, far, grad = pl.pallas_call(
        functools.partial(prep_kernel, cols),
        in_specs=[vmem()] * 4,
        out_specs=[vmem()] * 3,
        out_shape=[out(packed), out(packed), out((pixels, width))],
        compiler_params=params(),
    )(gain, query, key_value, cot)
    pairs = [(i, i ^ 1) for i in range(bands) if i ^ 1 < bands]
    others = [(i, ((i + 1) ^ 1) - 1) for i in range(1, bands) if ((i + 1) ^ 1) - 1 < bands]
    near = lax.ppermute(near, "rows", pairs)
    far = lax.ppermute(far, "rows", others)
    grad_q, grad_kv = pl.pallas_call(
        functools.partial(fine_kernel, cols),
        in_specs=[smem()] + [vmem()] * 6,
        out_specs=[vmem()] * 2,
        out_shape=[out((pixels, width)), out((pixels, 2 * width))],
        compiler_params=params(),
        cost_estimate=pl.CostEstimate(flops=400_000_000, bytes_accessed=1_000_000, transcendentals=300_000),
    )(valid_cols, after, query, key_value, grad, near, far)
    return grad_q.reshape(fine_q.shape), grad_kv.reshape(fine_kv.shape)


def coarse_direct(coarse_q, coarse_kv, cotangent, gain_table, timesteps, valid_cols):
    frames, bands = lax.axis_size("frames"), lax.axis_size("rows")
    _, rows, cols, width = cotangent.shape
    tokens, cwidth = coarse_q.shape[-2:]
    head_width = cwidth // frames
    tile = 4 * tokens * head_width // LANES
    sent, gain = pl.pallas_call(
        functools.partial(send_kernel, cols, bands),
        in_specs=[smem()] + [hbm()] * 4,
        out_specs=[vmem()] * 2,
        out_shape=[out((frames * bands * tile, LANES)), out((1, width), F32)],
        scratch_shapes=[
            pltpu.VMEM((rows * cols, width), BF16),
            pltpu.VMEM((8, width), F32),
            pltpu.VMEM((tokens, cwidth), BF16),
            pltpu.VMEM((tokens, 2 * cwidth), BF16),
            pltpu.SemaphoreType.DMA((4,)),
        ],
        compiler_params=params(),
    )(
        timesteps,
        in_hbm(cotangent.reshape(rows * cols, width)),
        in_hbm(gain_table),
        in_hbm(coarse_q.reshape(tokens, cwidth)),
        in_hbm(coarse_kv.reshape(tokens, 2 * cwidth)),
    )
    held = lax.all_to_all(
        sent.reshape(frames * bands, tile, LANES),
        ("frames", "rows"),
        split_axis=0,
        concat_axis=0,
        tiled=True,
    ).reshape(frames * bands * tile, LANES)
    count = frames * bands * tokens
    *outs, after = pl.pallas_call(
        functools.partial(coarse_kernel, frames, tokens),
        in_specs=[smem(), vmem()],
        out_specs=[vmem()] * 4,
        out_shape=[out((frames, tokens, head_width))] * 3 + [out((8, LANES), F32)],
        scratch_shapes=[
            pltpu.VMEM(held.shape, F32),
            pltpu.VMEM((head_width // LANES, count, 2 * count), F32),
            pltpu.VMEM((head_width // LANES, count, 2 * count), F32),
        ],
        compiler_params=params(),
        cost_estimate=pl.CostEstimate(flops=100_000_000_000, bytes_accessed=100_000_000, transcendentals=0),
    )(valid_cols, held)
    return tuple(x.reshape(frames, 1, tokens, head_width) for x in outs), gain, after


def normalize(scores):
    row_max = jnp.max(scores, axis=-1, keepdims=True)
    return row_max + jnp.log(jnp.sum(jnp.exp(scores - row_max), axis=-1, keepdims=True))


def coarse_gathered(coarse_q, coarse_kv, cotangent, gain_table, timesteps, valid_cols):
    score_scale = 1.0 / math.sqrt(HD)
    frames_here, _, cols_here, fine_width = cotangent.shape
    total_frames = valid_cols.shape[0]
    steps_all = gain_table.shape[0]
    select = (timesteps[:, None] == jnp.arange(steps_all)[None, :]).astype(F32)
    frame_gain = jnp.dot(select, gain_table, precision=lax.Precision.HIGHEST)
    scaled_grad = frame_gain[:, None, None, :] * cotangent.astype(F32)
    half_pool = POOL // 2
    coarse_cols = cols_here // POOL
    coarse_width = coarse_q.shape[-1]
    coarse_count = frames_here * coarse_cols
    blocks = scaled_grad.reshape(frames_here, 2, half_pool, coarse_cols, 2, half_pool, fine_width)
    pooled = (
        jnp.sum(blocks, axis=(2, 5))
        .transpose(0, 2, 1, 3, 4)
        .reshape(coarse_count, coarse_width)
        .astype(BF16)
    )
    mine_query = coarse_q.reshape(coarse_count, coarse_width)
    mine_keys = coarse_kv[..., :coarse_width].reshape(coarse_count, coarse_width)
    mine_values = coarse_kv[..., coarse_width:].reshape(coarse_count, coarse_width)
    head_query, head_keys, head_values, head_grad = (
        lax.all_to_all(mine_query, "frames", split_axis=1, concat_axis=0, tiled=True),
        lax.all_to_all(mine_keys, "frames", split_axis=1, concat_axis=0, tiled=True),
        lax.all_to_all(mine_values, "frames", split_axis=1, concat_axis=0, tiled=True),
        lax.all_to_all(pooled, "frames", split_axis=1, concat_axis=0, tiled=True),
    )
    head_tokens, head_width = head_query.shape
    head_groups = head_width // HD
    query_heads = head_query.reshape(head_tokens, head_groups, HD)
    grad_heads = head_grad.reshape(head_tokens, head_groups, HD)
    every_keys, every_values = (
        lax.all_gather(head_keys, "rows", axis=0, tiled=True),
        lax.all_gather(head_values, "rows", axis=0, tiled=True),
    )
    every_count = every_keys.shape[0]
    key_heads = every_keys.reshape(every_count, head_groups, HD)
    value_heads = every_values.reshape(every_count, head_groups, HD)
    position = jnp.arange(every_count) % head_tokens
    key_frame = position // coarse_cols
    key_column = position % coarse_cols
    col_limit = jnp.sum(
        jnp.where(key_frame[:, None] == jnp.arange(total_frames)[None, :], valid_cols[None, :], 0),
        axis=1,
    )
    key_ok = key_column * POOL < col_limit
    coarse_scores = (
        jnp.einsum("qhd,khd->hqk", query_heads, key_heads, preferred_element_type=F32)
        * score_scale
    )
    coarse_scores = jnp.where(key_ok[None, None, :], coarse_scores, NEGATIVE)
    log_total = normalize(coarse_scores)
    coarse_weights = jnp.exp(coarse_scores - log_total)
    coarse_low = coarse_weights.astype(BF16)
    coarse_out = jnp.einsum("hqk,khd->qhd", coarse_low, value_heads, preferred_element_type=F32)
    coarse_dot = jnp.sum(grad_heads.astype(F32) * coarse_out, axis=-1)
    coarse_wgrad = jnp.einsum("qhd,khd->hqk", grad_heads, value_heads, preferred_element_type=F32)
    coarse_sgrad = (coarse_weights * (coarse_wgrad - coarse_dot.T[:, :, None])).astype(BF16)
    coarse_qgrad = (
        jnp.einsum("hqk,khd->qhd", coarse_sgrad, key_heads, preferred_element_type=F32)
        * score_scale
    )
    count = head_tokens * lax.axis_size("rows")
    key_part = (
        jnp.einsum("hqk,qhd->khd", coarse_sgrad, query_heads, preferred_element_type=F32)
        * score_scale
    )
    value_part = jnp.einsum("hqk,qhd->khd", coarse_low, grad_heads, preferred_element_type=F32)
    terms = lax.psum_scatter(
        jnp.concatenate(
            [key_part.reshape(count, head_width), value_part.reshape(count, head_width)], axis=1
        ),
        "rows",
        scatter_dimension=0,
        tiled=True,
    )
    total_keys = terms[:, :head_width]
    total_values = terms[:, head_width:]
    out_dims = (head_tokens // coarse_cols, 1, coarse_cols, head_width)
    return (
        coarse_qgrad.reshape(out_dims).astype(BF16),
        total_keys.reshape(out_dims).astype(BF16),
        total_values.reshape(out_dims).astype(BF16),
    ), frame_gain, jnp.zeros((8, LANES), F32)


def local(fine_q, fine_kv, coarse_q, coarse_kv, cotangent, gain_table, timesteps, valid_cols):
    frames, bands = lax.axis_size("frames"), lax.axis_size("rows")
    head_width = coarse_q.shape[-1] // frames
    tokens = coarse_q.shape[-2]
    direct = (
        head_width == cotangent.shape[-1]
        and 4 * tokens * head_width // LANES == 16
        and frames * bands * tokens <= 128
    )
    coarse = coarse_direct if direct else coarse_gathered
    coarse_grads, gain, after = coarse(
        coarse_q, coarse_kv, cotangent, gain_table, timesteps, valid_cols
    )
    fine_grads = fine_level(after, gain, fine_q, fine_kv, cotangent, valid_cols)
    return fine_grads + coarse_grads


def solution(mesh):
    placed = (
        P("frames", "rows", None, None),
        P("frames", "rows", None, None),
        P("frames", "rows", None, None),
        P("frames", "rows", None, None),
        P("frames", "rows", None, None),
        P(),
        P("frames"),
        P(),
    )
    return jax.shard_map(
        local,
        mesh=mesh,
        in_specs=placed,
        out_specs=(
            P("frames", "rows", None, None),
            P("frames", "rows", None, None),
            P(None, "rows", None, "frames"),
            P(None, "rows", None, "frames"),
            P(None, "rows", None, "frames"),
        ),
        check_vma=False,
    )
```

time: 28.6 us -> 23.4 us (0.82)
  Pallas kernels: 9.34 us -> 6.84 us
  waiting for transfers between devices: 6.64 us -> 5.04 us
  local copies, waits for them, and re-layouts: 1.35 us -> 0.02 us
    ppermute x1, waiting for transfers between devices: 6.63 us -> 0.01 us  [fine_level(): near = lax.ppermute(near, 'rows', pairs)]
    all_to_all x1, waiting for transfers between devices: 0.01 us -> 5.03 us  [coarse_direct(): lax.all_to_all(sent.reshape(frames * bands, tile, LANES), ('frames', 'row...]
    pallas_call x2, Pallas kernels: 3.37 us -> 1.75 us  [the longest x1 1.71 us: coarse_direct(): pl.pallas_call(functools.partial(send_kernel, cols, bands), in_specs=[sme...]
    unnamed x6 -> x8, local copies, waits for them, and re-layouts: 1.35 us -> 0.02 us
    pallas_call x1, Pallas kernels: 3.68 us -> 3.12 us  [fine_level(): pl.pallas_call(functools.partial(fine_kernel, cols), in_specs=[smem()] +...]
    pallas_call x1, Pallas kernels: 2.29 us -> 1.97 us  [coarse_direct(): pl.pallas_call(functools.partial(coarse_kernel, frames, tokens), in_specs...]
  transfers between devices with their start and end apart: 3 -> 3, of which waited for: 1 -> 1; matrix products, arithmetic and copies ran while one was open for 0% -> 0% of each run, Pallas kernels for 19% -> 9%
where the time goes in v2:
time: 23.4 us; the launch traced here: 23.2 us
  starting transfers between devices  9.92 us (42%)
  Pallas kernels  6.84 us (29%)
  waiting for transfers between devices  5.04 us (22%)
  between operations  1.36 us (6%)
    all_to_all x1, starting transfers between devices, coarse_direct(): lax.all_to_all(sent.reshape(frames * bands, tile, LANES), ('frames', 'row...  7.3 us
    all_to_all x1, waiting for transfers between devices, coarse_direct(): lax.all_to_all(sent.reshape(frames * bands, tile, LANES), ('frames', 'row...  5.03 us
    pallas_call x1, Pallas kernels, fine_level(): pl.pallas_call(functools.partial(fine_kernel, cols), in_specs=[smem()] +...  3.12 us
    pallas_call x1, Pallas kernels, coarse_direct(): pl.pallas_call(functools.partial(coarse_kernel, frames, tokens), in_specs...  1.97 us
    ppermute x1, starting transfers between devices, fine_level(): near = lax.ppermute(near, 'rows', pairs)  1.83 us
    pallas_call x1, Pallas kernels, coarse_direct(): pl.pallas_call(functools.partial(send_kernel, cols, bands), in_specs=[sme...  1.71 us
    ppermute x1, starting transfers between devices, fine_level(): far = lax.ppermute(far, 'rows', others)  0.79 us
  transfers between devices with their start and end apart: 3, of which 1 were waited for; matrix products, arithmetic and copies ran while one was open for 0% of the time, Pallas kernels for 9%

profile of v2, /device:TPU:0, one launch (start us, length us, event | category | flops | bytes accessed | tf_op | source)
XLA Modules:
  0.0 23.2 jit_solution(4832035153004852679)
XLA Ops:
  1.3 1.7 %shard_map.119 = (bf16[512,128]{1,0:T(8,128)(2,1)}, f32[1,256]{1,0:T(1,128)S(1)}) custom-call(s32[1]{0:T(128)S(6)} %copy.16.step_ref, bf16[128,256]{1,0:T(8,128)(2,1)} %bitcast.18, f32[1000,256]{1,0:T(8,128)} %gain_hbm.1, bf16[2,1024]{1,0:T(2,128)(2,1)} %bitcast.26, bf16[2,2048]{1,0:T(2,128)(2,1)} %bitcast.25), custom_call_target="tpu_custom_call" | custom-call | tf_op jit(solution)/shard_map/pallas_call | solution.py:347
  3.0 0.0 copy-start
  3.0 0.0 copy-start.1
  3.0 0.0 copy-start.2
  3.0 7.3 %all-to-all-start = ((bf16[32,16,128]{2,1,0:T(8,128)(2,1)}), bf16[32,16,128]{2,1,0:T(8,128)(2,1)S(1)}, u32[]{:S(2)}, u32[]{:S(2)}) async-start(bf16[32,16,128]{2,1,0:T(8,128)(2,1)} %bitcast.3), calls=%async_computation | async-start | bytes 262144 | tf_op jit(solution)/shard_map/all_to_all | solution.py:367
  10.3 0.0 copy-done
  10.4 0.0 copy-done.1
  10.4 0.0 copy-done.2
  10.4 1.8 %collective-permute-start = (bf16[144,512]{1,0:T(8,128)(2,1)S(1)}, bf16[144,512]{1,0:T(8,128)(2,1)S(1)}, u32[]{:S(2)}, u32[]{:S(2)}) collective-permute-start(bf16[144,512]{1,0:T(8,128)(2,1)S(1)} %get-tuple-element.20), channel_id=1, source_target_pairs={{0,1},{1,0},{2,3},{3,2},{4,5},{5,4},{6,7},{7,6},{8,9},{9,8},{10,11... | collective-permute-start | bytes 442376 | tf_op jit(solution)/shard_map/ppermute | solution.py:328
  12.3 0.0 copy-start.3
  12.3 0.8 %collective-permute-start.1 = (bf16[144,512]{1,0:T(8,128)(2,1)S(1)}, bf16[144,512]{1,0:T(8,128)(2,1)S(1)}, u32[]{:S(2)}, u32[]{:S(2)}) collective-permute-start(bf16[144,512]{1,0:T(8,128)(2,1)S(1)} %get-tuple-element.21), channel_id=1, source_target_pairs={{1,2},{2,1},{3,4},{4,3},{5,6},{6,5},{9,10},{10,9},{11,12},{12,11},... | collective-permute-start | bytes 442376 | tf_op jit(solution)/shard_map/ppermute | solution.py:329
  13.1 5.0 %all-to-all-done = bf16[32,16,128]{2,1,0:T(8,128)(2,1)S(1)} async-done(((bf16[32,16,128]{2,1,0:T(8,128)(2,1)}), bf16[32,16,128]{2,1,0:T(8,128)(2,1)S(1)}, u32[]{:S(2)}, u32[]{:S(2)}) %all-to-all-start) | async-done | bytes 131104 | tf_op jit(solution)/shard_map/all_to_all | solution.py:367
  18.1 0.0 copy-done.3
  18.1 2.0 %shard_map.120 = (bf16[4,2,256]{2,1,0:T(2,128)(2,1)}, bf16[4,2,256]{2,1,0:T(2,128)(2,1)}, bf16[4,2,256]{2,1,0:T(2,128)(2,1)}, f32[8,128]{1,0:T(8,128)S(1)}) custom-call(s32[4]{0:T(128)S(1)} %copy-done.3, bf16[512,128]{1,0:T(8,128)(2,1)S(1)} %bitcast.22), custom_call_target="tpu_custom_call" | custom-call | flops 99999997952 | bytes 100000000 | tf_op jit(solution)/shard_map/pallas_call | solution.py:375
  20.1 0.0 collective-permute-done.near_ref
  20.1 0.0 collective-permute-done.1.far_ref
  20.1 3.1 %shard_map.122 = (bf16[128,256]{1,0:T(8,128)(2,1)}, bf16[128,512]{1,0:T(8,128)(2,1)}) custom-call(s32[4]{0:T(128)S(1)} %copy-done.3, f32[8,128]{1,0:T(8,128)S(1)} %get-tuple-element.17.after_ref, bf16[128,256]{1,0:T(8,128)(2,1)S(1)} %bitcast.24, bf16[128,512]{1,0:T(8,128)(2,1)S(1)} %bitcast.21, bf16[128,256]{1,0:T(8,128)(2,1)S(1)} %get-tuple-element.19.grad_ref, ...), custom_call_target="tpu_custom_call" | custom-call | flops 400000000 | bytes 1000000 | tf_op jit(solution)/shard_map/pallas_call | solution.py:330
  (1 shorter events, 0.0 us)
Async XLA Ops:
  3.0 7.3 %copy-start = (bf16[1,8,16,256]{3,2,1,0:T(8,128)(2,1)S(1)}, bf16[1,8,16,256]{3,2,1,0:T(8,128)(2,1)}, u32[]{:S(2)}) copy-start(bf16[1,8,16,256]{3,2,1,0:T(8,128)(2,1)} %param.12) | copy-start | bytes 196612
  3.0 7.3 %copy-start.1 = (bf16[1,8,16,512]{3,2,1,0:T(8,128)(2,1)S(1)}, bf16[1,8,16,512]{3,2,1,0:T(8,128)(2,1)}, u32[]{:S(2)}) copy-start(bf16[1,8,16,512]{3,2,1,0:T(8,128)(2,1)} %param.9) | copy-start | bytes 393220
  3.0 7.3 %copy-start.2 = (bf16[1,8,16,256]{3,2,1,0:T(8,128)(2,1)S(1)}, bf16[1,8,16,256]{3,2,1,0:T(8,128)(2,1)}, u32[]{:S(2)}) copy-start(bf16[1,8,16,256]{3,2,1,0:T(8,128)(2,1)} %param.8) | copy-start | bytes 196612
  3.0 15.1 %all-to-all-start = ((bf16[32,16,128]{2,1,0:T(8,128)(2,1)}), bf16[32,16,128]{2,1,0:T(8,128)(2,1)S(1)}, u32[]{:S(2)}, u32[]{:S(2)}) async-start(bf16[32,16,128]{2,1,0:T(8,128)(2,1)} %bitcast.3), calls=%async_computation | async-start | bytes 262144 | tf_op jit(solution)/shard_map/all_to_all | solution.py:367
  10.4 9.6 %collective-permute-start = (bf16[144,512]{1,0:T(8,128)(2,1)S(1)}, bf16[144,512]{1,0:T(8,128)(2,1)S(1)}, u32[]{:S(2)}, u32[]{:S(2)}) collective-permute-start(bf16[144,512]{1,0:T(8,128)(2,1)S(1)} %get-tuple-element.20), channel_id=1, source_target_pairs={{0,1},{1,0},{2,3},{3,2},{4,5},{5,4},{6,7},{7,6},{8,9},{9,8},{10,11... | collective-permute-start | bytes 442376 | tf_op jit(solution)/shard_map/ppermute | solution.py:328
  12.3 5.8 %copy-start.3 = (s32[4]{0:T(128)S(1)}, s32[4]{0:T(128)}, u32[]{:S(2)}) copy-start(s32[4]{0:T(128)} %valid_ref.3) | copy-start | bytes 52
  12.3 7.8 %collective-permute-start.1 = (bf16[144,512]{1,0:T(8,128)(2,1)S(1)}, bf16[144,512]{1,0:T(8,128)(2,1)S(1)}, u32[]{:S(2)}, u32[]{:S(2)}) collective-permute-start(bf16[144,512]{1,0:T(8,128)(2,1)S(1)} %get-tuple-element.21), channel_id=1, source_target_pairs={{1,2},{2,1},{3,4},{4,3},{5,6},{6,5},{9,10},{10,9},{11,12},{12,11},... | collective-permute-start | bytes 442376 | tf_op jit(solution)/shard_map/ppermute | solution.py:329

commit v3 on v2

--- a/solution.py
+++ b/solution.py
@@ -46,10 +46,10 @@
 def softmax_grads(scores, weight_grad, axis):
     top = jnp.max(scores, axis=axis, keepdims=True)
     raised = jnp.exp(scores - top)
-    weights = raised * (1.0 / jnp.sum(raised, axis=axis, keepdims=True))
-    low = weights.astype(BF16)
-    row_dot = jnp.sum(low.astype(F32) * weight_grad, axis=axis, keepdims=True)
-    return low, (weights * (weight_grad - row_dot)).astype(BF16)
+    share = 1.0 / jnp.sum(raised, axis=axis, keepdims=True)
+    row_dot = jnp.sum(raised * weight_grad, axis=axis, keepdims=True) * share
+    weights = raised * share
+    return weights.astype(BF16), (weights * (weight_grad - row_dot)).astype(BF16)
 
 
 def send_kernel(
@@ -64,7 +64,7 @@
     copies = [
         pltpu.make_async_copy(source, target, sems.at[1 + at])
         for at, (source, target) in enumerate(
-            ((cot_hbm, cot_ref), (cq_hbm, cq_ref), (ckv_hbm, ckv_ref))
+            tuple((cot_hbm.at[pl.ds(r, 32)], cot_ref.at[pl.ds(r, 32)]) for r in range(0, 128, 32)) + ((cq_hbm, cq_ref), (ckv_hbm, ckv_ref))
         )
     ]
     for copy in copies:
@@ -128,98 +128,130 @@
         pack(far_ref, False)
 
 
-def fine_kernel(cols, valid_ref, after_ref, q_ref, kv_ref, grad_ref, near_ref, far_ref, dq_ref, dkv_ref):
+def plan_kernel(
+    cols, valid_ref, q_ref, kv_ref, grad_ref,
+    own_ref, above_ref, below_ref, queries_ref, grads_ref, keys_t_ref,
+):
     radius = KERNEL // 2
     pixels, width = q_ref.shape
     rows = pixels // cols
+    scale = 1.0 / math.sqrt(HD)
+    band, frame = lax.axis_index("rows"), lax.axis_index("frames")
+    first, last = band == 0, band == lax.axis_size("rows") - 1
+    valid = sum(
+        jnp.where(frame == f, valid_ref[:, f : f + 1], 0) for f in range(valid_ref.shape[1])
+    )
+
+    def bias(ref, key_row, lane_rows, query_row):
+        place = iota(ref.shape, 0)
+        krow, kcol = key_row(place // cols), place % cols
+        lane = iota(ref.shape, 1)
+        qrow, qcol = lane // cols % lane_rows + query_row, lane % cols
+        seen = (jnp.abs(krow - qrow) <= radius) & (jnp.abs(kcol - qcol) <= radius) & (kcol < valid)
+        seen = seen & ((krow >= 0) | jnp.logical_not(first))
+        seen = seen & ((krow < rows) | jnp.logical_not(last))
+        seen = seen | ((krow == qrow) & (kcol == qcol))
+        ref[...] = jnp.where(seen, 0.0, NEGATIVE)
+
+    def own_row(at):
+        above = at - rows - radius
+        return jnp.where(at < rows, at, jnp.where(above < 0, above, above + rows))
+
+    bias(own_ref, own_row, rows, 0)
+    bias(above_ref, lambda at: jnp.where(at < radius, at, at - 3 * radius), radius + 1, -radius)
+    bias(below_ref, lambda at: at + rows - radius, radius + 1, rows)
+    queries_ref[...] = jnp.concatenate(pairs_of(q_ref[...] * scale), axis=0)
+    grads_ref[...] = jnp.concatenate(pairs_of(grad_ref[...]), axis=0)
+    keys_t_ref[...] = kv_ref[:, :width].T
+
+
+def fine_kernel(cols, carried, *refs):
+    (kv_ref, near_ref, far_ref, own_ref, above_ref, below_ref, queries_ref, grads_ref, keys_t_ref) = refs[:9]
+    outs = refs[9 + carried : 11 + 2 * carried]
+    dq_ref, dkv_ref, sems = refs[11 + 2 * carried :]
+    copies = [
+        pltpu.make_async_copy(source, target, sems.at[2 + at])
+        for at, (source, target) in enumerate(zip(refs[9 : 9 + carried], outs[2:]))
+    ]
+    for copy in copies:
+        copy.start()
+    radius = KERNEL // 2
+    pixels, width = dq_ref.shape
     one, two = radius * cols, 2 * radius * cols
     scale = 1.0 / math.sqrt(HD)
-    band = lax.axis_index("rows")
-    valid = valid_ref[lax.axis_index("frames")]
-    first, last = band == 0, band == lax.axis_size("rows") - 1
-    even = band % 2 == 0
+    even = lax.axis_index("rows") % 2 == 0
 
     def received(rows_at, cols_at):
         near, far = near_ref[rows_at, cols_at], far_ref[rows_at, cols_at]
         return jnp.where(even, far, near), jnp.where(even, near, far)
 
-    def extended(cols_at):
-        above, below = received(slice(0, two), cols_at)
-        return jnp.concatenate([above, kv_ref[:, cols_at], below], axis=0)
-
-    keys, values = extended(slice(0, width)), extended(slice(width, 2 * width))
+    def joined(table):
+        return jnp.concatenate(table, axis=0)
+
+    k_above, k_below = received(slice(0, two), slice(0, width))
+    v_above, v_below = received(slice(0, two), slice(width, 2 * width))
     q_above, q_below = received(slice(two, two + one), slice(0, width))
     g_above, g_below = received(slice(two, two + one), slice(width, 2 * width))
-
-    def bias(key_count, key_row, lanes, query_count, query_row, ends):
-        key, lane = iota((key_count, lanes), 0), iota((key_count, lanes), 1) & (query_count - 1)
-        krow, kcol = (key >> 4) + key_row, key & (cols - 1)
-        qrow, qcol = (lane >> 4) + query_row, lane & (cols - 1)
-        seen = (jnp.abs(krow - qrow) <= radius) & (jnp.abs(kcol - qcol) <= radius) & (kcol < valid)
-        if ends:
-            seen = seen & ((krow >= 0) | jnp.logical_not(first))
-            seen = seen & ((krow < rows) | jnp.logical_not(last))
-        seen = seen | ((krow == qrow) & (kcol == qcol))
-        return jnp.where(seen, 0.0, NEGATIVE)
-
-    lo, hi = one, one + pixels + two
-    own_keys, own_values = keys[lo:hi], values[lo:hi]
-    own_bias = bias(hi - lo, -radius, pixels, pixels, 0, True)
-    own_bias = jnp.concatenate([own_bias, own_bias], axis=1)
-    keys_t = own_keys.T
-    dq, dk, dv = [], [], []
-    for p, (query, grad) in enumerate(zip(pairs_of(q_ref[...] * scale), pairs_of(grad_ref[...]))):
+    keys, values = kv_ref[:, :width], kv_ref[:, width:]
+    own_keys = joined([keys, k_above[one:], k_below[:one]])
+    own_values = joined([values, v_above[one:], v_below[:one]])
+    keys_t = jnp.concatenate([keys_t_ref[...], joined([k_above[one:], k_below[:one]]).T], axis=1)
+    pad = jnp.zeros((cols, width), BF16)
+    sides = [
+        (
+            joined([keys[:one], k_above]),
+            joined([values[:one], v_above]),
+            pairs_of(joined([q_above * scale, pad])),
+            pairs_of(joined([g_above, pad])),
+            above_ref,
+        ),
+        (
+            joined([keys[pixels - one :], k_below]),
+            joined([values[pixels - one :], v_below]),
+            pairs_of(joined([q_below * scale, pad])),
+            pairs_of(joined([g_below, pad])),
+            below_ref,
+        ),
+    ]
+    rest = jnp.zeros((pixels - one, LANES), BF16)
+    stack = 2 * pixels
+    own_bias = jnp.concatenate([own_ref[...], own_ref[...]], axis=1)
+    for p in range(width // LANES):
         at = slice(p * LANES, (p + 1) * LANES)
+        query, grad = (ref[p * stack : (p + 1) * stack] for ref in (queries_ref, grads_ref))
         low, sgrad = softmax_grads(
             dot_nt(own_keys[:, at], query) + own_bias, dot_nt(own_values[:, at], grad), 0
         )
         dq_t = dot_nn(keys_t[at], sgrad)
-        dq_t = jnp.concatenate([dq_t[:HD, :pixels], dq_t[HD:, pixels:]], axis=0)
-        dq.append((dq_t * scale).T)
-        dk.append(dot_nn(sgrad[one : one + pixels], query))
-        dv.append(dot_nn(low[one : one + pixels], grad))
-    dq_ref[...] = jnp.concatenate(dq, axis=1).astype(BF16)
-
-    pad = jnp.zeros((cols, width), BF16)
-
-    def outside(query, grad, key_lo, key_row, query_row, keep):
-        count, lanes = one + two, 2 * (one + cols)
-        outside_bias = bias(count, key_row, lanes, one + cols, query_row, False)
-        query, grad = (
-            pairs_of(jnp.concatenate([t, pad], axis=0)) for t in (query * scale, grad)
-        )
-        found = []
-        for p in range(len(query)):
-            at = slice(p * LANES, (p + 1) * LANES)
+        dq_t = joined([dq_t[:HD, :pixels], dq_t[HD:, pixels:]])
+        dq_ref[:, at] = (dq_t * scale).T.astype(BF16)
+        lows, sgrads, all_queries, all_grads = [low[:pixels]], [sgrad[:pixels]], [query], [grad]
+        for side, (side_keys, side_values, side_query, side_grad, side_bias) in enumerate(sides):
             low, sgrad = softmax_grads(
-                dot_nt(keys[key_lo : key_lo + count, at], query[p]) + outside_bias,
-                dot_nt(values[key_lo : key_lo + count, at], grad[p]),
+                dot_nt(side_keys[:, at], side_query[p]) + side_bias[...],
+                dot_nt(side_values[:, at], side_grad[p]),
                 0,
             )
-            found.append(
-                (
-                    dot_nn(sgrad[keep : keep + one], query[p]),
-                    dot_nn(low[keep : keep + one], grad[p]),
-                )
-            )
-        return found
-
-    above = outside(q_above, g_above, 0, -2 * radius, -radius, two)
-    below = outside(q_below, g_below, pixels + one, rows - radius, rows, 0)
-    for p in range(len(dk)):
-        for at, inner in enumerate((dk[p], dv[p])):
-            lo = at * width + p * LANES
-            dkv_ref[:, lo : lo + LANES] = jnp.concatenate(
-                [
-                    inner[:one] + above[p][at],
-                    inner[one : pixels - one],
-                    inner[pixels - one :] + below[p][at],
-                ],
-                axis=0,
-            ).astype(BF16)
-
-
-def coarse_kernel(frames, tokens, valid_ref, x_ref, dq_ref, dk_ref, dv_ref, after_ref, wide, low_ref, sg_ref):
+            order = slice(None, None, -1 if side else 1)
+            lows.append(joined([low[:one], rest][order]))
+            sgrads.append(joined([sgrad[:one], rest][order]))
+            all_queries.append(side_query[p])
+            all_grads.append(side_grad[p])
+        dkv_ref[:, at] = dot_nn(jnp.concatenate(sgrads, axis=1), joined(all_queries)).astype(BF16)
+        dkv_ref[:, width + p * LANES : width + (p + 1) * LANES] = dot_nn(
+            jnp.concatenate(lows, axis=1), joined(all_grads)
+        ).astype(BF16)
+    copies += [
+        pltpu.make_async_copy(source, target, sems.at[at])
+        for at, (source, target) in enumerate(((dq_ref, outs[0]), (dkv_ref, outs[1])))
+    ]
+    for copy in copies[carried:]:
+        copy.start()
+    for copy in copies:
+        copy.wait()
+
+
+def coarse_kernel(frames, tokens, valid_ref, x_ref, dq_ref, dk_ref, dv_ref, wide, low_ref, sg_ref):
     bands = lax.axis_size("rows")
     width = dq_ref.shape[-1]
     parts = width // LANES
@@ -227,7 +259,6 @@
     band = lax.axis_index("rows")
     scale = 1.0 / math.sqrt(HD)
     wide[...] = x_ref[...].astype(F32)
-    after_ref[...] = jnp.zeros_like(after_ref)
     devices, own = frames * bands, frames * tokens
 
     def every(array, b):
@@ -249,7 +280,7 @@
         token, frame = place // devices, place // bands % frames
         limit = jnp.zeros(shape, jnp.int32)
         for f in range(frames):
-            limit = jnp.where(frame == f, valid_ref[f], limit)
+            limit = jnp.where(frame == f, valid_ref[:, f : f + 1], limit)
         return jnp.where(token * POOL < limit, 0.0, NEGATIVE)
 
     bias, own_bias = key_bias((count, 2 * count), 0), key_bias((2 * own, count), 1)
@@ -307,7 +338,7 @@
     return jax.ShapeDtypeStruct(shape, dtype)
 
 
-def fine_level(after, gain, fine_q, fine_kv, cotangent, valid_cols):
+def fine_level(carried, gain, fine_q, fine_kv, cotangent, valid_cols):
     bands = lax.axis_size("rows")
     _, rows, cols, width = fine_q.shape
     pixels = rows * cols
@@ -327,15 +358,37 @@
     others = [(i, ((i + 1) ^ 1) - 1) for i in range(1, bands) if ((i + 1) ^ 1) - 1 < bands]
     near = lax.ppermute(near, "rows", pairs)
     far = lax.ppermute(far, "rows", others)
-    grad_q, grad_kv = pl.pallas_call(
-        functools.partial(fine_kernel, cols),
-        in_specs=[smem()] + [vmem()] * 6,
-        out_specs=[vmem()] * 2,
-        out_shape=[out((pixels, width)), out((pixels, 2 * width))],
+    outside = (3 * radius * cols, 2 * (radius + 1) * cols)
+    stacked = (2 * width // LANES * pixels, LANES)
+    plan = pl.pallas_call(
+        functools.partial(plan_kernel, cols),
+        in_specs=[vmem()] * 4,
+        out_specs=[vmem()] * 6,
+        out_shape=[
+            out((pixels + 2 * radius * cols, pixels), F32),
+            out(outside, F32),
+            out(outside, F32),
+            out(stacked),
+            out(stacked),
+            out((width, pixels)),
+        ],
+        compiler_params=params(),
+    )(valid_cols.reshape(1, -1), query, key_value, grad)
+    grads = pl.pallas_call(
+        functools.partial(fine_kernel, cols, len(carried)),
+        in_specs=[vmem()] * (9 + len(carried)),
+        out_specs=[hbm()] * (2 + len(carried)),
+        out_shape=[out((pixels, width)), out((pixels, 2 * width))]
+        + [out(x.shape) for x in carried],
+        scratch_shapes=[
+            pltpu.VMEM((pixels, width), BF16),
+            pltpu.VMEM((pixels, 2 * width), BF16),
+            pltpu.SemaphoreType.DMA((2 + len(carried),)),
+        ],
         compiler_params=params(),
         cost_estimate=pl.CostEstimate(flops=400_000_000, bytes_accessed=1_000_000, transcendentals=300_000),
-    )(valid_cols, after, query, key_value, grad, near, far)
-    return grad_q.reshape(fine_q.shape), grad_kv.reshape(fine_kv.shape)
+    )(key_value, near, far, *plan, *carried)
+    return (grads[0].reshape(fine_q.shape), grads[1].reshape(fine_kv.shape), *grads[2:])
 
 
 def coarse_direct(coarse_q, coarse_kv, cotangent, gain_table, timesteps, valid_cols):
@@ -354,7 +407,7 @@
             pltpu.VMEM((8, width), F32),
             pltpu.VMEM((tokens, cwidth), BF16),
             pltpu.VMEM((tokens, 2 * cwidth), BF16),
-            pltpu.SemaphoreType.DMA((4,)),
+            pltpu.SemaphoreType.DMA((7,)),
         ],
         compiler_params=params(),
     )(
@@ -372,11 +425,11 @@
         tiled=True,
     ).reshape(frames * bands * tile, LANES)
     count = frames * bands * tokens
-    *outs, after = pl.pallas_call(
+    outs = pl.pallas_call(
         functools.partial(coarse_kernel, frames, tokens),
-        in_specs=[smem(), vmem()],
-        out_specs=[vmem()] * 4,
-        out_shape=[out((frames, tokens, head_width))] * 3 + [out((8, LANES), F32)],
+        in_specs=[vmem()] * 2,
+        out_specs=[vmem()] * 3,
+        out_shape=[out((frames, tokens, head_width))] * 3,
         scratch_shapes=[
             pltpu.VMEM(held.shape, F32),
             pltpu.VMEM((head_width // LANES, count, 2 * count), F32),
@@ -384,8 +437,8 @@
         ],
         compiler_params=params(),
         cost_estimate=pl.CostEstimate(flops=100_000_000_000, bytes_accessed=100_000_000, transcendentals=0),
-    )(valid_cols, held)
-    return tuple(x.reshape(frames, 1, tokens, head_width) for x in outs), gain, after
+    )(valid_cols.reshape(1, -1), held)
+    return outs, gain
 
 
 def normalize(scores):
@@ -477,7 +530,7 @@
         coarse_qgrad.reshape(out_dims).astype(BF16),
         total_keys.reshape(out_dims).astype(BF16),
         total_values.reshape(out_dims).astype(BF16),
-    ), frame_gain, jnp.zeros((8, LANES), F32)
+    ), frame_gain
 
 
 def local(fine_q, fine_kv, coarse_q, coarse_kv, cotangent, gain_table, timesteps, valid_cols):
@@ -489,12 +542,15 @@
         and 4 * tokens * head_width // LANES == 16
         and frames * bands * tokens <= 128
     )
-    coarse = coarse_direct if direct else coarse_gathered
-    coarse_grads, gain, after = coarse(
-        coarse_q, coarse_kv, cotangent, gain_table, timesteps, valid_cols
-    )
-    fine_grads = fine_level(after, gain, fine_q, fine_kv, cotangent, valid_cols)
-    return fine_grads + coarse_grads
+    operands = (coarse_q, coarse_kv, cotangent, gain_table, timesteps, valid_cols)
+    fine = (fine_q, fine_kv, cotangent, valid_cols)
+    if direct:
+        carried, gain = coarse_direct(*operands)
+        grad_q, grad_kv, *coarse_grads = fine_level(carried, gain, *fine)
+        shape = (frames, 1, tokens, head_width)
+        return (grad_q, grad_kv, *(x.reshape(shape) for x in coarse_grads))
+    coarse_grads, gain = coarse_gathered(*operands)
+    return (*fine_level([], gain, *fine), *coarse_grads)
 
 
 def solution(mesh):

time: 23.4 us -> 22 us (0.940)
  Pallas kernels: 6.84 us -> 4.79 us
  local copies, waits for them, and re-layouts: 0.02 us -> 0.67 us
    pallas_call x1, Pallas kernels: 1.97 us -> 0.75 us  [coarse_direct(): pl.pallas_call(functools.partial(coarse_kernel, frames, tokens), in_specs...]
    all_to_all x1, waiting for transfers between devices: 5.03 us -> 4.14 us  [coarse_direct(): lax.all_to_all(sent.reshape(frames * bands, tile, LANES), ('frames', 'row...]
    ppermute x1, waiting for transfers between devices: 0.01 us -> 0.9 us  [fine_level(): near = lax.ppermute(near, 'rows', pairs)]
    pallas_call x1 -> x2, Pallas kernels: 3.12 us -> 2.32 us  [the longest x1 1.96 us: fine_level(): pl.pallas_call(functools.partial(fine_kernel, cols, len(carried)), in_spe...]
    unnamed x8, local copies, waits for them, and re-layouts: 0.02 us -> 0.67 us
  transfers between devices with their start and end apart: 3 -> 3, of which waited for: 1 -> 2; matrix products, arithmetic and copies ran while one was open for 0% -> 0% of each run, Pallas kernels for 9% -> 5%
where the time goes in v3:
time: 22 us; the launch traced here: 21.7 us
  starting transfers between devices  9.79 us (44%)
  waiting for transfers between devices  5.04 us (23%)
  Pallas kernels  4.79 us (22%)
  between operations  1.38 us (6%)
  local copies, waits for them, and re-layouts  0.67 us (3%)
    all_to_all x1, starting transfers between devices, coarse_direct(): lax.all_to_all(sent.reshape(frames * bands, tile, LANES), ('frames', 'row...  7.3 us
    all_to_all x1, waiting for transfers between devices, coarse_direct(): lax.all_to_all(sent.reshape(frames * bands, tile, LANES), ('frames', 'row...  4.14 us
    pallas_call x1, Pallas kernels, fine_level(): pl.pallas_call(functools.partial(fine_kernel, cols, len(carried)), in_spe...  1.96 us
    ppermute x1, starting transfers between devices, fine_level(): near = lax.ppermute(near, 'rows', pairs)  1.83 us
    pallas_call x1, Pallas kernels, coarse_direct(): pl.pallas_call(functools.partial(send_kernel, cols, bands), in_specs=[sme...  1.67 us
    ppermute x1, waiting for transfers between devices, fine_level(): near = lax.ppermute(near, 'rows', pairs)  0.9 us
    pallas_call x1, Pallas kernels, coarse_direct(): pl.pallas_call(functools.partial(coarse_kernel, frames, tokens), in_specs...  0.75 us
    unnamed x8, local copies, waits for them, and re-layouts  0.67 us
  transfers between devices with their start and end apart: 3, of which 2 were waited for; matrix products, arithmetic and copies ran while one was open for 0% of the time, Pallas kernels for 5%

profile of v3, /device:TPU:0, one launch (start us, length us, event | category | flops | bytes accessed | tf_op | source)
XLA Modules:
  0.0 21.7 jit_solution(3171164639387721294)
XLA Ops:
  1.3 1.7 %shard_map.119 = (bf16[512,128]{1,0:T(8,128)(2,1)}, f32[1,256]{1,0:T(1,128)S(1)}) custom-call(s32[1]{0:T(128)S(6)} %copy.16.step_ref, bf16[128,256]{1,0:T(8,128)(2,1)} %bitcast.24, f32[1000,256]{1,0:T(8,128)} %gain_hbm.1, bf16[2,1024]{1,0:T(2,128)(2,1)} %bitcast.30, bf16[2,2048]{1,0:T(2,128)(2,1)} %bitcast.29), custom_call_target="tpu_custom_call" | custom-call | tf_op jit(solution)/shard_map/pallas_call | solution.py:400
  3.0 0.0 copy-start
  3.0 0.0 copy-start.1
  3.0 0.0 copy-start.2
  3.0 7.3 %all-to-all-start = ((bf16[32,16,128]{2,1,0:T(8,128)(2,1)}), bf16[32,16,128]{2,1,0:T(8,128)(2,1)S(1)}, u32[]{:S(2)}, u32[]{:S(2)}) async-start(bf16[32,16,128]{2,1,0:T(8,128)(2,1)} %bitcast.6), calls=%async_computation | async-start | bytes 262144 | tf_op jit(solution)/shard_map/all_to_all | solution.py:420
  10.3 0.0 copy-done
  10.3 0.0 copy-done.1
  10.3 0.0 copy-done.2
  10.4 1.8 %collective-permute-start = (bf16[144,512]{1,0:T(8,128)(2,1)S(1)}, bf16[144,512]{1,0:T(8,128)(2,1)S(1)}, u32[]{:S(2)}, u32[]{:S(2)}) collective-permute-start(bf16[144,512]{1,0:T(8,128)(2,1)S(1)} %get-tuple-element.25), channel_id=1, source_target_pairs={{0,1},{1,0},{2,3},{3,2},{4,5},{5,4},{6,7},{7,6},{8,9},{9,8},{10,11... | collective-permute-start | bytes 442376 | tf_op jit(solution)/shard_map/ppermute | solution.py:359
  12.2 0.7 %collective-permute-start.1 = (bf16[144,512]{1,0:T(8,128)(2,1)S(1)}, bf16[144,512]{1,0:T(8,128)(2,1)S(1)}, u32[]{:S(2)}, u32[]{:S(2)}) collective-permute-start(bf16[144,512]{1,0:T(8,128)(2,1)S(1)} %get-tuple-element.26), channel_id=1, source_target_pairs={{1,2},{2,1},{3,4},{4,3},{5,6},{6,5},{9,10},{10,9},{11,12},{12,11},... | collective-permute-start | bytes 442376 | tf_op jit(solution)/shard_map/ppermute | solution.py:360
  12.9 0.0 copy-start.3
  12.9 0.6 %copy-done.3 = s32[4]{0:T(128)S(1)} copy-done((s32[4]{0:T(128)S(1)}, s32[4]{0:T(128)}, u32[]{:S(2)}) %copy-start.3) | copy-done | bytes 40
  13.5 0.4 %shard_map.121 = (f32[224,128]{1,0:T(8,128)S(1)}, f32[144,128]{1,0:T(8,128)S(1)}, f32[144,128]{1,0:T(8,128)S(1)}, bf16[512,128]{1,0:T(8,128)(2,1)S(1)}, bf16[512...) custom-call(s32[1,4]{1,0:T(1,128)S(1)} %bitcast.27, bf16[128,256]{1,0:T(8,128)(2,1)S(1)} %bitcast.23, ...), custom_call_target="tpu_custom_call" | custom-call | tf_op jit(solution)/shard_map/pallas_call | solution.py:363
  13.9 4.1 %all-to-all-done = bf16[32,16,128]{2,1,0:T(8,128)(2,1)S(1)} async-done(((bf16[32,16,128]{2,1,0:T(8,128)(2,1)}), bf16[32,16,128]{2,1,0:T(8,128)(2,1)S(1)}, u32[]{:S(2)}, u32[]{:S(2)}) %all-to-all-start) | async-done | bytes 131104 | tf_op jit(solution)/shard_map/all_to_all | solution.py:420
  18.1 0.8 %shard_map.122 = (bf16[4,2,256]{2,1,0:T(2,128)(2,1)S(1)}, bf16[4,2,256]{2,1,0:T(2,128)(2,1)S(1)}, bf16[4,2,256]{2,1,0:T(2,128)(2,1)S(1)}) custom-call(s32[1,4]{1,0:T(1,128)S(1)} %bitcast.28, bf16[512,128]{1,0:T(8,128)(2,1)S(1)} %bitcast.26), custom_call_target="tpu_custom_call" | custom-call | flops 99999997952 | bytes 100000000 | tf_op jit(solution)/shard_map/pallas_call | solution.py:428
  18.8 0.9 %collective-permute-done.refs_1_ = bf16[144,512]{1,0:T(8,128)(2,1)S(1)} collective-permute-done((bf16[144,512]{1,0:T(8,128)(2,1)S(1)}, bf16[144,512]{1,0:T(8,128)(2,1)S(1)}, u32[]{:S(2)}, u32[]{:S(2)}) %collective-permute-start) | collective-permute-done | bytes 147488 | tf_op jit(solution)/shard_map/ppermute | solution.py:359
  19.7 0.0 collective-permute-done.1.refs_2_
  19.7 2.0 %shard_map.123 = (bf16[128,256]{1,0:T(8,128)(2,1)}, bf16[128,512]{1,0:T(8,128)(2,1)}, bf16[4,2,256]{2,1,0:T(2,128)(2,1)}, bf16[4,2,256]{2,1,0:T(2,128)(2,1)}, bf16[4,2,256]{2,1,0:T(2,128)(2,1)}) custom-call(bf16[128,512]{1,0:T(8,128)(2,1)S(1)} %bitcast.21, bf16[144,512]{1,0:T(8,128)(2,1)S(1)} %collective-permute-done.refs_1_, ...), custom_call_target="tpu_custom_call" | custom-call | flops 400000000 | bytes 1000000 | tf_op jit(solution)/shard_map/pallas_call | solution.py:377
  (1 shorter events, 0.0 us)
Async XLA Ops:
  3.0 7.3 %copy-start = (bf16[1,8,16,512]{3,2,1,0:T(8,128)(2,1)S(1)}, bf16[1,8,16,512]{3,2,1,0:T(8,128)(2,1)}, u32[]{:S(2)}) copy-start(bf16[1,8,16,512]{3,2,1,0:T(8,128)(2,1)} %param.9) | copy-start | bytes 393220
  3.0 7.3 %copy-start.1 = (bf16[1,8,16,256]{3,2,1,0:T(8,128)(2,1)S(1)}, bf16[1,8,16,256]{3,2,1,0:T(8,128)(2,1)}, u32[]{:S(2)}) copy-start(bf16[1,8,16,256]{3,2,1,0:T(8,128)(2,1)} %param.8) | copy-start | bytes 196612
  3.0 7.3 %copy-start.2 = (bf16[1,8,16,256]{3,2,1,0:T(8,128)(2,1)S(1)}, bf16[1,8,16,256]{3,2,1,0:T(8,128)(2,1)}, u32[]{:S(2)}) copy-start(bf16[1,8,16,256]{3,2,1,0:T(8,128)(2,1)} %param.12) | copy-start | bytes 196612
  3.0 15.1 %all-to-all-start = ((bf16[32,16,128]{2,1,0:T(8,128)(2,1)}), bf16[32,16,128]{2,1,0:T(8,128)(2,1)S(1)}, u32[]{:S(2)}, u32[]{:S(2)}) async-start(bf16[32,16,128]{2,1,0:T(8,128)(2,1)} %bitcast.6), calls=%async_computation | async-start | bytes 262144 | tf_op jit(solution)/shard_map/all_to_all | solution.py:420
  10.4 9.3 %collective-permute-start = (bf16[144,512]{1,0:T(8,128)(2,1)S(1)}, bf16[144,512]{1,0:T(8,128)(2,1)S(1)}, u32[]{:S(2)}, u32[]{:S(2)}) collective-permute-start(bf16[144,512]{1,0:T(8,128)(2,1)S(1)} %get-tuple-element.25), channel_id=1, source_target_pairs={{0,1},{1,0},{2,3},{3,2},{4,5},{5,4},{6,7},{7,6},{8,9},{9,8},{10,11... | collective-permute-start | bytes 442376 | tf_op jit(solution)/shard_map/ppermute | solution.py:359
  12.2 7.5 %collective-permute-start.1 = (bf16[144,512]{1,0:T(8,128)(2,1)S(1)}, bf16[144,512]{1,0:T(8,128)(2,1)S(1)}, u32[]{:S(2)}, u32[]{:S(2)}) collective-permute-start(bf16[144,512]{1,0:T(8,128)(2,1)S(1)} %get-tuple-element.26), channel_id=1, source_target_pairs={{1,2},{2,1},{3,4},{4,3},{5,6},{6,5},{9,10},{10,9},{11,12},{12,11},... | collective-permute-start | bytes 442376 | tf_op jit(solution)/shard_map/ppermute | solution.py:360
  12.9 0.7 %copy-start.3 = (s32[4]{0:T(128)S(1)}, s32[4]{0:T(128)}, u32[]{:S(2)}) copy-start(s32[4]{0:T(128)} %param.15) | copy-start | bytes 52

commit v4 on v3

--- a/solution.py
+++ b/solution.py
@@ -53,8 +53,8 @@
 
 
 def send_kernel(
-    cols, bands, step_ref, cot_hbm, gain_hbm, cq_hbm, ckv_hbm,
-    send_ref, gain_ref, cot_ref, eight_ref, cq_ref, ckv_ref, sems,
+    cols, bands, step_ref, valid_hbm, cot_hbm, gain_hbm, cq_hbm, ckv_hbm,
+    send_ref, gain_ref, valid_ref, cot_ref, eight_ref, cq_ref, ckv_ref, sems,
 ):
     step = step_ref[0]
     eight = eight_ref.shape[0]
@@ -64,7 +64,7 @@
     copies = [
         pltpu.make_async_copy(source, target, sems.at[1 + at])
         for at, (source, target) in enumerate(
-            tuple((cot_hbm.at[pl.ds(r, 32)], cot_ref.at[pl.ds(r, 32)]) for r in range(0, 128, 32)) + ((cq_hbm, cq_ref), (ckv_hbm, ckv_ref))
+            tuple((cot_hbm.at[pl.ds(r, 32)], cot_ref.at[pl.ds(r, 32)]) for r in range(0, 128, 32)) + ((cq_hbm, cq_ref), (ckv_hbm, ckv_ref), (valid_hbm, valid_ref))
         )
     ]
     for copy in copies:
@@ -104,142 +104,227 @@
             send_ref[start : start + height, :] = tile
 
 
-def prep_kernel(cols, gain_ref, q_ref, kv_ref, cot_ref, near_ref, far_ref, grad_ref):
+def valid_here(valid_ref):
+    frame = lax.axis_index("frames")
+    return sum(
+        jnp.where(frame == f, valid_ref[:, f : f + 1], 0) for f in range(valid_ref.shape[1])
+    )
+
+
+def window_bias(shape, cols, valid, key_row, lane_rows, query_row, present=None):
+    radius = KERNEL // 2
+    place, lane = iota(shape, 0), iota(shape, 1)
+    krow, kcol = key_row(place // cols), place % cols
+    qrow, qcol = lane // cols % lane_rows + query_row, lane % cols
+    seen = (jnp.abs(krow - qrow) <= radius) & (jnp.abs(kcol - qcol) <= radius) & (kcol < valid)
+    if present is not None:
+        seen = seen & present(krow)
+    seen = seen | ((krow == qrow) & (kcol == qcol))
+    return jnp.where(seen, 0.0, NEGATIVE)
+
+
+def partial_sums(scores, weight_grad):
+    top = jnp.max(scores, axis=0, keepdims=True)
+    raised = jnp.exp(scores - top)
+    total = jnp.sum(raised, axis=0, keepdims=True)
+    return top, raised, total, jnp.sum(raised * weight_grad, axis=0, keepdims=True)
+
+
+def completed(kept, scores, weight_grad):
+    top_kept, total_kept, dot_kept = kept
+    top = jnp.maximum(top_kept, jnp.max(scores, axis=0, keepdims=True))
+    factor = jnp.exp(top_kept - top)
+    raised = jnp.exp(scores - top)
+    total = total_kept * factor + jnp.sum(raised, axis=0, keepdims=True)
+    share = jnp.where(total > 0, 1.0 / total, 0.0)
+    dot = dot_kept * factor + jnp.sum(raised * weight_grad, axis=0, keepdims=True)
+    return factor * share, raised * share, dot * share
+
+
+def in_parts(row):
+    parts = []
+    for _ in range(3):
+        part = row.astype(BF16).astype(F32)
+        parts.append(part)
+        row = row - part
+    return parts
+
+
+def prep_kernel(cols, valid_ref, gain_ref, q_ref, kv_ref, cot_ref, near_ref, far_ref, grad_ref):
     radius = KERNEL // 2
     pixels, width = q_ref.shape
+    rows = pixels // cols
     one, two = radius * cols, 2 * radius * cols
+    scale = 1.0 / math.sqrt(HD)
     even = lax.axis_index("rows") % 2 == 0
+    valid = valid_here(valid_ref)
     grad_ref[...] = (gain_ref[...] * cot_ref[...].astype(F32)).astype(BF16)
-
-    def pack(target, top):
-        lo_one, lo_two = (0, 0) if top else (pixels - one, pixels - two)
-        target[:two, :] = kv_ref[lo_two : lo_two + two, :]
-        target[two:, :width] = q_ref[lo_one : lo_one + one, :]
-        target[two:, width:] = grad_ref[lo_one : lo_one + one, :]
+    pad = jnp.zeros((cols, width), BF16)
+
+    sides = []
+    for lo, key_lo, query_row in ((0, 0, 0), (pixels - one, pixels - two, radius)):
+        bias = window_bias((two, LANES), cols, valid, lambda at: at, radius + 1, query_row)
+        query = pairs_of(jnp.concatenate([q_ref[lo : lo + one, :] * scale, pad], axis=0))
+        grad = pairs_of(jnp.concatenate([grad_ref[lo : lo + one, :], pad], axis=0))
+        products = []
+        for p in range(width // LANES):
+            at = p * LANES
+            keys = kv_ref[key_lo : key_lo + two, at : at + LANES]
+            values = kv_ref[key_lo : key_lo + two, width + at : width + at + LANES]
+            products.append((dot_nt(keys, query[p]) + bias, dot_nt(values, grad[p])))
+        sides.append(products)
+
+    def sums(products):
+        tiles = []
+        for scores, wgrad in products:
+            top, _, total, dot = partial_sums(scores, wgrad)
+            found = [part for row in (top, total, dot) for part in in_parts(row)]
+            found.append(jnp.zeros((16 - len(found), LANES), F32))
+            tiles.append(jnp.concatenate(found, axis=0))
+        return jnp.concatenate(tiles, axis=1).astype(BF16)
+
+    upper, lower = (sums(products) for products in sides)
+
+    def pack(target, lo, found):
+        parts = (kv_ref[lo : lo + one, :width], kv_ref[lo : lo + one, width:])
+        parts += (q_ref[lo : lo + one, :], grad_ref[lo : lo + one, :])
+        for at, part in enumerate(parts):
+            target[at * one : (at + 1) * one, :] = part
+        target[len(parts) * one :, :] = found
 
     @pl.when(even)
     def _():
-        pack(near_ref, False)
-        pack(far_ref, True)
+        pack(near_ref, pixels - one, lower)
+        pack(far_ref, 0, upper)
 
     @pl.when(jnp.logical_not(even))
     def _():
-        pack(near_ref, True)
-        pack(far_ref, False)
+        pack(near_ref, 0, upper)
+        pack(far_ref, pixels - one, lower)
 
 
 def plan_kernel(
     cols, valid_ref, q_ref, kv_ref, grad_ref,
-    own_ref, above_ref, below_ref, queries_ref, grads_ref, keys_t_ref,
+    beside_ref, above_ref, below_ref, queries_ref, grads_ref, keys_t_ref, raised_ref, wgrad_ref, sums_ref,
 ):
     radius = KERNEL // 2
     pixels, width = q_ref.shape
     rows = pixels // cols
     scale = 1.0 / math.sqrt(HD)
-    band, frame = lax.axis_index("rows"), lax.axis_index("frames")
+    band = lax.axis_index("rows")
     first, last = band == 0, band == lax.axis_size("rows") - 1
-    valid = sum(
-        jnp.where(frame == f, valid_ref[:, f : f + 1], 0) for f in range(valid_ref.shape[1])
-    )
-
-    def bias(ref, key_row, lane_rows, query_row):
-        place = iota(ref.shape, 0)
-        krow, kcol = key_row(place // cols), place % cols
-        lane = iota(ref.shape, 1)
-        qrow, qcol = lane // cols % lane_rows + query_row, lane % cols
-        seen = (jnp.abs(krow - qrow) <= radius) & (jnp.abs(kcol - qcol) <= radius) & (kcol < valid)
-        seen = seen & ((krow >= 0) | jnp.logical_not(first))
-        seen = seen & ((krow < rows) | jnp.logical_not(last))
-        seen = seen | ((krow == qrow) & (kcol == qcol))
-        ref[...] = jnp.where(seen, 0.0, NEGATIVE)
-
-    def own_row(at):
-        above = at - rows - radius
-        return jnp.where(at < rows, at, jnp.where(above < 0, above, above + rows))
-
-    bias(own_ref, own_row, rows, 0)
-    bias(above_ref, lambda at: jnp.where(at < radius, at, at - 3 * radius), radius + 1, -radius)
-    bias(below_ref, lambda at: at + rows - radius, radius + 1, rows)
-    queries_ref[...] = jnp.concatenate(pairs_of(q_ref[...] * scale), axis=0)
-    grads_ref[...] = jnp.concatenate(pairs_of(grad_ref[...]), axis=0)
+    valid = valid_here(valid_ref)
+
+    def present(krow):
+        return ((krow >= 0) | jnp.logical_not(first)) & ((krow < rows) | jnp.logical_not(last))
+
+    beside_ref[...] = window_bias(
+        beside_ref.shape, cols, valid,
+        lambda at: jnp.where(at < radius, at - radius, at - radius + rows), rows, 0, present,
+    )
+    above_ref[...] = window_bias(
+        above_ref.shape, cols, valid, lambda at: at, radius + 1, -radius
+    )
+    below_ref[...] = window_bias(
+        below_ref.shape, cols, valid, lambda at: at + rows - radius, radius + 1, rows
+    )
+    bias = window_bias((pixels, pixels), cols, valid, lambda at: at, rows, 0)
+    bias = jnp.concatenate([bias, bias], axis=1)
     keys_t_ref[...] = kv_ref[:, :width].T
+    for p, (query, grad) in enumerate(zip(pairs_of(q_ref[...] * scale), pairs_of(grad_ref[...]))):
+        at = p * LANES
+        queries_ref[p], grads_ref[p] = query, grad
+        wgrad = dot_nt(kv_ref[:, width + at : width + at + LANES], grad)
+        top, raised, total, dot = partial_sums(
+            dot_nt(kv_ref[:, at : at + LANES], query) + bias, wgrad
+        )
+        raised_ref[p], wgrad_ref[p] = raised, wgrad
+        for row, value in enumerate((top, total, dot)):
+            sums_ref[p, row : row + 1, :] = value
 
 
 def fine_kernel(cols, carried, *refs):
-    (kv_ref, near_ref, far_ref, own_ref, above_ref, below_ref, queries_ref, grads_ref, keys_t_ref) = refs[:9]
-    outs = refs[9 + carried : 11 + 2 * carried]
-    dq_ref, dkv_ref, sems = refs[11 + 2 * carried :]
+    (kv_ref, near_ref, far_ref, beside_ref, above_ref, below_ref, queries_ref, grads_ref) = refs[:8]
+    (keys_t_ref, raised_ref, wgrad_ref, sums_ref) = refs[8:12]
+    outs = refs[12 + carried : 14 + 2 * carried]
+    dq_ref, dkv_ref, sems = refs[14 + 2 * carried :]
     copies = [
         pltpu.make_async_copy(source, target, sems.at[2 + at])
-        for at, (source, target) in enumerate(zip(refs[9 : 9 + carried], outs[2:]))
+        for at, (source, target) in enumerate(zip(refs[12 : 12 + carried], outs[2:]))
     ]
     for copy in copies:
         copy.start()
     radius = KERNEL // 2
     pixels, width = dq_ref.shape
-    one, two = radius * cols, 2 * radius * cols
+    one = radius * cols
     scale = 1.0 / math.sqrt(HD)
     even = lax.axis_index("rows") % 2 == 0
 
-    def received(rows_at, cols_at):
-        near, far = near_ref[rows_at, cols_at], far_ref[rows_at, cols_at]
+    def received(at):
+        rows_at = slice(at * one, (at + 1) * one) if at < 4 else slice(at * one, None)
+        near, far = near_ref[rows_at, :], far_ref[rows_at, :]
         return jnp.where(even, far, near), jnp.where(even, near, far)
 
     def joined(table):
         return jnp.concatenate(table, axis=0)
 
-    k_above, k_below = received(slice(0, two), slice(0, width))
-    v_above, v_below = received(slice(0, two), slice(width, 2 * width))
-    q_above, q_below = received(slice(two, two + one), slice(0, width))
-    g_above, g_below = received(slice(two, two + one), slice(width, 2 * width))
-    keys, values = kv_ref[:, :width], kv_ref[:, width:]
-    own_keys = joined([keys, k_above[one:], k_below[:one]])
-    own_values = joined([values, v_above[one:], v_below[:one]])
-    keys_t = jnp.concatenate([keys_t_ref[...], joined([k_above[one:], k_below[:one]]).T], axis=1)
+    beside_keys, beside_values = joined(received(0)), joined(received(1))
+    beside_t = beside_keys.T
     pad = jnp.zeros((cols, width), BF16)
-    sides = [
-        (
-            joined([keys[:one], k_above]),
-            joined([values[:one], v_above]),
-            pairs_of(joined([q_above * scale, pad])),
-            pairs_of(joined([g_above, pad])),
-            above_ref,
-        ),
-        (
-            joined([keys[pixels - one :], k_below]),
-            joined([values[pixels - one :], v_below]),
-            pairs_of(joined([q_below * scale, pad])),
-            pairs_of(joined([g_below, pad])),
-            below_ref,
-        ),
-    ]
     rest = jnp.zeros((pixels - one, LANES), BF16)
-    stack = 2 * pixels
-    own_bias = jnp.concatenate([own_ref[...], own_ref[...]], axis=1)
-    for p in range(width // LANES):
-        at = slice(p * LANES, (p + 1) * LANES)
-        query, grad = (ref[p * stack : (p + 1) * stack] for ref in (queries_ref, grads_ref))
-        low, sgrad = softmax_grads(
-            dot_nt(own_keys[:, at], query) + own_bias, dot_nt(own_values[:, at], grad), 0
+    side_lo = (0, pixels - one)
+    side_query = [pairs_of(joined([t * scale, pad])) for t in received(2)]
+    side_grad = [pairs_of(joined([t, pad])) for t in received(3)]
+    side_sums = [t.astype(F32) for t in received(4)]
+    beside_bias = jnp.concatenate([beside_ref[...], beside_ref[...]], axis=1)
+    pairs = range(width // LANES)
+    ats = [slice(p * LANES, (p + 1) * LANES) for p in pairs]
+    value_ats = [slice(width + p * LANES, width + (p + 1) * LANES) for p in pairs]
+    sides = [(side, p) for side in range(2) for p in pairs]
+    beside_scores = [dot_nt(beside_keys[:, ats[p]], queries_ref[p]) + beside_bias for p in pairs]
+    beside_wgrad = [dot_nt(beside_values[:, ats[p]], grads_ref[p]) for p in pairs]
+    side_scores, side_wgrad = {}, {}
+    for side, p in sides:
+        keys_at = slice(side_lo[side], side_lo[side] + one)
+        bias_ref = (above_ref, below_ref)[side]
+        side_scores[side, p] = (
+            dot_nt(kv_ref[keys_at, ats[p]], side_query[side][p]) + bias_ref[...]
         )
-        dq_t = dot_nn(keys_t[at], sgrad)
+        side_wgrad[side, p] = dot_nt(kv_ref[keys_at, value_ats[p]], side_grad[side][p])
+    lows, sgrads, beside_sgrads = {}, {}, {}
+    for p in pairs:
+        factor, beside_weights, row_dot = completed(
+            tuple(sums_ref[p, row : row + 1, :] for row in range(3)),
+            beside_scores[p],
+            beside_wgrad[p],
+        )
+        beside_sgrads[p] = (beside_weights * (beside_wgrad[p] - row_dot)).astype(BF16)
+        weights = raised_ref[p] * factor
+        lows[p] = weights.astype(BF16)
+        sgrads[p] = (weights * (wgrad_ref[p] - row_dot)).astype(BF16)
+    for side, p in sides:
+        found = side_sums[side][:, ats[p]]
+        kept = tuple(
+            found[row : row + 1] + found[row + 1 : row + 2] + found[row + 2 : row + 3]
+            for row in (0, 3, 6)
+        )
+        _, weights, row_dot = completed(kept, side_scores[side, p], side_wgrad[side, p])
+        order = slice(None, None, -1 if side else 1)
+        lows[side, p] = joined([weights.astype(BF16), rest][order])
+        sgrad = (weights * (side_wgrad[side, p] - row_dot)).astype(BF16)
+        sgrads[side, p] = joined([sgrad, rest][order])
+    for p in pairs:
+        dq_t = dot_nn(keys_t_ref[ats[p], :], sgrads[p]) + dot_nn(beside_t[ats[p]], beside_sgrads[p])
         dq_t = joined([dq_t[:HD, :pixels], dq_t[HD:, pixels:]])
-        dq_ref[:, at] = (dq_t * scale).T.astype(BF16)
-        lows, sgrads, all_queries, all_grads = [low[:pixels]], [sgrad[:pixels]], [query], [grad]
-        for side, (side_keys, side_values, side_query, side_grad, side_bias) in enumerate(sides):
-            low, sgrad = softmax_grads(
-                dot_nt(side_keys[:, at], side_query[p]) + side_bias[...],
-                dot_nt(side_values[:, at], side_grad[p]),
-                0,
-            )
-            order = slice(None, None, -1 if side else 1)
-            lows.append(joined([low[:one], rest][order]))
-            sgrads.append(joined([sgrad[:one], rest][order]))
-            all_queries.append(side_query[p])
-            all_grads.append(side_grad[p])
-        dkv_ref[:, at] = dot_nn(jnp.concatenate(sgrads, axis=1), joined(all_queries)).astype(BF16)
-        dkv_ref[:, width + p * LANES : width + (p + 1) * LANES] = dot_nn(
-            jnp.concatenate(lows, axis=1), joined(all_grads)
+        dq_ref[:, ats[p]] = (dq_t * scale).astype(BF16).T
+    for p in pairs:
+        dkv_ref[:, ats[p]] = dot_nn(
+            jnp.concatenate([sgrads[p], sgrads[0, p], sgrads[1, p]], axis=1),
+            joined([queries_ref[p], side_query[0][p], side_query[1][p]]),
+        ).astype(BF16)
+        dkv_ref[:, value_ats[p]] = dot_nn(
+            jnp.concatenate([lows[p], lows[0, p], lows[1, p]], axis=1),
+            joined([grads_ref[p], side_grad[0][p], side_grad[1][p]]),
         ).astype(BF16)
     copies += [
         pltpu.make_async_copy(source, target, sems.at[at])
@@ -284,34 +369,38 @@
         return jnp.where(token * POOL < limit, 0.0, NEGATIVE)
 
     bias, own_bias = key_bias((count, 2 * count), 0), key_bias((2 * own, count), 1)
-    for b in range(parts):
-        at = slice(b * LANES, (b + 1) * LANES)
-        key, value = every(1, b), every(2, b)
-        (query,), (grad,) = pairs_of(every(0, b) * scale), pairs_of(every(3, b))
-        low, sgrad = softmax_grads(dot_nt(key, query) + bias, dot_nt(value, grad), 0)
-        low_ref[b] = low.astype(F32)
-        sg_ref[b] = sgrad.astype(F32)
-
-        def mine_rows(ref):
-            pieces = [
-                ref[b, pl.ds(t * devices + f * bands + band, 1), :]
-                for f in range(frames)
-                for t in range(tokens)
-            ]
-            return jnp.concatenate(pieces, axis=0).astype(BF16)
-
-        (own_query,), (own_grad,) = pairs_of(mine(0, b) * scale), pairs_of(mine(3, b))
-        _, own_sgrad = softmax_grads(
-            dot_nt(own_query, key) + own_bias, dot_nt(own_grad, value), 1
-        )
-        full = dot_nn(own_sgrad, key)
+    halves = range(parts)
+    keys, values = ([every(a, b) for b in halves] for a in (1, 2))
+    queries, grads = ([pairs_of(every(a, b))[0] for b in halves] for a in (0, 3))
+    queries = [query * scale for query in queries]
+    own_queries = [pairs_of(mine(0, b) * scale)[0] for b in halves]
+    own_grads = [pairs_of(mine(3, b))[0] for b in halves]
+    scores = [dot_nt(keys[b], queries[b]) + bias for b in halves]
+    wgrads = [dot_nt(values[b], grads[b]) for b in halves]
+    own_scores = [dot_nt(own_queries[b], keys[b]) + own_bias for b in halves]
+    own_wgrads = [dot_nt(own_grads[b], values[b]) for b in halves]
+    found = [softmax_grads(scores[b], wgrads[b], 0) for b in halves]
+    own_sgrads = [softmax_grads(own_scores[b], own_wgrads[b], 1)[1] for b in halves]
+    for b in halves:
+        low_ref[b], sg_ref[b] = found[b][0].astype(F32), found[b][1].astype(F32)
+
+    def mine_rows(ref, b):
+        pieces = [
+            ref[b, pl.ds(t * devices + f * bands + band, 1), :]
+            for f in range(frames)
+            for t in range(tokens)
+        ]
+        return jnp.concatenate(pieces, axis=0).astype(BF16)
+
+    for b in halves:
+        full = dot_nn(own_sgrads[b], keys[b])
         dq = jnp.where(iota((own, LANES), 1) < HD, full[:own], full[own:]) * scale
-        dk = dot_nn(mine_rows(sg_ref), query)
-        dv = dot_nn(mine_rows(low_ref), grad)
+        dk = dot_nn(mine_rows(sg_ref, b), queries[b])
+        dv = dot_nn(mine_rows(low_ref, b), grads[b])
         for ref, table in ((dq_ref, dq), (dk_ref, dk), (dv_ref, dv)):
             rounded = table.astype(BF16)
             for f in range(frames):
-                ref[f, :, at] = rounded[f * tokens : (f + 1) * tokens]
+                ref[f, :, b * LANES : (b + 1) * LANES] = rounded[f * tokens : (f + 1) * tokens]
 
 
 def vmem():
@@ -338,7 +427,7 @@
     return jax.ShapeDtypeStruct(shape, dtype)
 
 
-def fine_level(carried, gain, fine_q, fine_kv, cotangent, valid_cols):
+def fine_level(carried, gain, valid, fine_q, fine_kv, cotangent):
     bands = lax.axis_size("rows")
     _, rows, cols, width = fine_q.shape
     pixels = rows * cols
@@ -346,37 +435,40 @@
     query = fine_q.reshape(pixels, width)
     key_value = fine_kv.reshape(pixels, 2 * width)
     cot = cotangent.reshape(pixels, width)
-    packed = (3 * radius * cols, 2 * width)
+    one, sums = radius * cols, 16
+    packed = (4 * one + sums, width)
     near, far, grad = pl.pallas_call(
         functools.partial(prep_kernel, cols),
-        in_specs=[vmem()] * 4,
+        in_specs=[vmem()] * 5,
         out_specs=[vmem()] * 3,
         out_shape=[out(packed), out(packed), out((pixels, width))],
         compiler_params=params(),
-    )(gain, query, key_value, cot)
+    )(valid, gain, query, key_value, cot)
     pairs = [(i, i ^ 1) for i in range(bands) if i ^ 1 < bands]
     others = [(i, ((i + 1) ^ 1) - 1) for i in range(1, bands) if ((i + 1) ^ 1) - 1 < bands]
     near = lax.ppermute(near, "rows", pairs)
     far = lax.ppermute(far, "rows", others)
-    outside = (3 * radius * cols, 2 * (radius + 1) * cols)
-    stacked = (2 * width // LANES * pixels, LANES)
+    count = width // LANES
     plan = pl.pallas_call(
         functools.partial(plan_kernel, cols),
         in_specs=[vmem()] * 4,
-        out_specs=[vmem()] * 6,
+        out_specs=[vmem()] * 9,
         out_shape=[
-            out((pixels + 2 * radius * cols, pixels), F32),
-            out(outside, F32),
-            out(outside, F32),
-            out(stacked),
-            out(stacked),
+            out((2 * one, pixels), F32),
+            out((one, LANES), F32),
+            out((one, LANES), F32),
+            out((count, 2 * pixels, LANES)),
+            out((count, 2 * pixels, LANES)),
             out((width, pixels)),
+            out((count, pixels, 2 * pixels), F32),
+            out((count, pixels, 2 * pixels), F32),
+            out((count, 8, 2 * pixels), F32),
         ],
         compiler_params=params(),
-    )(valid_cols.reshape(1, -1), query, key_value, grad)
+    )(valid, query, key_value, grad)
     grads = pl.pallas_call(
         functools.partial(fine_kernel, cols, len(carried)),
-        in_specs=[vmem()] * (9 + len(carried)),
+        in_specs=[vmem()] * (12 + len(carried)),
         out_specs=[hbm()] * (2 + len(carried)),
         out_shape=[out((pixels, width)), out((pixels, 2 * width))]
         + [out(x.shape) for x in carried],
@@ -397,21 +489,26 @@
     tokens, cwidth = coarse_q.shape[-2:]
     head_width = cwidth // frames
     tile = 4 * tokens * head_width // LANES
-    sent, gain = pl.pallas_call(
+    sent, gain, valid = pl.pallas_call(
         functools.partial(send_kernel, cols, bands),
-        in_specs=[smem()] + [hbm()] * 4,
-        out_specs=[vmem()] * 2,
-        out_shape=[out((frames * bands * tile, LANES)), out((1, width), F32)],
+        in_specs=[smem()] + [hbm()] * 5,
+        out_specs=[vmem()] * 3,
+        out_shape=[
+            out((frames * bands * tile, LANES)),
+            out((1, width), F32),
+            out((1, frames), jnp.int32),
+        ],
         scratch_shapes=[
             pltpu.VMEM((rows * cols, width), BF16),
             pltpu.VMEM((8, width), F32),
             pltpu.VMEM((tokens, cwidth), BF16),
             pltpu.VMEM((tokens, 2 * cwidth), BF16),
-            pltpu.SemaphoreType.DMA((7,)),
+            pltpu.SemaphoreType.DMA((8,)),
         ],
         compiler_params=params(),
     )(
         timesteps,
+        in_hbm(valid_cols.reshape(1, -1)),
         in_hbm(cotangent.reshape(rows * cols, width)),
         in_hbm(gain_table),
         in_hbm(coarse_q.reshape(tokens, cwidth)),
@@ -437,8 +534,8 @@
         ],
         compiler_params=params(),
         cost_estimate=pl.CostEstimate(flops=100_000_000_000, bytes_accessed=100_000_000, transcendentals=0),
-    )(valid_cols.reshape(1, -1), held)
-    return outs, gain
+    )(valid, held)
+    return outs, gain, valid
 
 
 def normalize(scores):
@@ -543,14 +640,14 @@
         and frames * bands * tokens <= 128
     )
     operands = (coarse_q, coarse_kv, cotangent, gain_table, timesteps, valid_cols)
-    fine = (fine_q, fine_kv, cotangent, valid_cols)
+    fine = (fine_q, fine_kv, cotangent)
     if direct:
-        carried, gain = coarse_direct(*operands)
-        grad_q, grad_kv, *coarse_grads = fine_level(carried, gain, *fine)
+        carried, gain, valid = coarse_direct(*operands)
+        grad_q, grad_kv, *coarse_grads = fine_level(carried, gain, valid, *fine)
         shape = (frames, 1, tokens, head_width)
         return (grad_q, grad_kv, *(x.reshape(shape) for x in coarse_grads))
     coarse_grads, gain = coarse_gathered(*operands)
-    return (*fine_level([], gain, *fine), *coarse_grads)
+    return (*fine_level([], gain, valid_cols.reshape(1, -1), *fine), *coarse_grads)
 
 
 def solution(mesh):

time: 22 us -> 20.3 us (0.923)
  local copies, waits for them, and re-layouts: 0.67 us -> 0.02 us
  waiting for transfers between devices: 5.04 us -> 4.49 us
  Pallas kernels: 4.79 us -> 4.34 us
    ppermute x1, waiting for transfers between devices: 0.9 us -> 0.01 us  [fine_level(): near = lax.ppermute(near, 'rows', pairs)]
    unnamed x8 -> x6, local copies, waits for them, and re-layouts: 0.67 us -> 0.02 us
    pallas_call x1, Pallas kernels: 1.96 us -> 1.39 us  [fine_level(): pl.pallas_call(functools.partial(fine_kernel, cols, len(carried)), in_spe...]
    all_to_all x1, waiting for transfers between devices: 4.14 us -> 4.48 us  [coarse_direct(): lax.all_to_all(sent.reshape(frames * bands, tile, LANES), ('frames', 'row...]
    pallas_call x1, Pallas kernels: 0.04 us -> 0.35 us  [fine_level(): pl.pallas_call(functools.partial(prep_kernel, cols), in_specs=[vmem()] *...]
  transfers between devices with their start and end apart: 3 -> 3, of which waited for: 2 -> 1; matrix products, arithmetic and copies ran while one was open for 0% -> 0% of each run, Pallas kernels for 5% -> 6%
where the time goes in v4:
time: 20.3 us; the launch traced here: 20 us
  starting transfers between devices  9.8 us (48%)
  waiting for transfers between devices  4.49 us (22%)
  Pallas kernels  4.34 us (21%)
  between operations  1.39 us (7%)
    all_to_all x1, starting transfers between devices, coarse_direct(): lax.all_to_all(sent.reshape(frames * bands, tile, LANES), ('frames', 'row...  7.3 us
    all_to_all x1, waiting for transfers between devices, coarse_direct(): lax.all_to_all(sent.reshape(frames * bands, tile, LANES), ('frames', 'row...  4.48 us
    ppermute x1, starting transfers between devices, fine_level(): near = lax.ppermute(near, 'rows', pairs)  1.84 us
    pallas_call x1, Pallas kernels, coarse_direct(): pl.pallas_call(functools.partial(send_kernel, cols, bands), in_specs=[sme...  1.68 us
    pallas_call x1, Pallas kernels, fine_level(): pl.pallas_call(functools.partial(fine_kernel, cols, len(carried)), in_spe...  1.39 us
    ppermute x1, starting transfers between devices, fine_level(): far = lax.ppermute(far, 'rows', others)  0.66 us
    pallas_call x1, Pallas kernels, coarse_direct(): pl.pallas_call(functools.partial(coarse_kernel, frames, tokens), in_specs...  0.56 us
  transfers between devices with their start and end apart: 3, of which 1 were waited for; matrix products, arithmetic and copies ran while one was open for 0% of the time, Pallas kernels for 6%

profile of v4, /device:TPU:0, one launch (start us, length us, event | category | flops | bytes accessed | tf_op | source)
XLA Modules:
  0.0 20.0 jit_solution(13427231783132878875)
XLA Ops:
  1.3 1.7 %shard_map.119 = (bf16[512,128]{1,0:T(8,128)(2,1)}, f32[1,256]{1,0:T(1,128)S(1)}, s32[1,4]{1,0:T(1,128)S(1)}) custom-call(s32[1]{0:T(128)S(6)} %copy.16.step_ref, s32[1,4]{1,0:T(1,128)} %bitcast.29, bf16[128,256]{1,0:T(8,128)(2,1)} %bitcast.22, f32[1000,256]{1,0:T(8,128)} %gain_hbm.1, bf16[2,1024]{1,0:T(2,128)(2,1)} %bitcast.28, bf16[2,2048]{1,0:T(2,128)(2,1)} %bitcast.27), custom_call_target="tpu_custom_call" | custom-call | tf_op jit(solution)/shard_map/pallas_call | solution.py:492
  3.0 0.0 copy-start
  3.0 0.0 copy-start.1
  3.0 0.0 copy-start.2
  3.0 7.3 %all-to-all-start = ((bf16[32,16,128]{2,1,0:T(8,128)(2,1)}), bf16[32,16,128]{2,1,0:T(8,128)(2,1)S(1)}, u32[]{:S(2)}, u32[]{:S(2)}) async-start(bf16[32,16,128]{2,1,0:T(8,128)(2,1)} %bitcast.6), calls=%async_computation | async-start | bytes 262144 | tf_op jit(solution)/shard_map/all_to_all | solution.py:517
  10.3 0.0 copy-done
  10.3 0.0 copy-done.1
  10.3 0.0 copy-done.2
  10.3 0.3 %shard_map.120 = (bf16[208,256]{1,0:T(8,128)(2,1)S(1)}, bf16[208,256]{1,0:T(8,128)(2,1)S(1)}, bf16[128,256]{1,0:T(8,128)(2,1)S(1)}) custom-call(s32[1,4]{1,0:T(1,128)S(1)} %get-tuple-element.28.valid_ref, f32[1,256]{1,0:T(1,128)S(1)} %get-tuple-element.29.gain_ref, bf16[128,256]{1,0:T(8,128)(2,1)S(1)} %bitcast.24, bf16[128,512]{1,0:T(8,128)(2,1)S(1)} %bitcast.19, ...), custom_call_target="tpu_custom_call" | custom-call | tf_op jit(solution)/shard_map/pallas_call | solution.py:440
  10.7 1.8 %collective-permute-start = (bf16[208,256]{1,0:T(8,128)(2,1)S(1)}, bf16[208,256]{1,0:T(8,128)(2,1)S(1)}, u32[]{:S(2)}, u32[]{:S(2)}) collective-permute-start(bf16[208,256]{1,0:T(8,128)(2,1)S(1)} %get-tuple-element.30), channel_id=1, source_target_pairs={{0,1},{1,0},{2,3},{3,2},{4,5},{5,4},{6,7},{7,6},{8,9},{9,8},{10,11... | collective-permute-start | bytes 319496 | tf_op jit(solution)/shard_map/ppermute | solution.py:449
  12.5 0.7 %collective-permute-start.1 = (bf16[208,256]{1,0:T(8,128)(2,1)S(1)}, bf16[208,256]{1,0:T(8,128)(2,1)S(1)}, u32[]{:S(2)}, u32[]{:S(2)}) collective-permute-start(bf16[208,256]{1,0:T(8,128)(2,1)S(1)} %get-tuple-element.31), channel_id=1, source_target_pairs={{1,2},{2,1},{3,4},{4,3},{5,6},{6,5},{9,10},{10,9},{11,12},{12,11},... | collective-permute-start | bytes 319496 | tf_op jit(solution)/shard_map/ppermute | solution.py:450
  13.2 0.4 %shard_map.121 = (f32[96,128]{1,0:T(8,128)S(1)}, f32[48,128]{1,0:T(8,128)S(1)}, f32[48,128]{1,0:T(8,128)S(1)}, bf16[2,256,128]{2,1,0:T(8,128)(2,1)S(1)}, bf16[2,...) custom-call(s32[1,4]{1,0:T(1,128)S(1)} %get-tuple-element.28.valid_r, ...), custom_call_target="tpu_custom_call" | custom-call | tf_op jit(solution)/shard_map/pallas_call | solution.py:452
  13.6 4.5 %all-to-all-done = bf16[32,16,128]{2,1,0:T(8,128)(2,1)S(1)} async-done(((bf16[32,16,128]{2,1,0:T(8,128)(2,1)}), bf16[32,16,128]{2,1,0:T(8,128)(2,1)S(1)}, u32[]{:S(2)}, u32[]{:S(2)}) %all-to-all-start) | async-done | bytes 131104 | tf_op jit(solution)/shard_map/all_to_all | solution.py:517
  18.1 0.6 %shard_map.122 = (bf16[4,2,256]{2,1,0:T(2,128)(2,1)S(1)}, bf16[4,2,256]{2,1,0:T(2,128)(2,1)S(1)}, bf16[4,2,256]{2,1,0:T(2,128)(2,1)S(1)}) custom-call(s32[1,4]{1,0:T(1,128)S(1)} %get-tuple-element.28.valid_ref, bf16[512,128]{1,0:T(8,128)(2,1)S(1)} %bitcast.26), custom_call_target="tpu_custom_call" | custom-call | flops 99999997952 | bytes 100000000 | tf_op jit(solution)/shard_map/pallas_call | solution.py:525
  18.6 0.0 collective-permute-done.refs_1_
  18.6 0.0 collective-permute-done.1.refs_2_
  18.6 1.4 %shard_map.123 = (bf16[128,256]{1,0:T(8,128)(2,1)}, bf16[128,512]{1,0:T(8,128)(2,1)}, bf16[4,2,256]{2,1,0:T(2,128)(2,1)}, bf16[4,2,256]{2,1,0:T(2,128)(2,1)}, bf16[4,2,256]{2,1,0:T(2,128)(2,1)}) custom-call(bf16[128,512]{1,0:T(8,128)(2,1)S(1)} %bitcast.21, bf16[208,256]{1,0:T(8,128)(2,1)S(1)} %collective-permute-done.refs_1_, ...), custom_call_target="tpu_custom_call" | custom-call | flops 400000000 | bytes 1000000 | tf_op jit(solution)/shard_map/pallas_call | solution.py:469
Async XLA Ops:
  3.0 7.3 %copy-start = (bf16[1,8,16,512]{3,2,1,0:T(8,128)(2,1)S(1)}, bf16[1,8,16,512]{3,2,1,0:T(8,128)(2,1)}, u32[]{:S(2)}) copy-start(bf16[1,8,16,512]{3,2,1,0:T(8,128)(2,1)} %param.9) | copy-start | bytes 393220
  3.0 7.3 %copy-start.1 = (bf16[1,8,16,256]{3,2,1,0:T(8,128)(2,1)S(1)}, bf16[1,8,16,256]{3,2,1,0:T(8,128)(2,1)}, u32[]{:S(2)}) copy-start(bf16[1,8,16,256]{3,2,1,0:T(8,128)(2,1)} %param.12) | copy-start | bytes 196612
  3.0 7.3 %copy-start.2 = (bf16[1,8,16,256]{3,2,1,0:T(8,128)(2,1)S(1)}, bf16[1,8,16,256]{3,2,1,0:T(8,128)(2,1)}, u32[]{:S(2)}) copy-start(bf16[1,8,16,256]{3,2,1,0:T(8,128)(2,1)} %param.8) | copy-start | bytes 196612
  3.0 15.1 %all-to-all-start = ((bf16[32,16,128]{2,1,0:T(8,128)(2,1)}), bf16[32,16,128]{2,1,0:T(8,128)(2,1)S(1)}, u32[]{:S(2)}, u32[]{:S(2)}) async-start(bf16[32,16,128]{2,1,0:T(8,128)(2,1)} %bitcast.6), calls=%async_computation | async-start | bytes 262144 | tf_op jit(solution)/shard_map/all_to_all | solution.py:517
  10.7 7.9 %collective-permute-start = (bf16[208,256]{1,0:T(8,128)(2,1)S(1)}, bf16[208,256]{1,0:T(8,128)(2,1)S(1)}, u32[]{:S(2)}, u32[]{:S(2)}) collective-permute-start(bf16[208,256]{1,0:T(8,128)(2,1)S(1)} %get-tuple-element.30), channel_id=1, source_target_pairs={{0,1},{1,0},{2,3},{3,2},{4,5},{5,4},{6,7},{7,6},{8,9},{9,8},{10,11... | collective-permute-start | bytes 319496 | tf_op jit(solution)/shard_map/ppermute | solution.py:449
  12.5 6.1 %collective-permute-start.1 = (bf16[208,256]{1,0:T(8,128)(2,1)S(1)}, bf16[208,256]{1,0:T(8,128)(2,1)S(1)}, u32[]{:S(2)}, u32[]{:S(2)}) collective-permute-start(bf16[208,256]{1,0:T(8,128)(2,1)S(1)} %get-tuple-element.31), channel_id=1, source_target_pairs={{1,2},{2,1},{3,4},{4,3},{5,6},{6,5},{9,10},{10,9},{11,12},{12,11},... | collective-permute-start | bytes 319496 | tf_op jit(solution)/shard_map/ppermute | solution.py:450

commit v5 on v4

--- a/solution.py
+++ b/solution.py
@@ -60,15 +60,16 @@
     eight = eight_ref.shape[0]
     first = pl.multiple_of(step // eight * eight, eight)
     gain_copy = pltpu.make_async_copy(gain_hbm.at[pl.ds(first, eight)], eight_ref, sems.at[0])
-    gain_copy.start()
     copies = [
         pltpu.make_async_copy(source, target, sems.at[1 + at])
         for at, (source, target) in enumerate(
             tuple((cot_hbm.at[pl.ds(r, 32)], cot_ref.at[pl.ds(r, 32)]) for r in range(0, 128, 32)) + ((cq_hbm, cq_ref), (ckv_hbm, ckv_ref), (valid_hbm, valid_ref))
         )
     ]
-    for copy in copies:
+    for copy in copies[:-1]:
         copy.start()
+    gain_copy.start()
+    copies[-1].start()
     pixels, width = cot_ref.shape
     tokens, cwidth = cq_ref.shape
     half = POOL // 2
@@ -111,14 +112,12 @@
     )
 
 
-def window_bias(shape, cols, valid, key_row, lane_rows, query_row, present=None):
+def window_bias(shape, cols, valid, lane_rows, query_row):
     radius = KERNEL // 2
     place, lane = iota(shape, 0), iota(shape, 1)
-    krow, kcol = key_row(place // cols), place % cols
+    krow, kcol = place // cols, place % cols
     qrow, qcol = lane // cols % lane_rows + query_row, lane % cols
     seen = (jnp.abs(krow - qrow) <= radius) & (jnp.abs(kcol - qcol) <= radius) & (kcol < valid)
-    if present is not None:
-        seen = seen & present(krow)
     seen = seen | ((krow == qrow) & (kcol == qcol))
     return jnp.where(seen, 0.0, NEGATIVE)
 
@@ -150,193 +149,245 @@
     return parts
 
 
-def prep_kernel(cols, valid_ref, gain_ref, q_ref, kv_ref, cot_ref, near_ref, far_ref, grad_ref):
+def prep_kernel(
+    cols, valid_ref, gain_ref, q_ref, kv_ref, cot_ref,
+    near_ref, far_ref, grad_ref, raised_ref, wgrad_ref, sums_ref, queries_ref, grads_ref,
+):
     radius = KERNEL // 2
     pixels, width = q_ref.shape
-    rows = pixels // cols
     one, two = radius * cols, 2 * radius * cols
     scale = 1.0 / math.sqrt(HD)
     even = lax.axis_index("rows") % 2 == 0
     valid = valid_here(valid_ref)
     grad_ref[...] = (gain_ref[...] * cot_ref[...].astype(F32)).astype(BF16)
     pad = jnp.zeros((cols, width), BF16)
-
-    sides = []
-    for lo, key_lo, query_row in ((0, 0, 0), (pixels - one, pixels - two, radius)):
-        bias = window_bias((two, LANES), cols, valid, lambda at: at, radius + 1, query_row)
+    pairs = range(width // LANES)
+    scores = {}
+    for side in range(2):
+        lo, key_lo = side * (pixels - one), side * (pixels - two)
+        bias = window_bias((two, LANES), cols, valid, radius + 1, side * radius)
         query = pairs_of(jnp.concatenate([q_ref[lo : lo + one, :] * scale, pad], axis=0))
         grad = pairs_of(jnp.concatenate([grad_ref[lo : lo + one, :], pad], axis=0))
-        products = []
-        for p in range(width // LANES):
+        for p in pairs:
             at = p * LANES
+            queries_ref[side, p], grads_ref[side, p] = query[p], grad[p]
             keys = kv_ref[key_lo : key_lo + two, at : at + LANES]
             values = kv_ref[key_lo : key_lo + two, width + at : width + at + LANES]
-            products.append((dot_nt(keys, query[p]) + bias, dot_nt(values, grad[p])))
-        sides.append(products)
-
-    def sums(products):
+            scores[side, p] = dot_nt(keys, query[p]) + bias, dot_nt(values, grad[p])
+    found = []
+    for side in range(2):
         tiles = []
-        for scores, wgrad in products:
-            top, _, total, dot = partial_sums(scores, wgrad)
-            found = [part for row in (top, total, dot) for part in in_parts(row)]
-            found.append(jnp.zeros((16 - len(found), LANES), F32))
-            tiles.append(jnp.concatenate(found, axis=0))
-        return jnp.concatenate(tiles, axis=1).astype(BF16)
-
-    upper, lower = (sums(products) for products in sides)
-
-    def pack(target, lo, found):
+        for p in pairs:
+            score, wgrad = scores[side, p]
+            top, raised, total, dot = partial_sums(score, wgrad)
+            raised_ref[side, p], wgrad_ref[side, p] = raised, wgrad
+            for row, value in enumerate((top, total, dot)):
+                sums_ref[side, p, row : row + 1, :] = value
+            parts = [part for row in (top, total, dot) for part in in_parts(row)]
+            parts.append(jnp.zeros((16 - len(parts), LANES), F32))
+            tiles.append(jnp.concatenate(parts, axis=0))
+        found.append(jnp.concatenate(tiles, axis=1).astype(BF16))
+
+    def pack(target, side):
+        lo = side * (pixels - one)
         parts = (kv_ref[lo : lo + one, :width], kv_ref[lo : lo + one, width:])
         parts += (q_ref[lo : lo + one, :], grad_ref[lo : lo + one, :])
         for at, part in enumerate(parts):
             target[at * one : (at + 1) * one, :] = part
-        target[len(parts) * one :, :] = found
+        target[len(parts) * one :, :] = found[side]
 
     @pl.when(even)
     def _():
-        pack(near_ref, pixels - one, lower)
-        pack(far_ref, 0, upper)
+        pack(near_ref, 1)
+        pack(far_ref, 0)
 
     @pl.when(jnp.logical_not(even))
     def _():
-        pack(near_ref, 0, upper)
-        pack(far_ref, pixels - one, lower)
+        pack(near_ref, 0)
+        pack(far_ref, 1)
 
 
 def plan_kernel(
-    cols, valid_ref, q_ref, kv_ref, grad_ref,
-    beside_ref, above_ref, below_ref, queries_ref, grads_ref, keys_t_ref, raised_ref, wgrad_ref, sums_ref,
+    cols, valid_ref, q_ref, kv_ref, grad_ref, own_bias_ref, halo_bias_ref, dq_ref, total_ref
 ):
     radius = KERNEL // 2
     pixels, width = q_ref.shape
     rows = pixels // cols
+    one, middle = radius * cols, pixels - 2 * radius * cols
     scale = 1.0 / math.sqrt(HD)
     band = lax.axis_index("rows")
-    first, last = band == 0, band == lax.axis_size("rows") - 1
     valid = valid_here(valid_ref)
-
-    def present(krow):
-        return ((krow >= 0) | jnp.logical_not(first)) & ((krow < rows) | jnp.logical_not(last))
-
-    beside_ref[...] = window_bias(
-        beside_ref.shape, cols, valid,
-        lambda at: jnp.where(at < radius, at - radius, at - radius + rows), rows, 0, present,
-    )
-    above_ref[...] = window_bias(
-        above_ref.shape, cols, valid, lambda at: at, radius + 1, -radius
-    )
-    below_ref[...] = window_bias(
-        below_ref.shape, cols, valid, lambda at: at + rows - radius, radius + 1, rows
-    )
-    bias = window_bias((pixels, pixels), cols, valid, lambda at: at, rows, 0)
-    bias = jnp.concatenate([bias, bias], axis=1)
-    keys_t_ref[...] = kv_ref[:, :width].T
-    for p, (query, grad) in enumerate(zip(pairs_of(q_ref[...] * scale), pairs_of(grad_ref[...]))):
-        at = p * LANES
-        queries_ref[p], grads_ref[p] = query, grad
-        wgrad = dot_nt(kv_ref[:, width + at : width + at + LANES], grad)
-        top, raised, total, dot = partial_sums(
-            dot_nt(kv_ref[:, at : at + LANES], query) + bias, wgrad
+    shape = own_bias_ref.shape[1:]
+    place, lane = iota(shape, 0), iota(shape, 1)
+    kcol, qcol = place % cols, lane % cols
+    gap = place // cols - lane // cols % (radius + 1)
+    close = (jnp.abs(kcol - qcol) <= radius) & (kcol < valid)
+    for side, missing in enumerate((band == 0, band == lax.axis_size("rows") - 1)):
+        own = gap if side == 0 else -gap
+        seen = close & (own >= 0) & jnp.logical_not(missing)
+        own_bias_ref[side] = jnp.where(seen, 0.0, NEGATIVE)
+        halo_bias_ref[side] = jnp.where(close & (own <= 0), 0.0, NEGATIVE)
+    head = iota((middle, width), 1) // HD
+
+    def by_head(table):
+        zero = jnp.zeros_like(table)
+        return jnp.concatenate(
+            [jnp.where(head == h, table, zero) for h in range(width // HD)], axis=0
         )
-        raised_ref[p], wgrad_ref[p] = raised, wgrad
-        for row, value in enumerate((top, total, dot)):
-            sums_ref[p, row : row + 1, :] = value
-
-
-def fine_kernel(cols, carried, *refs):
-    (kv_ref, near_ref, far_ref, beside_ref, above_ref, below_ref, queries_ref, grads_ref) = refs[:8]
-    (keys_t_ref, raised_ref, wgrad_ref, sums_ref) = refs[8:12]
-    outs = refs[12 + carried : 14 + 2 * carried]
-    dq_ref, dkv_ref, sems = refs[14 + 2 * carried :]
-    copies = [
-        pltpu.make_async_copy(source, target, sems.at[2 + at])
-        for at, (source, target) in enumerate(zip(refs[12 : 12 + carried], outs[2:]))
-    ]
-    for copy in copies:
-        copy.start()
+
+    query = by_head(q_ref[one : one + middle, :] * scale)
+    grad = by_head(grad_ref[one : one + middle, :])
+    keys, values = kv_ref[:, :width], kv_ref[:, width:]
+    bias = window_bias((pixels, query.shape[0]), cols, valid, middle // cols, radius)
+    low, sgrad = softmax_grads(dot_nt(keys, query) + bias, dot_nt(values, grad), 0)
+    full = dot_nn(sgrad.T, keys)
+    dq = sum(
+        jnp.where(head == h, full[h * middle : (h + 1) * middle], 0.0) for h in range(width // HD)
+    )
+    dq_ref[...] = (dq * scale).astype(BF16)
+    total_ref[:, :width] = dot_nn(sgrad, query)
+    total_ref[:, width:] = dot_nn(low, grad)
+
+
+def side_rows(cols, pixels, side):
+    two = 2 * (KERNEL // 2) * cols
+    window = pl.ds(pl.multiple_of(side * (pixels - two), cols), two)
+    others = pl.ds(pl.multiple_of((1 - side) * two, cols), pixels - two)
+    return window, others
+
+
+def side_terms(cols, side, refs, meanwhile=lambda: None, later=lambda: None):
+    (kv_ref, halo_ref, own_bias_ref, halo_bias_ref, raised_ref, wgrad_ref, sums_ref) = refs[:7]
+    queries_ref, grads_ref = refs[7:]
     radius = KERNEL // 2
-    pixels, width = dq_ref.shape
-    one = radius * cols
+    pixels, width = kv_ref.shape[0], kv_ref.shape[1] // 2
+    one, two = radius * cols, 2 * radius * cols
     scale = 1.0 / math.sqrt(HD)
-    even = lax.axis_index("rows") % 2 == 0
-
-    def received(at):
-        rows_at = slice(at * one, (at + 1) * one) if at < 4 else slice(at * one, None)
-        near, far = near_ref[rows_at, :], far_ref[rows_at, :]
-        return jnp.where(even, far, near), jnp.where(even, near, far)
+    window, _ = side_rows(cols, pixels, side)
+    border = pl.ds(pl.multiple_of(side * (pixels - one), cols), one)
+    halo_keys, halo_values = halo_ref[:one, :], halo_ref[one:two, :]
+    pad = jnp.zeros((cols, width), BF16)
 
     def joined(table):
         return jnp.concatenate(table, axis=0)
 
-    beside_keys, beside_values = joined(received(0)), joined(received(1))
-    beside_t = beside_keys.T
-    pad = jnp.zeros((cols, width), BF16)
-    rest = jnp.zeros((pixels - one, LANES), BF16)
-    side_lo = (0, pixels - one)
-    side_query = [pairs_of(joined([t * scale, pad])) for t in received(2)]
-    side_grad = [pairs_of(joined([t, pad])) for t in received(3)]
-    side_sums = [t.astype(F32) for t in received(4)]
-    beside_bias = jnp.concatenate([beside_ref[...], beside_ref[...]], axis=1)
+    def at_border(table):
+        table, zero = table.astype(BF16), jnp.zeros(table.shape, BF16)
+        return joined([jnp.where(side == 0, table, zero), jnp.where(side == 0, zero, table)])
+
+    halo_query = pairs_of(joined([halo_ref[two : two + one, :] * scale, pad]))
+    halo_grad = pairs_of(joined([halo_ref[two + one : 2 * two, :], pad]))
+    halo_sums = halo_ref[2 * two :, :].astype(F32)
     pairs = range(width // LANES)
     ats = [slice(p * LANES, (p + 1) * LANES) for p in pairs]
     value_ats = [slice(width + p * LANES, width + (p + 1) * LANES) for p in pairs]
-    sides = [(side, p) for side in range(2) for p in pairs]
-    beside_scores = [dot_nt(beside_keys[:, ats[p]], queries_ref[p]) + beside_bias for p in pairs]
-    beside_wgrad = [dot_nt(beside_values[:, ats[p]], grads_ref[p]) for p in pairs]
-    side_scores, side_wgrad = {}, {}
-    for side, p in sides:
-        keys_at = slice(side_lo[side], side_lo[side] + one)
-        bias_ref = (above_ref, below_ref)[side]
-        side_scores[side, p] = (
-            dot_nt(kv_ref[keys_at, ats[p]], side_query[side][p]) + bias_ref[...]
-        )
-        side_wgrad[side, p] = dot_nt(kv_ref[keys_at, value_ats[p]], side_grad[side][p])
-    lows, sgrads, beside_sgrads = {}, {}, {}
+    own_bias, halo_bias = own_bias_ref[side], halo_bias_ref[side]
+    own_scores = [dot_nt(halo_keys[:, ats[p]], queries_ref[side, p]) + own_bias for p in pairs]
+    own_wgrad = [dot_nt(halo_values[:, ats[p]], grads_ref[side, p]) for p in pairs]
+    halo_scores = [dot_nt(kv_ref[border, ats[p]], halo_query[p]) + halo_bias for p in pairs]
+    halo_wgrad = [dot_nt(kv_ref[border, value_ats[p]], halo_grad[p]) for p in pairs]
+    meanwhile()
+    lows, sgrads, beyond, halo_lows, halo_sgrads = [], [], [], [], []
     for p in pairs:
-        factor, beside_weights, row_dot = completed(
-            tuple(sums_ref[p, row : row + 1, :] for row in range(3)),
-            beside_scores[p],
-            beside_wgrad[p],
-        )
-        beside_sgrads[p] = (beside_weights * (beside_wgrad[p] - row_dot)).astype(BF16)
-        weights = raised_ref[p] * factor
-        lows[p] = weights.astype(BF16)
-        sgrads[p] = (weights * (wgrad_ref[p] - row_dot)).astype(BF16)
-    for side, p in sides:
-        found = side_sums[side][:, ats[p]]
+        kept = tuple(sums_ref[side, p, row : row + 1, :] for row in range(3))
+        factor, weights, row_dot = completed(kept, own_scores[p], own_wgrad[p])
+        beyond.append((weights * (own_wgrad[p] - row_dot)).astype(BF16))
+        weights = raised_ref[side, p] * factor
+        lows.append(weights.astype(BF16))
+        sgrads.append((weights * (wgrad_ref[side, p] - row_dot)).astype(BF16))
+        found = halo_sums[:, ats[p]]
         kept = tuple(
             found[row : row + 1] + found[row + 1 : row + 2] + found[row + 2 : row + 3]
             for row in (0, 3, 6)
         )
-        _, weights, row_dot = completed(kept, side_scores[side, p], side_wgrad[side, p])
-        order = slice(None, None, -1 if side else 1)
-        lows[side, p] = joined([weights.astype(BF16), rest][order])
-        sgrad = (weights * (side_wgrad[side, p] - row_dot)).astype(BF16)
-        sgrads[side, p] = joined([sgrad, rest][order])
+        _, weights, row_dot = completed(kept, halo_scores[p], halo_wgrad[p])
+        halo_lows.append(at_border(weights))
+        halo_sgrads.append(at_border(weights * (halo_wgrad[p] - row_dot)))
+    later()
+    dq, dk, dv = [], [], []
     for p in pairs:
-        dq_t = dot_nn(keys_t_ref[ats[p], :], sgrads[p]) + dot_nn(beside_t[ats[p]], beside_sgrads[p])
-        dq_t = joined([dq_t[:HD, :pixels], dq_t[HD:, pixels:]])
-        dq_ref[:, ats[p]] = (dq_t * scale).astype(BF16).T
-    for p in pairs:
-        dkv_ref[:, ats[p]] = dot_nn(
-            jnp.concatenate([sgrads[p], sgrads[0, p], sgrads[1, p]], axis=1),
-            joined([queries_ref[p], side_query[0][p], side_query[1][p]]),
-        ).astype(BF16)
-        dkv_ref[:, value_ats[p]] = dot_nn(
-            jnp.concatenate([lows[p], lows[0, p], lows[1, p]], axis=1),
-            joined([grads_ref[p], side_grad[0][p], side_grad[1][p]]),
-        ).astype(BF16)
-    copies += [
+        dk.append(
+            dot_nn(
+                jnp.concatenate([sgrads[p], halo_sgrads[p]], axis=1),
+                joined([queries_ref[side, p], halo_query[p]]),
+            )
+        )
+        dv.append(
+            dot_nn(
+                jnp.concatenate([lows[p], halo_lows[p]], axis=1),
+                joined([grads_ref[side, p], halo_grad[p]]),
+            )
+        )
+        full = dot_nn(
+            joined([sgrads[p], beyond[p]]).T, joined([kv_ref[window, ats[p]], halo_keys[:, ats[p]]])
+        )
+        first = iota((one, LANES), 1) < HD
+        dq.append(jnp.where(first, full[:one], full[one + cols : two + cols]) * scale)
+    return jnp.concatenate(dq, axis=1).astype(BF16), dk + dv
+
+
+def side_border(cols, pixels, side):
+    one = KERNEL // 2 * cols
+    return pl.ds(pl.multiple_of(side * (pixels - one), cols), one)
+
+
+def near_kernel(cols, middle_ref, total_in, *refs, hooks=()):
+    *refs, dq_ref, total_ref = refs
+    side = 1 - lax.axis_index("rows") % 2
+    pixels = total_ref.shape[0]
+    one = KERNEL // 2 * cols
+    window, others = side_rows(cols, pixels, side)
+    dq, terms = side_terms(cols, side, refs, *hooks)
+    dq_ref[one : pixels - one, :] = middle_ref[...]
+    dq_ref[side_border(cols, pixels, side), :] = dq
+    total_ref[others, :] = total_in[others, :]
+    for at, term in enumerate(terms):
+        lanes = slice(at * LANES, (at + 1) * LANES)
+        total_ref[window, lanes] = total_in[window, lanes] + term
+
+
+def far_kernel(cols, carried, *refs):
+    dq_in, total_in = refs[:2]
+    given = refs[2 : 2 + carried]
+    refs = refs[2 + carried :]
+    outs = refs[9 : 11 + carried]
+    dq_ref, dkv_ref, sems = refs[11 + carried :]
+    side = lax.axis_index("rows") % 2
+    pixels = total_in.shape[0]
+    one = KERNEL // 2 * cols
+    window, others = side_rows(cols, pixels, side)
+    near_border = side_border(cols, pixels, 1 - side)
+    early = [
+        (dkv_ref.at[others], outs[1].at[others]),
+        *zip(given, outs[2:]),
+    ]
+    late = [(dq_ref, outs[0]), (dkv_ref.at[window], outs[1].at[window])]
+    copies = [
         pltpu.make_async_copy(source, target, sems.at[at])
-        for at, (source, target) in enumerate(((dq_ref, outs[0]), (dkv_ref, outs[1])))
+        for at, (source, target) in enumerate(early + late)
     ]
-    for copy in copies[carried:]:
+
+    def meanwhile():
+        for copy in copies[: len(early)]:
+            copy.start()
+
+    dkv_ref[others, :] = total_in[others, :].astype(BF16)
+    dq, terms = side_terms(cols, side, refs[:9], meanwhile)
+    dq_ref[one : pixels - one, :] = dq_in[one : pixels - one, :]
+    dq_ref[near_border, :] = dq_in[near_border, :]
+    dq_ref[side_border(cols, pixels, side), :] = dq
+    for at, term in enumerate(terms):
+        lanes = slice(at * LANES, (at + 1) * LANES)
+        dkv_ref[window, lanes] = (total_in[window, lanes] + term).astype(BF16)
+    for copy in copies[len(early) :]:
         copy.start()
     for copy in copies:
         copy.wait()
 
 
-def coarse_kernel(frames, tokens, valid_ref, x_ref, dq_ref, dk_ref, dv_ref, wide, low_ref, sg_ref):
+def coarse_stages(
+    frames, tokens, valid_ref, x_ref, dq_ref, dk_ref, dv_ref, wide, low_ref, sg_ref
+):
     bands = lax.axis_size("rows")
     width = dq_ref.shape[-1]
     parts = width // LANES
@@ -379,10 +430,13 @@
     wgrads = [dot_nt(values[b], grads[b]) for b in halves]
     own_scores = [dot_nt(own_queries[b], keys[b]) + own_bias for b in halves]
     own_wgrads = [dot_nt(own_grads[b], values[b]) for b in halves]
+    yield
     found = [softmax_grads(scores[b], wgrads[b], 0) for b in halves]
     own_sgrads = [softmax_grads(own_scores[b], own_wgrads[b], 1)[1] for b in halves]
     for b in halves:
         low_ref[b], sg_ref[b] = found[b][0].astype(F32), found[b][1].astype(F32)
+
+    yield
 
     def mine_rows(ref, b):
         pieces = [
@@ -401,6 +455,15 @@
             rounded = table.astype(BF16)
             for f in range(frames):
                 ref[f, :, b * LANES : (b + 1) * LANES] = rounded[f * tokens : (f + 1) * tokens]
+    yield
+
+
+def near_and_coarse_kernel(cols, frames, tokens, *refs):
+    coarse_in, near_in = refs[:2], refs[2:13]
+    coarse_out, near_out, scratch = refs[13:16], refs[16:18], refs[18:]
+    stages = coarse_stages(frames, tokens, *coarse_in, *coarse_out, *scratch)
+    next(stages)
+    near_kernel(cols, *near_in, *near_out, hooks=[lambda: next(stages)] * 2)
 
 
 def vmem():
@@ -427,7 +490,7 @@
     return jax.ShapeDtypeStruct(shape, dtype)
 
 
-def fine_level(carried, gain, valid, fine_q, fine_kv, cotangent):
+def fine_level(coarse, gain, valid, fine_q, fine_kv, cotangent):
     bands = lax.axis_size("rows")
     _, rows, cols, width = fine_q.shape
     pixels = rows * cols
@@ -437,49 +500,79 @@
     cot = cotangent.reshape(pixels, width)
     one, sums = radius * cols, 16
     packed = (4 * one + sums, width)
-    near, far, grad = pl.pallas_call(
+    count, stack = width // LANES, 2 * (one + cols)
+    near, far, grad, *kept = pl.pallas_call(
         functools.partial(prep_kernel, cols),
         in_specs=[vmem()] * 5,
-        out_specs=[vmem()] * 3,
-        out_shape=[out(packed), out(packed), out((pixels, width))],
+        out_specs=[vmem()] * 8,
+        out_shape=[
+            out(packed),
+            out(packed),
+            out((pixels, width)),
+            out((2, count, 2 * one, LANES), F32),
+            out((2, count, 2 * one, LANES), F32),
+            out((2, count, 8, LANES), F32),
+            out((2, count, stack, LANES)),
+            out((2, count, stack, LANES)),
+        ],
         compiler_params=params(),
     )(valid, gain, query, key_value, cot)
     pairs = [(i, i ^ 1) for i in range(bands) if i ^ 1 < bands]
     others = [(i, ((i + 1) ^ 1) - 1) for i in range(1, bands) if ((i + 1) ^ 1) - 1 < bands]
     near = lax.ppermute(near, "rows", pairs)
     far = lax.ppermute(far, "rows", others)
-    count = width // LANES
-    plan = pl.pallas_call(
+    *biases, middle_q, total = pl.pallas_call(
         functools.partial(plan_kernel, cols),
         in_specs=[vmem()] * 4,
-        out_specs=[vmem()] * 9,
+        out_specs=[vmem()] * 4,
         out_shape=[
-            out((2 * one, pixels), F32),
-            out((one, LANES), F32),
-            out((one, LANES), F32),
-            out((count, 2 * pixels, LANES)),
-            out((count, 2 * pixels, LANES)),
-            out((width, pixels)),
-            out((count, pixels, 2 * pixels), F32),
-            out((count, pixels, 2 * pixels), F32),
-            out((count, 8, 2 * pixels), F32),
+            out((2, one, LANES), F32),
+            out((2, one, LANES), F32),
+            out((pixels - 2 * one, width)),
+            out((pixels, 2 * width), F32),
         ],
         compiler_params=params(),
     )(valid, query, key_value, grad)
+    near_in = (middle_q, total, key_value, near, *biases, *kept)
+    near_out = [out((pixels, width)), out((pixels, 2 * width), F32)]
+    if coarse is None:
+        dq, total = pl.pallas_call(
+            functools.partial(near_kernel, cols),
+            in_specs=[vmem()] * len(near_in),
+            out_specs=[vmem()] * 2,
+            out_shape=near_out,
+            compiler_params=params(),
+        )(*near_in)
+        carried = []
+    else:
+        held, frames, tokens, head_width = coarse
+        all_tokens = frames * bands * tokens
+        by_query = pltpu.VMEM((head_width // LANES, all_tokens, 2 * all_tokens), F32)
+        *carried, dq, total = pl.pallas_call(
+            functools.partial(near_and_coarse_kernel, cols, frames, tokens),
+            in_specs=[vmem()] * (2 + len(near_in)),
+            out_specs=[vmem()] * 5,
+            out_shape=[out((frames, tokens, head_width))] * 3 + near_out,
+            scratch_shapes=[pltpu.VMEM(held.shape, F32), by_query, by_query],
+            compiler_params=params(),
+            cost_estimate=pl.CostEstimate(
+                flops=100_000_000_000, bytes_accessed=100_000_000, transcendentals=0
+            ),
+        )(valid, held, *near_in)
     grads = pl.pallas_call(
-        functools.partial(fine_kernel, cols, len(carried)),
-        in_specs=[vmem()] * (12 + len(carried)),
+        functools.partial(far_kernel, cols, len(carried)),
+        in_specs=[vmem()] * (11 + len(carried)),
         out_specs=[hbm()] * (2 + len(carried)),
         out_shape=[out((pixels, width)), out((pixels, 2 * width))]
         + [out(x.shape) for x in carried],
         scratch_shapes=[
             pltpu.VMEM((pixels, width), BF16),
             pltpu.VMEM((pixels, 2 * width), BF16),
-            pltpu.SemaphoreType.DMA((2 + len(carried),)),
+            pltpu.SemaphoreType.DMA((3 + len(carried),)),
         ],
         compiler_params=params(),
         cost_estimate=pl.CostEstimate(flops=400_000_000, bytes_accessed=1_000_000, transcendentals=300_000),
-    )(key_value, near, far, *plan, *carried)
+    )(dq, total, *carried, key_value, far, *biases, *kept)
     return (grads[0].reshape(fine_q.shape), grads[1].reshape(fine_kv.shape), *grads[2:])
 
 
@@ -521,21 +614,7 @@
         concat_axis=0,
         tiled=True,
     ).reshape(frames * bands * tile, LANES)
-    count = frames * bands * tokens
-    outs = pl.pallas_call(
-        functools.partial(coarse_kernel, frames, tokens),
-        in_specs=[vmem()] * 2,
-        out_specs=[vmem()] * 3,
-        out_shape=[out((frames, tokens, head_width))] * 3,
-        scratch_shapes=[
-            pltpu.VMEM(held.shape, F32),
-            pltpu.VMEM((head_width // LANES, count, 2 * count), F32),
-            pltpu.VMEM((head_width // LANES, count, 2 * count), F32),
-        ],
-        compiler_params=params(),
-        cost_estimate=pl.CostEstimate(flops=100_000_000_000, bytes_accessed=100_000_000, transcendentals=0),
-    )(valid, held)
-    return outs, gain, valid
+    return (held, frames, tokens, head_width), gain, valid
 
 
 def normalize(scores):
@@ -642,12 +721,13 @@
     operands = (coarse_q, coarse_kv, cotangent, gain_table, timesteps, valid_cols)
     fine = (fine_q, fine_kv, cotangent)
     if direct:
-        carried, gain, valid = coarse_direct(*operands)
-        grad_q, grad_kv, *coarse_grads = fine_level(carried, gain, valid, *fine)
+        coarse, gain, valid = coarse_direct(*operands)
+        grad_q, grad_kv, *coarse_grads = fine_level(coarse, gain, valid, *fine)
         shape = (frames, 1, tokens, head_width)
         return (grad_q, grad_kv, *(x.reshape(shape) for x in coarse_grads))
     coarse_grads, gain = coarse_gathered(*operands)
-    return (*fine_level([], gain, valid_cols.reshape(1, -1), *fine), *coarse_grads)
+    valid = valid_cols.reshape(1, -1)
+    return (*fine_level(None, gain, valid, *fine), *coarse_grads)
 
 
 def solution(mesh):

time: 20.3 us -> 20.4 us (level)
    all_to_all x1, waiting for transfers between devices: 4.48 us -> 1.1 us  [coarse_direct(): lax.all_to_all(sent.reshape(frames * bands, tile, LANES), ('frames', 'row...]
    ppermute x1, waiting for transfers between devices: 0.01 us -> 3.25 us  [fine_level(): near = lax.ppermute(near, 'rows', pairs)]
  transfers between devices with their start and end apart: 3 -> 3, of which waited for: 1 -> 2; matrix products, arithmetic and copies ran while one was open for 0% -> 0% of each run, Pallas kernels for 6% -> 8%
where the time goes in v5:
time: 20.4 us; the launch traced here: 20 us
  starting transfers between devices  9.8 us (48%)
  Pallas kernels  4.51 us (22%)
  waiting for transfers between devices  4.35 us (21%)
  between operations  1.37 us (7%)
    all_to_all x1, starting transfers between devices, coarse_direct(): lax.all_to_all(sent.reshape(frames * bands, tile, LANES), ('frames', 'row...  7.3 us
    ppermute x1, waiting for transfers between devices, fine_level(): near = lax.ppermute(near, 'rows', pairs)  3.25 us
    ppermute x1, starting transfers between devices, fine_level(): near = lax.ppermute(near, 'rows', pairs)  1.84 us
    pallas_call x1, Pallas kernels, coarse_direct(): pl.pallas_call(functools.partial(send_kernel, cols, bands), in_specs=[sme...  1.66 us
    pallas_call x1, Pallas kernels, fine_level(): pl.pallas_call(functools.partial(far_kernel, cols, len(carried)), in_spec...  1.25 us
    all_to_all x1, waiting for transfers between devices, coarse_direct(): lax.all_to_all(sent.reshape(frames * bands, tile, LANES), ('frames', 'row...  1.1 us
    pallas_call x1, Pallas kernels, fine_level(): pl.pallas_call(functools.partial(near_and_coarse_kernel, cols, frames, to...  0.75 us
    ppermute x1, starting transfers between devices, fine_level(): far = lax.ppermute(far, 'rows', others)  0.66 us
  transfers between devices with their start and end apart: 3, of which 2 were waited for; matrix products, arithmetic and copies ran while one was open for 0% of the time, Pallas kernels for 8%

profile of v5, /device:TPU:0, one launch (start us, length us, event | category | flops | bytes accessed | tf_op | source)
XLA Modules:
  0.0 20.0 jit_solution(17122386768846418101)
XLA Ops:
  1.3 1.7 %shard_map.119 = (bf16[512,128]{1,0:T(8,128)(2,1)}, f32[1,256]{1,0:T(1,128)S(1)}, s32[1,4]{1,0:T(1,128)S(1)}) custom-call(s32[1]{0:T(128)S(6)} %copy.16.step_ref, s32[1,4]{1,0:T(1,128)} %bitcast.30, bf16[128,256]{1,0:T(8,128)(2,1)} %bitcast.23, f32[1000,256]{1,0:T(8,128)} %gain_hbm.1, bf16[2,1024]{1,0:T(2,128)(2,1)} %bitcast.29, bf16[2,2048]{1,0:T(2,128)(2,1)} %bitcast.28), custom_call_target="tpu_custom_call" | custom-call | tf_op jit(solution)/shard_map/pallas_call | solution.py:585
  2.9 0.0 copy-start
  3.0 0.0 copy-start.1
  3.0 0.0 copy-start.2
  3.0 7.3 %all-to-all-start = ((bf16[32,16,128]{2,1,0:T(8,128)(2,1)}), bf16[32,16,128]{2,1,0:T(8,128)(2,1)S(1)}, u32[]{:S(2)}, u32[]{:S(2)}) async-start(bf16[32,16,128]{2,1,0:T(8,128)(2,1)} %bitcast.4), calls=%async_computation | async-start | bytes 262144 | tf_op jit(solution)/shard_map/all_to_all | solution.py:610
  10.3 0.0 copy-done
  10.3 0.0 copy-done.1
  10.3 0.0 copy-done.2
  10.3 0.4 %shard_map.120 = (bf16[208,256]{1,0:T(8,128)(2,1)S(1)}, bf16[208,256]{1,0:T(8,128)(2,1)S(1)}, bf16[128,256]{1,0:T(8,128)(2,1)S(1)}, f32[2,2,96,128]{3,2,1,0:T(8,...) custom-call(s32[1,4]{1,0:T(1,128)S(1)} %get-tuple-element.30.valid_r, ...), custom_call_target="tpu_custom_call" | custom-call | tf_op jit(solution)/shard_map/pallas_call | solution.py:504
  10.7 1.8 %collective-permute-start = (bf16[208,256]{1,0:T(8,128)(2,1)S(1)}, bf16[208,256]{1,0:T(8,128)(2,1)S(1)}, u32[]{:S(2)}, u32[]{:S(2)}) collective-permute-start(bf16[208,256]{1,0:T(8,128)(2,1)S(1)} %get-tuple-element.36), channel_id=1, source_target_pairs={{0,1},{1,0},{2,3},{3,2},{4,5},{5,4},{6,7},{7,6},{8,9},{9,8},{10,11... | collective-permute-start | bytes 319496 | tf_op jit(solution)/shard_map/ppermute | solution.py:522
  12.5 0.7 %collective-permute-start.1 = (bf16[208,256]{1,0:T(8,128)(2,1)S(1)}, bf16[208,256]{1,0:T(8,128)(2,1)S(1)}, u32[]{:S(2)}, u32[]{:S(2)}) collective-permute-start(bf16[208,256]{1,0:T(8,128)(2,1)S(1)} %get-tuple-element.49), channel_id=1, source_target_pairs={{1,2},{2,1},{3,4},{4,3},{5,6},{6,5},{9,10},{10,9},{11,12},{12,11},... | collective-permute-start | bytes 319496 | tf_op jit(solution)/shard_map/ppermute | solution.py:523
  13.2 0.5 %shard_map.121 = (f32[2,48,128]{2,1,0:T(8,128)S(1)}, f32[2,48,128]{2,1,0:T(8,128)S(1)}, bf16[32,256]{1,0:T(8,128)(2,1)S(1)}, f32[128,512]{1,0:T(8,128)S(1)}) custom-call(s32[1,4]{1,0:T(1,128)S(1)} %get-tuple-element.30.valid_ref.refs_0_, bf16[128,256]{1,0:T(8,128)(2,1)S(1)} %bitcast.26, bf16[128,512]{1,0:T(8,128)(2,1)S(1)} %bitcast.20, ...), custom_call_target="tpu_custom_call" | custom-call | tf_op jit(solution)/shard_map/pallas_call | solution.py:524
  13.7 3.2 %collective-permute-done.refs_5_ = bf16[208,256]{1,0:T(8,128)(2,1)S(1)} collective-permute-done((bf16[208,256]{1,0:T(8,128)(2,1)S(1)}, bf16[208,256]{1,0:T(8,128)(2,1)S(1)}, u32[]{:S(2)}, u32[]{:S(2)}) %collective-permute-start) | collective-permute-done | bytes 106528 | tf_op jit(solution)/shard_map/ppermute | solution.py:522
  16.9 1.1 %all-to-all-done = bf16[32,16,128]{2,1,0:T(8,128)(2,1)S(1)} async-done(((bf16[32,16,128]{2,1,0:T(8,128)(2,1)}), bf16[32,16,128]{2,1,0:T(8,128)(2,1)S(1)}, u32[]{:S(2)}, u32[]{:S(2)}) %all-to-all-start) | async-done | bytes 131104 | tf_op jit(solution)/shard_map/all_to_all | solution.py:610
  18.0 0.8 %shard_map.122 = (bf16[4,2,256]{2,1,0:T(2,128)(2,1)S(1)}, bf16[4,2,256]{2,1,0:T(2,128)(2,1)S(1)}, bf16[4,2,256]{2,1,0:T(2,128)(2,1)S(1)}, bf16[128,256]{1,0:T(8,128)(2,1)S(1)}, f32[128,512]{1,0:T(8,128)S(1)}) custom-call(s32[1,4]{1,0:T(1,128)S(1)} %get-tuple-element.30.valid_ref.refs_0_, bf16[512,128]{1,0:T(8,128)(2,1)S(1)} %bitcast.27, ...), custom_call_target="tpu_custom_call" | custom-call | flops 99999997952 | bytes 100000000 | tf_op jit(solution)/shard_map/pallas_call | solution.py:551
  18.8 0.0 collective-permute-done.1.refs_6_
  18.8 1.2 %shard_map.123 = (bf16[128,256]{1,0:T(8,128)(2,1)}, bf16[128,512]{1,0:T(8,128)(2,1)}, bf16[4,2,256]{2,1,0:T(2,128)(2,1)}, bf16[4,2,256]{2,1,0:T(2,128)(2,1)}, bf16[4,2,256]{2,1,0:T(2,128)(2,1)}) custom-call(bf16[128,256]{1,0:T(8,128)(2,1)S(1)} %get-tuple-element.44.refs_0_, f32[128,512]{1,0:T(8,128)S(1)} %get-tuple-element.45.refs_1_, ...), custom_call_target="tpu_custom_call" | custom-call | flops 400000000 | bytes 1000000 | tf_op jit(solution)/shard_map/pallas_call | solution.py:562
Async XLA Ops:
  2.9 7.3 %copy-start = (bf16[1,8,16,512]{3,2,1,0:T(8,128)(2,1)S(1)}, bf16[1,8,16,512]{3,2,1,0:T(8,128)(2,1)}, u32[]{:S(2)}) copy-start(bf16[1,8,16,512]{3,2,1,0:T(8,128)(2,1)} %param.9) | copy-start | bytes 393220
  3.0 7.3 %copy-start.1 = (bf16[1,8,16,256]{3,2,1,0:T(8,128)(2,1)S(1)}, bf16[1,8,16,256]{3,2,1,0:T(8,128)(2,1)}, u32[]{:S(2)}) copy-start(bf16[1,8,16,256]{3,2,1,0:T(8,128)(2,1)} %param.12) | copy-start | bytes 196612
  3.0 7.3 %copy-start.2 = (bf16[1,8,16,256]{3,2,1,0:T(8,128)(2,1)S(1)}, bf16[1,8,16,256]{3,2,1,0:T(8,128)(2,1)}, u32[]{:S(2)}) copy-start(bf16[1,8,16,256]{3,2,1,0:T(8,128)(2,1)} %param.8) | copy-start | bytes 196612
  3.0 15.1 %all-to-all-start = ((bf16[32,16,128]{2,1,0:T(8,128)(2,1)}), bf16[32,16,128]{2,1,0:T(8,128)(2,1)S(1)}, u32[]{:S(2)}, u32[]{:S(2)}) async-start(bf16[32,16,128]{2,1,0:T(8,128)(2,1)} %bitcast.4), calls=%async_computation | async-start | bytes 262144 | tf_op jit(solution)/shard_map/all_to_all | solution.py:610
  10.7 6.2 %collective-permute-start = (bf16[208,256]{1,0:T(8,128)(2,1)S(1)}, bf16[208,256]{1,0:T(8,128)(2,1)S(1)}, u32[]{:S(2)}, u32[]{:S(2)}) collective-permute-start(bf16[208,256]{1,0:T(8,128)(2,1)S(1)} %get-tuple-element.36), channel_id=1, source_target_pairs={{0,1},{1,0},{2,3},{3,2},{4,5},{5,4},{6,7},{7,6},{8,9},{9,8},{10,11... | collective-permute-start | bytes 319496 | tf_op jit(solution)/shard_map/ppermute | solution.py:522
  12.5 6.3 %collective-permute-start.1 = (bf16[208,256]{1,0:T(8,128)(2,1)S(1)}, bf16[208,256]{1,0:T(8,128)(2,1)S(1)}, u32[]{:S(2)}, u32[]{:S(2)}) collective-permute-start(bf16[208,256]{1,0:T(8,128)(2,1)S(1)} %get-tuple-element.49), channel_id=1, source_target_pairs={{1,2},{2,1},{3,4},{4,3},{5,6},{6,5},{9,10},{10,9},{11,12},{12,11},... | collective-permute-start | bytes 319496 | tf_op jit(solution)/shard_map/ppermute | solution.py:523

commit v6 on v4

--- a/solution.py
+++ b/solution.py
@@ -60,15 +60,16 @@
     eight = eight_ref.shape[0]
     first = pl.multiple_of(step // eight * eight, eight)
     gain_copy = pltpu.make_async_copy(gain_hbm.at[pl.ds(first, eight)], eight_ref, sems.at[0])
-    gain_copy.start()
     copies = [
         pltpu.make_async_copy(source, target, sems.at[1 + at])
         for at, (source, target) in enumerate(
             tuple((cot_hbm.at[pl.ds(r, 32)], cot_ref.at[pl.ds(r, 32)]) for r in range(0, 128, 32)) + ((cq_hbm, cq_ref), (ckv_hbm, ckv_ref), (valid_hbm, valid_ref))
         )
     ]
-    for copy in copies:
+    for copy in copies[:-1]:
         copy.start()
+    gain_copy.start()
+    copies[-1].start()
     pixels, width = cot_ref.shape
     tokens, cwidth = cq_ref.shape
     half = POOL // 2

time: 20.3 us -> 20.3 us (level)
  no operation moved by 1% of the time
where the time goes in v6:
time: 20.3 us; the launch traced here: 20 us
  starting transfers between devices  9.8 us (48%)
  waiting for transfers between devices  4.49 us (22%)
  Pallas kernels  4.32 us (21%)
  between operations  1.39 us (7%)
    all_to_all x1, starting transfers between devices, coarse_direct(): lax.all_to_all(sent.reshape(frames * bands, tile, LANES), ('frames', 'row...  7.3 us
    all_to_all x1, waiting for transfers between devices, coarse_direct(): lax.all_to_all(sent.reshape(frames * bands, tile, LANES), ('frames', 'row...  4.48 us
    ppermute x1, starting transfers between devices, fine_level(): near = lax.ppermute(near, 'rows', pairs)  1.84 us
    pallas_call x1, Pallas kernels, coarse_direct(): pl.pallas_call(functools.partial(send_kernel, cols, bands), in_specs=[sme...  1.66 us
    pallas_call x1, Pallas kernels, fine_level(): pl.pallas_call(functools.partial(fine_kernel, cols, len(carried)), in_spe...  1.4 us
    ppermute x1, starting transfers between devices, fine_level(): far = lax.ppermute(far, 'rows', others)  0.66 us
    pallas_call x1, Pallas kernels, coarse_direct(): pl.pallas_call(functools.partial(coarse_kernel, frames, tokens), in_specs...  0.56 us
  transfers between devices with their start and end apart: 3, of which 1 were waited for; matrix products, arithmetic and copies ran while one was open for 0% of the time, Pallas kernels for 6%

profile of v6, /device:TPU:0, one launch (start us, length us, event | category | flops | bytes accessed | tf_op | source)
XLA Modules:
  0.0 20.0 jit_solution(7825385087460503429)
XLA Ops:
  1.3 1.7 %shard_map.119 = (bf16[512,128]{1,0:T(8,128)(2,1)}, f32[1,256]{1,0:T(1,128)S(1)}, s32[1,4]{1,0:T(1,128)S(1)}) custom-call(s32[1]{0:T(128)S(6)} %copy.16.step_ref, s32[1,4]{1,0:T(1,128)} %bitcast.29, bf16[128,256]{1,0:T(8,128)(2,1)} %bitcast.22, f32[1000,256]{1,0:T(8,128)} %gain_hbm.1, bf16[2,1024]{1,0:T(2,128)(2,1)} %bitcast.28, bf16[2,2048]{1,0:T(2,128)(2,1)} %bitcast.27), custom_call_target="tpu_custom_call" | custom-call | tf_op jit(solution)/shard_map/pallas_call | solution.py:493
  2.9 0.0 copy-start
  3.0 0.0 copy-start.1
  3.0 0.0 copy-start.2
  3.0 7.3 %all-to-all-start = ((bf16[32,16,128]{2,1,0:T(8,128)(2,1)}), bf16[32,16,128]{2,1,0:T(8,128)(2,1)S(1)}, u32[]{:S(2)}, u32[]{:S(2)}) async-start(bf16[32,16,128]{2,1,0:T(8,128)(2,1)} %bitcast.6), calls=%async_computation | async-start | bytes 262144 | tf_op jit(solution)/shard_map/all_to_all | solution.py:518
  10.3 0.0 copy-done
  10.3 0.0 copy-done.1
  10.3 0.0 copy-done.2
  10.3 0.3 %shard_map.120 = (bf16[208,256]{1,0:T(8,128)(2,1)S(1)}, bf16[208,256]{1,0:T(8,128)(2,1)S(1)}, bf16[128,256]{1,0:T(8,128)(2,1)S(1)}) custom-call(s32[1,4]{1,0:T(1,128)S(1)} %get-tuple-element.28.valid_ref, f32[1,256]{1,0:T(1,128)S(1)} %get-tuple-element.29.gain_ref, bf16[128,256]{1,0:T(8,128)(2,1)S(1)} %bitcast.24, bf16[128,512]{1,0:T(8,128)(2,1)S(1)} %bitcast.19, ...), custom_call_target="tpu_custom_call" | custom-call | tf_op jit(solution)/shard_map/pallas_call | solution.py:441
  10.7 1.8 %collective-permute-start = (bf16[208,256]{1,0:T(8,128)(2,1)S(1)}, bf16[208,256]{1,0:T(8,128)(2,1)S(1)}, u32[]{:S(2)}, u32[]{:S(2)}) collective-permute-start(bf16[208,256]{1,0:T(8,128)(2,1)S(1)} %get-tuple-element.30), channel_id=1, source_target_pairs={{0,1},{1,0},{2,3},{3,2},{4,5},{5,4},{6,7},{7,6},{8,9},{9,8},{10,11... | collective-permute-start | bytes 319496 | tf_op jit(solution)/shard_map/ppermute | solution.py:450
  12.5 0.7 %collective-permute-start.1 = (bf16[208,256]{1,0:T(8,128)(2,1)S(1)}, bf16[208,256]{1,0:T(8,128)(2,1)S(1)}, u32[]{:S(2)}, u32[]{:S(2)}) collective-permute-start(bf16[208,256]{1,0:T(8,128)(2,1)S(1)} %get-tuple-element.31), channel_id=1, source_target_pairs={{1,2},{2,1},{3,4},{4,3},{5,6},{6,5},{9,10},{10,9},{11,12},{12,11},... | collective-permute-start | bytes 319496 | tf_op jit(solution)/shard_map/ppermute | solution.py:451
  13.2 0.4 %shard_map.121 = (f32[96,128]{1,0:T(8,128)S(1)}, f32[48,128]{1,0:T(8,128)S(1)}, f32[48,128]{1,0:T(8,128)S(1)}, bf16[2,256,128]{2,1,0:T(8,128)(2,1)S(1)}, bf16[2,...) custom-call(s32[1,4]{1,0:T(1,128)S(1)} %get-tuple-element.28.valid_r, ...), custom_call_target="tpu_custom_call" | custom-call | tf_op jit(solution)/shard_map/pallas_call | solution.py:453
  13.6 4.5 %all-to-all-done = bf16[32,16,128]{2,1,0:T(8,128)(2,1)S(1)} async-done(((bf16[32,16,128]{2,1,0:T(8,128)(2,1)}), bf16[32,16,128]{2,1,0:T(8,128)(2,1)S(1)}, u32[]{:S(2)}, u32[]{:S(2)}) %all-to-all-start) | async-done | bytes 131104 | tf_op jit(solution)/shard_map/all_to_all | solution.py:518
  18.0 0.6 %shard_map.122 = (bf16[4,2,256]{2,1,0:T(2,128)(2,1)S(1)}, bf16[4,2,256]{2,1,0:T(2,128)(2,1)S(1)}, bf16[4,2,256]{2,1,0:T(2,128)(2,1)S(1)}) custom-call(s32[1,4]{1,0:T(1,128)S(1)} %get-tuple-element.28.valid_ref, bf16[512,128]{1,0:T(8,128)(2,1)S(1)} %bitcast.26), custom_call_target="tpu_custom_call" | custom-call | flops 99999997952 | bytes 100000000 | tf_op jit(solution)/shard_map/pallas_call | solution.py:526
  18.6 0.0 collective-permute-done.refs_1_
  18.6 0.0 collective-permute-done.1.refs_2_
  18.6 1.4 %shard_map.123 = (bf16[128,256]{1,0:T(8,128)(2,1)}, bf16[128,512]{1,0:T(8,128)(2,1)}, bf16[4,2,256]{2,1,0:T(2,128)(2,1)}, bf16[4,2,256]{2,1,0:T(2,128)(2,1)}, bf16[4,2,256]{2,1,0:T(2,128)(2,1)}) custom-call(bf16[128,512]{1,0:T(8,128)(2,1)S(1)} %bitcast.21, bf16[208,256]{1,0:T(8,128)(2,1)S(1)} %collective-permute-done.refs_1_, ...), custom_call_target="tpu_custom_call" | custom-call | flops 400000000 | bytes 1000000 | tf_op jit(solution)/shard_map/pallas_call | solution.py:470
Async XLA Ops:
  2.9 7.3 %copy-start = (bf16[1,8,16,512]{3,2,1,0:T(8,128)(2,1)S(1)}, bf16[1,8,16,512]{3,2,1,0:T(8,128)(2,1)}, u32[]{:S(2)}) copy-start(bf16[1,8,16,512]{3,2,1,0:T(8,128)(2,1)} %param.9) | copy-start | bytes 393220
  3.0 7.3 %copy-start.1 = (bf16[1,8,16,256]{3,2,1,0:T(8,128)(2,1)S(1)}, bf16[1,8,16,256]{3,2,1,0:T(8,128)(2,1)}, u32[]{:S(2)}) copy-start(bf16[1,8,16,256]{3,2,1,0:T(8,128)(2,1)} %param.12) | copy-start | bytes 196612
  3.0 7.3 %copy-start.2 = (bf16[1,8,16,256]{3,2,1,0:T(8,128)(2,1)S(1)}, bf16[1,8,16,256]{3,2,1,0:T(8,128)(2,1)}, u32[]{:S(2)}) copy-start(bf16[1,8,16,256]{3,2,1,0:T(8,128)(2,1)} %param.8) | copy-start | bytes 196612
  3.0 15.1 %all-to-all-start = ((bf16[32,16,128]{2,1,0:T(8,128)(2,1)}), bf16[32,16,128]{2,1,0:T(8,128)(2,1)S(1)}, u32[]{:S(2)}, u32[]{:S(2)}) async-start(bf16[32,16,128]{2,1,0:T(8,128)(2,1)} %bitcast.6), calls=%async_computation | async-start | bytes 262144 | tf_op jit(solution)/shard_map/all_to_all | solution.py:518
  10.7 7.9 %collective-permute-start = (bf16[208,256]{1,0:T(8,128)(2,1)S(1)}, bf16[208,256]{1,0:T(8,128)(2,1)S(1)}, u32[]{:S(2)}, u32[]{:S(2)}) collective-permute-start(bf16[208,256]{1,0:T(8,128)(2,1)S(1)} %get-tuple-element.30), channel_id=1, source_target_pairs={{0,1},{1,0},{2,3},{3,2},{4,5},{5,4},{6,7},{7,6},{8,9},{9,8},{10,11... | collective-permute-start | bytes 319496 | tf_op jit(solution)/shard_map/ppermute | solution.py:450
  12.5 6.1 %collective-permute-start.1 = (bf16[208,256]{1,0:T(8,128)(2,1)S(1)}, bf16[208,256]{1,0:T(8,128)(2,1)S(1)}, u32[]{:S(2)}, u32[]{:S(2)}) collective-permute-start(bf16[208,256]{1,0:T(8,128)(2,1)S(1)} %get-tuple-element.31), channel_id=1, source_target_pairs={{1,2},{2,1},{3,4},{4,3},{5,6},{6,5},{9,10},{10,9},{11,12},{12,11},... | collective-permute-start | bytes 319496 | tf_op jit(solution)/shard_map/ppermute | solution.py:451

commit v7 on v6

--- a/solution.py
+++ b/solution.py
@@ -79,11 +79,13 @@
     pixel = iota((groups * tokens, pixels), 1)
     row, col = pixel // cols, pixel % cols
     inside = (row // half == group // 2) & (col // half == token * 2 + group % 2)
-    for copy in copies:
+    for copy in copies[-3:]:
+        copy.wait()
+    query = cq_ref[...].astype(F32)
+    both = ckv_ref[...].astype(F32)
+    for copy in copies[:-3]:
         copy.wait()
     summed = dot_nn(inside.astype(BF16), cot_ref[...])
-    query = cq_ref[...].astype(F32)
-    both = ckv_ref[...].astype(F32)
     gain_copy.wait()
     gain = eight_ref[pl.ds(step - first, 1), :]
     gain_ref[...] = gain

time: 20.3 us -> 20.3 us (level)
  no operation moved by 1% of the time
where the time goes in v7:
time: 20.3 us; the launch traced here: 20 us
  starting transfers between devices  9.8 us (48%)
  waiting for transfers between devices  4.49 us (22%)
  Pallas kernels  4.33 us (21%)
  between operations  1.39 us (7%)
    all_to_all x1, starting transfers between devices, coarse_direct(): lax.all_to_all(sent.reshape(frames * bands, tile, LANES), ('frames', 'row...  7.3 us
    all_to_all x1, waiting for transfers between devices, coarse_direct(): lax.all_to_all(sent.reshape(frames * bands, tile, LANES), ('frames', 'row...  4.48 us
    ppermute x1, starting transfers between devices, fine_level(): near = lax.ppermute(near, 'rows', pairs)  1.84 us
    pallas_call x1, Pallas kernels, coarse_direct(): pl.pallas_call(functools.partial(send_kernel, cols, bands), in_specs=[sme...  1.67 us
    pallas_call x1, Pallas kernels, fine_level(): pl.pallas_call(functools.partial(fine_kernel, cols, len(carried)), in_spe...  1.39 us
    ppermute x1, starting transfers between devices, fine_level(): far = lax.ppermute(far, 'rows', others)  0.66 us
    pallas_call x1, Pallas kernels, coarse_direct(): pl.pallas_call(functools.partial(coarse_kernel, frames, tokens), in_specs...  0.56 us
  transfers between devices with their start and end apart: 3, of which 1 were waited for; matrix products, arithmetic and copies ran while one was open for 0% of the time, Pallas kernels for 6%

profile of v7, /device:TPU:0, one launch (start us, length us, event | category | flops | bytes accessed | tf_op | source)
XLA Modules:
  0.0 20.0 jit_solution(6328362606614809920)
XLA Ops:
  1.3 1.7 %shard_map.119 = (bf16[512,128]{1,0:T(8,128)(2,1)}, f32[1,256]{1,0:T(1,128)S(1)}, s32[1,4]{1,0:T(1,128)S(1)}) custom-call(s32[1]{0:T(128)S(6)} %copy.16.step_ref, s32[1,4]{1,0:T(1,128)} %bitcast.29, bf16[128,256]{1,0:T(8,128)(2,1)} %bitcast.22, f32[1000,256]{1,0:T(8,128)} %gain_hbm.1, bf16[2,1024]{1,0:T(2,128)(2,1)} %bitcast.28, bf16[2,2048]{1,0:T(2,128)(2,1)} %bitcast.27), custom_call_target="tpu_custom_call" | custom-call | tf_op jit(solution)/shard_map/pallas_call | solution.py:495
  3.0 0.0 copy-start
  3.0 0.0 copy-start.1
  3.0 0.0 copy-start.2
  3.0 7.3 %all-to-all-start = ((bf16[32,16,128]{2,1,0:T(8,128)(2,1)}), bf16[32,16,128]{2,1,0:T(8,128)(2,1)S(1)}, u32[]{:S(2)}, u32[]{:S(2)}) async-start(bf16[32,16,128]{2,1,0:T(8,128)(2,1)} %bitcast.6), calls=%async_computation | async-start | bytes 262144 | tf_op jit(solution)/shard_map/all_to_all | solution.py:520
  10.3 0.0 copy-done
  10.3 0.0 copy-done.1
  10.3 0.0 copy-done.2
  10.3 0.3 %shard_map.120 = (bf16[208,256]{1,0:T(8,128)(2,1)S(1)}, bf16[208,256]{1,0:T(8,128)(2,1)S(1)}, bf16[128,256]{1,0:T(8,128)(2,1)S(1)}) custom-call(s32[1,4]{1,0:T(1,128)S(1)} %get-tuple-element.28.valid_ref, f32[1,256]{1,0:T(1,128)S(1)} %get-tuple-element.29.gain_ref, bf16[128,256]{1,0:T(8,128)(2,1)S(1)} %bitcast.24, bf16[128,512]{1,0:T(8,128)(2,1)S(1)} %bitcast.19, ...), custom_call_target="tpu_custom_call" | custom-call | tf_op jit(solution)/shard_map/pallas_call | solution.py:443
  10.7 1.8 %collective-permute-start = (bf16[208,256]{1,0:T(8,128)(2,1)S(1)}, bf16[208,256]{1,0:T(8,128)(2,1)S(1)}, u32[]{:S(2)}, u32[]{:S(2)}) collective-permute-start(bf16[208,256]{1,0:T(8,128)(2,1)S(1)} %get-tuple-element.30), channel_id=1, source_target_pairs={{0,1},{1,0},{2,3},{3,2},{4,5},{5,4},{6,7},{7,6},{8,9},{9,8},{10,11... | collective-permute-start | bytes 319496 | tf_op jit(solution)/shard_map/ppermute | solution.py:452
  12.5 0.7 %collective-permute-start.1 = (bf16[208,256]{1,0:T(8,128)(2,1)S(1)}, bf16[208,256]{1,0:T(8,128)(2,1)S(1)}, u32[]{:S(2)}, u32[]{:S(2)}) collective-permute-start(bf16[208,256]{1,0:T(8,128)(2,1)S(1)} %get-tuple-element.31), channel_id=1, source_target_pairs={{1,2},{2,1},{3,4},{4,3},{5,6},{6,5},{9,10},{10,9},{11,12},{12,11},... | collective-permute-start | bytes 319496 | tf_op jit(solution)/shard_map/ppermute | solution.py:453
  13.2 0.4 %shard_map.121 = (f32[96,128]{1,0:T(8,128)S(1)}, f32[48,128]{1,0:T(8,128)S(1)}, f32[48,128]{1,0:T(8,128)S(1)}, bf16[2,256,128]{2,1,0:T(8,128)(2,1)S(1)}, bf16[2,...) custom-call(s32[1,4]{1,0:T(1,128)S(1)} %get-tuple-element.28.valid_r, ...), custom_call_target="tpu_custom_call" | custom-call | tf_op jit(solution)/shard_map/pallas_call | solution.py:455
  13.6 4.5 %all-to-all-done = bf16[32,16,128]{2,1,0:T(8,128)(2,1)S(1)} async-done(((bf16[32,16,128]{2,1,0:T(8,128)(2,1)}), bf16[32,16,128]{2,1,0:T(8,128)(2,1)S(1)}, u32[]{:S(2)}, u32[]{:S(2)}) %all-to-all-start) | async-done | bytes 131104 | tf_op jit(solution)/shard_map/all_to_all | solution.py:520
  18.0 0.6 %shard_map.122 = (bf16[4,2,256]{2,1,0:T(2,128)(2,1)S(1)}, bf16[4,2,256]{2,1,0:T(2,128)(2,1)S(1)}, bf16[4,2,256]{2,1,0:T(2,128)(2,1)S(1)}) custom-call(s32[1,4]{1,0:T(1,128)S(1)} %get-tuple-element.28.valid_ref, bf16[512,128]{1,0:T(8,128)(2,1)S(1)} %bitcast.26), custom_call_target="tpu_custom_call" | custom-call | flops 99999997952 | bytes 100000000 | tf_op jit(solution)/shard_map/pallas_call | solution.py:528
  18.6 0.0 collective-permute-done.refs_1_
  18.6 0.0 collective-permute-done.1.refs_2_
  18.6 1.4 %shard_map.123 = (bf16[128,256]{1,0:T(8,128)(2,1)}, bf16[128,512]{1,0:T(8,128)(2,1)}, bf16[4,2,256]{2,1,0:T(2,128)(2,1)}, bf16[4,2,256]{2,1,0:T(2,128)(2,1)}, bf16[4,2,256]{2,1,0:T(2,128)(2,1)}) custom-call(bf16[128,512]{1,0:T(8,128)(2,1)S(1)} %bitcast.21, bf16[208,256]{1,0:T(8,128)(2,1)S(1)} %collective-permute-done.refs_1_, ...), custom_call_target="tpu_custom_call" | custom-call | flops 400000000 | bytes 1000000 | tf_op jit(solution)/shard_map/pallas_call | solution.py:472
Async XLA Ops:
  3.0 7.3 %copy-start = (bf16[1,8,16,512]{3,2,1,0:T(8,128)(2,1)S(1)}, bf16[1,8,16,512]{3,2,1,0:T(8,128)(2,1)}, u32[]{:S(2)}) copy-start(bf16[1,8,16,512]{3,2,1,0:T(8,128)(2,1)} %param.9) | copy-start | bytes 393220
  3.0 7.3 %copy-start.1 = (bf16[1,8,16,256]{3,2,1,0:T(8,128)(2,1)S(1)}, bf16[1,8,16,256]{3,2,1,0:T(8,128)(2,1)}, u32[]{:S(2)}) copy-start(bf16[1,8,16,256]{3,2,1,0:T(8,128)(2,1)} %param.12) | copy-start | bytes 196612
  3.0 7.3 %copy-start.2 = (bf16[1,8,16,256]{3,2,1,0:T(8,128)(2,1)S(1)}, bf16[1,8,16,256]{3,2,1,0:T(8,128)(2,1)}, u32[]{:S(2)}) copy-start(bf16[1,8,16,256]{3,2,1,0:T(8,128)(2,1)} %param.8) | copy-start | bytes 196612
  3.0 15.1 %all-to-all-start = ((bf16[32,16,128]{2,1,0:T(8,128)(2,1)}), bf16[32,16,128]{2,1,0:T(8,128)(2,1)S(1)}, u32[]{:S(2)}, u32[]{:S(2)}) async-start(bf16[32,16,128]{2,1,0:T(8,128)(2,1)} %bitcast.6), calls=%async_computation | async-start | bytes 262144 | tf_op jit(solution)/shard_map/all_to_all | solution.py:520
  10.7 7.9 %collective-permute-start = (bf16[208,256]{1,0:T(8,128)(2,1)S(1)}, bf16[208,256]{1,0:T(8,128)(2,1)S(1)}, u32[]{:S(2)}, u32[]{:S(2)}) collective-permute-start(bf16[208,256]{1,0:T(8,128)(2,1)S(1)} %get-tuple-element.30), channel_id=1, source_target_pairs={{0,1},{1,0},{2,3},{3,2},{4,5},{5,4},{6,7},{7,6},{8,9},{9,8},{10,11... | collective-permute-start | bytes 319496 | tf_op jit(solution)/shard_map/ppermute | solution.py:452
  12.5 6.1 %collective-permute-start.1 = (bf16[208,256]{1,0:T(8,128)(2,1)S(1)}, bf16[208,256]{1,0:T(8,128)(2,1)S(1)}, u32[]{:S(2)}, u32[]{:S(2)}) collective-permute-start(bf16[208,256]{1,0:T(8,128)(2,1)S(1)} %get-tuple-element.31), channel_id=1, source_target_pairs={{1,2},{2,1},{3,4},{4,3},{5,6},{6,5},{9,10},{10,9},{11,12},{12,11},... | collective-permute-start | bytes 319496 | tf_op jit(solution)/shard_map/ppermute | solution.py:453

commit v8 on v7

--- a/solution.py
+++ b/solution.py
@@ -63,7 +63,7 @@
     copies = [
         pltpu.make_async_copy(source, target, sems.at[1 + at])
         for at, (source, target) in enumerate(
-            tuple((cot_hbm.at[pl.ds(r, 32)], cot_ref.at[pl.ds(r, 32)]) for r in range(0, 128, 32)) + ((cq_hbm, cq_ref), (ckv_hbm, ckv_ref), (valid_hbm, valid_ref))
+            tuple((cot_hbm.at[pl.ds(r, 64)], cot_ref.at[pl.ds(r, 64)]) for r in range(0, 128, 64)) + ((cq_hbm, cq_ref), (ckv_hbm, ckv_ref), (valid_hbm, valid_ref))
         )
     ]
     for copy in copies[:-1]:

time: 20.3 us -> 20.3 us (level)
  no operation moved by 1% of the time
where the time goes in v8:
time: 20.3 us; the launch traced here: 20 us
  starting transfers between devices  9.8 us (48%)
  waiting for transfers between devices  4.49 us (22%)
  Pallas kernels  4.32 us (21%)
  between operations  1.39 us (7%)
    all_to_all x1, starting transfers between devices, coarse_direct(): lax.all_to_all(sent.reshape(frames * bands, tile, LANES), ('frames', 'row...  7.3 us
    all_to_all x1, waiting for transfers between devices, coarse_direct(): lax.all_to_all(sent.reshape(frames * bands, tile, LANES), ('frames', 'row...  4.48 us
    ppermute x1, starting transfers between devices, fine_level(): near = lax.ppermute(near, 'rows', pairs)  1.84 us
    pallas_call x1, Pallas kernels, coarse_direct(): pl.pallas_call(functools.partial(send_kernel, cols, bands), in_specs=[sme...  1.65 us
    pallas_call x1, Pallas kernels, fine_level(): pl.pallas_call(functools.partial(fine_kernel, cols, len(carried)), in_spe...  1.4 us
    ppermute x1, starting transfers between devices, fine_level(): far = lax.ppermute(far, 'rows', others)  0.66 us
    pallas_call x1, Pallas kernels, coarse_direct(): pl.pallas_call(functools.partial(coarse_kernel, frames, tokens), in_specs...  0.56 us
  transfers between devices with their start and end apart: 3, of which 1 were waited for; matrix products, arithmetic and copies ran while one was open for 0% of the time, Pallas kernels for 6%

profile of v8, /device:TPU:0, one launch (start us, length us, event | category | flops | bytes accessed | tf_op | source)
XLA Modules:
  0.0 20.0 jit_solution(5575792437094735345)
XLA Ops:
  1.3 1.7 %shard_map.119 = (bf16[512,128]{1,0:T(8,128)(2,1)}, f32[1,256]{1,0:T(1,128)S(1)}, s32[1,4]{1,0:T(1,128)S(1)}) custom-call(s32[1]{0:T(128)S(6)} %copy.16.step_ref, s32[1,4]{1,0:T(1,128)} %bitcast.29, bf16[128,256]{1,0:T(8,128)(2,1)} %bitcast.22, f32[1000,256]{1,0:T(8,128)} %gain_hbm.1, bf16[2,1024]{1,0:T(2,128)(2,1)} %bitcast.28, bf16[2,2048]{1,0:T(2,128)(2,1)} %bitcast.27), custom_call_target="tpu_custom_call" | custom-call | tf_op jit(solution)/shard_map/pallas_call | solution.py:495
  2.9 0.0 copy-start
  3.0 0.0 copy-start.1
  3.0 0.0 copy-start.2
  3.0 7.3 %all-to-all-start = ((bf16[32,16,128]{2,1,0:T(8,128)(2,1)}), bf16[32,16,128]{2,1,0:T(8,128)(2,1)S(1)}, u32[]{:S(2)}, u32[]{:S(2)}) async-start(bf16[32,16,128]{2,1,0:T(8,128)(2,1)} %bitcast.6), calls=%async_computation | async-start | bytes 262144 | tf_op jit(solution)/shard_map/all_to_all | solution.py:520
  10.3 0.0 copy-done
  10.3 0.0 copy-done.1
  10.3 0.0 copy-done.2
  10.3 0.3 %shard_map.120 = (bf16[208,256]{1,0:T(8,128)(2,1)S(1)}, bf16[208,256]{1,0:T(8,128)(2,1)S(1)}, bf16[128,256]{1,0:T(8,128)(2,1)S(1)}) custom-call(s32[1,4]{1,0:T(1,128)S(1)} %get-tuple-element.28.valid_ref, f32[1,256]{1,0:T(1,128)S(1)} %get-tuple-element.29.gain_ref, bf16[128,256]{1,0:T(8,128)(2,1)S(1)} %bitcast.24, bf16[128,512]{1,0:T(8,128)(2,1)S(1)} %bitcast.19, ...), custom_call_target="tpu_custom_call" | custom-call | tf_op jit(solution)/shard_map/pallas_call | solution.py:443
  10.7 1.8 %collective-permute-start = (bf16[208,256]{1,0:T(8,128)(2,1)S(1)}, bf16[208,256]{1,0:T(8,128)(2,1)S(1)}, u32[]{:S(2)}, u32[]{:S(2)}) collective-permute-start(bf16[208,256]{1,0:T(8,128)(2,1)S(1)} %get-tuple-element.30), channel_id=1, source_target_pairs={{0,1},{1,0},{2,3},{3,2},{4,5},{5,4},{6,7},{7,6},{8,9},{9,8},{10,11... | collective-permute-start | bytes 319496 | tf_op jit(solution)/shard_map/ppermute | solution.py:452
  12.5 0.7 %collective-permute-start.1 = (bf16[208,256]{1,0:T(8,128)(2,1)S(1)}, bf16[208,256]{1,0:T(8,128)(2,1)S(1)}, u32[]{:S(2)}, u32[]{:S(2)}) collective-permute-start(bf16[208,256]{1,0:T(8,128)(2,1)S(1)} %get-tuple-element.31), channel_id=1, source_target_pairs={{1,2},{2,1},{3,4},{4,3},{5,6},{6,5},{9,10},{10,9},{11,12},{12,11},... | collective-permute-start | bytes 319496 | tf_op jit(solution)/shard_map/ppermute | solution.py:453
  13.2 0.4 %shard_map.121 = (f32[96,128]{1,0:T(8,128)S(1)}, f32[48,128]{1,0:T(8,128)S(1)}, f32[48,128]{1,0:T(8,128)S(1)}, bf16[2,256,128]{2,1,0:T(8,128)(2,1)S(1)}, bf16[2,...) custom-call(s32[1,4]{1,0:T(1,128)S(1)} %get-tuple-element.28.valid_r, ...), custom_call_target="tpu_custom_call" | custom-call | tf_op jit(solution)/shard_map/pallas_call | solution.py:455
  13.5 4.5 %all-to-all-done = bf16[32,16,128]{2,1,0:T(8,128)(2,1)S(1)} async-done(((bf16[32,16,128]{2,1,0:T(8,128)(2,1)}), bf16[32,16,128]{2,1,0:T(8,128)(2,1)S(1)}, u32[]{:S(2)}, u32[]{:S(2)}) %all-to-all-start) | async-done | bytes 131104 | tf_op jit(solution)/shard_map/all_to_all | solution.py:520
  18.0 0.6 %shard_map.122 = (bf16[4,2,256]{2,1,0:T(2,128)(2,1)S(1)}, bf16[4,2,256]{2,1,0:T(2,128)(2,1)S(1)}, bf16[4,2,256]{2,1,0:T(2,128)(2,1)S(1)}) custom-call(s32[1,4]{1,0:T(1,128)S(1)} %get-tuple-element.28.valid_ref, bf16[512,128]{1,0:T(8,128)(2,1)S(1)} %bitcast.26), custom_call_target="tpu_custom_call" | custom-call | flops 99999997952 | bytes 100000000 | tf_op jit(solution)/shard_map/pallas_call | solution.py:528
  18.6 0.0 collective-permute-done.refs_1_
  18.6 0.0 collective-permute-done.1.refs_2_
  18.6 1.4 %shard_map.123 = (bf16[128,256]{1,0:T(8,128)(2,1)}, bf16[128,512]{1,0:T(8,128)(2,1)}, bf16[4,2,256]{2,1,0:T(2,128)(2,1)}, bf16[4,2,256]{2,1,0:T(2,128)(2,1)}, bf16[4,2,256]{2,1,0:T(2,128)(2,1)}) custom-call(bf16[128,512]{1,0:T(8,128)(2,1)S(1)} %bitcast.21, bf16[208,256]{1,0:T(8,128)(2,1)S(1)} %collective-permute-done.refs_1_, ...), custom_call_target="tpu_custom_call" | custom-call | flops 400000000 | bytes 1000000 | tf_op jit(solution)/shard_map/pallas_call | solution.py:472
Async XLA Ops:
  2.9 7.3 %copy-start = (bf16[1,8,16,512]{3,2,1,0:T(8,128)(2,1)S(1)}, bf16[1,8,16,512]{3,2,1,0:T(8,128)(2,1)}, u32[]{:S(2)}) copy-start(bf16[1,8,16,512]{3,2,1,0:T(8,128)(2,1)} %param.9) | copy-start | bytes 393220
  3.0 7.3 %copy-start.1 = (bf16[1,8,16,256]{3,2,1,0:T(8,128)(2,1)S(1)}, bf16[1,8,16,256]{3,2,1,0:T(8,128)(2,1)}, u32[]{:S(2)}) copy-start(bf16[1,8,16,256]{3,2,1,0:T(8,128)(2,1)} %param.12) | copy-start | bytes 196612
  3.0 7.3 %copy-start.2 = (bf16[1,8,16,256]{3,2,1,0:T(8,128)(2,1)S(1)}, bf16[1,8,16,256]{3,2,1,0:T(8,128)(2,1)}, u32[]{:S(2)}) copy-start(bf16[1,8,16,256]{3,2,1,0:T(8,128)(2,1)} %param.8) | copy-start | bytes 196612
  3.0 15.1 %all-to-all-start = ((bf16[32,16,128]{2,1,0:T(8,128)(2,1)}), bf16[32,16,128]{2,1,0:T(8,128)(2,1)S(1)}, u32[]{:S(2)}, u32[]{:S(2)}) async-start(bf16[32,16,128]{2,1,0:T(8,128)(2,1)} %bitcast.6), calls=%async_computation | async-start | bytes 262144 | tf_op jit(solution)/shard_map/all_to_all | solution.py:520
  10.7 7.9 %collective-permute-start = (bf16[208,256]{1,0:T(8,128)(2,1)S(1)}, bf16[208,256]{1,0:T(8,128)(2,1)S(1)}, u32[]{:S(2)}, u32[]{:S(2)}) collective-permute-start(bf16[208,256]{1,0:T(8,128)(2,1)S(1)} %get-tuple-element.30), channel_id=1, source_target_pairs={{0,1},{1,0},{2,3},{3,2},{4,5},{5,4},{6,7},{7,6},{8,9},{9,8},{10,11... | collective-permute-start | bytes 319496 | tf_op jit(solution)/shard_map/ppermute | solution.py:452
  12.5 6.1 %collective-permute-start.1 = (bf16[208,256]{1,0:T(8,128)(2,1)S(1)}, bf16[208,256]{1,0:T(8,128)(2,1)S(1)}, u32[]{:S(2)}, u32[]{:S(2)}) collective-permute-start(bf16[208,256]{1,0:T(8,128)(2,1)S(1)} %get-tuple-element.31), channel_id=1, source_target_pairs={{1,2},{2,1},{3,4},{4,3},{5,6},{6,5},{9,10},{10,9},{11,12},{12,11},... | collective-permute-start | bytes 319496 | tf_op jit(solution)/shard_map/ppermute | solution.py:453
